TPU v7x, 32 devices: a whole 2x2x4 slice. The times are simulated.
32 devices in a mesh: subj: 8 (over z, y), feat: 4 (over x, core).
Axes of the slice: x: 2, y: 2, z: 4, core: 2. Of those that a mesh axis runs over, the one named last changes fastest.
Arguments:
- visits: bfloat16 [64, 56, 10240], P('subj', None, 'feat'), may hold values from -6 to 6
- tile_pattern: int32 [64, 80], P('subj', 'feat'), may hold values 0 or 1
- counts: int32 [64], P('subj'), may hold values from 1 to 56, 1792 in all
- codes_t: bfloat16 [256, 10240], P('subj', 'feat'), may hold values from -0.0625 to 0.0625
- core: bfloat16 [256, 256], replicated, may hold values from -0.375 to 0.375
- patient_weights: float32 [64, 256], P('subj'), may hold values from 0.3 to 3
Outputs:
- code_mttkrp: float32 [256, 10240], P('subj', 'feat')
- patient_mttkrp: float32 [64, 256], P('subj')
Inputs may be any that keep to these rules, and one draw needn't show every extreme that they name: `counts`: every patient has at least one visit; some patient has exactly 56.
All inputs are finite; a program needn't handle non-finite values. No bound on the sum of `tile_pattern` or of `counts` on one device may be relied on, other than what follows from the above.
Results may differ from a plain program's by a relative error of at most 0.0019.
Values may be sent and summed in bfloat16 or wider, within the bound.
No kernel may reach another device: no remote copies, remote signals or barrier semaphores. Data moves between devices by JAX's collectives and lax.ppermute only.
A program may use at most 64 MiB of HBM per device.

v0:
```python
import jax
import jax.numpy as jnp
from jax import lax
from jax.sharding import PartitionSpec as P

NS_STEPS = 8


def procrustes(projected, weights, core_f):
    scaled = projected * weights[:, None, :]
    target = jnp.einsum("pir,sr->pis", scaled, core_f, precision=lax.Precision.HIGHEST)
    total = jnp.sum(target * target, axis=(1, 2))
    rotation = target * lax.rsqrt(total + 1e-06)[:, None, None]
    for step in range(NS_STEPS):
        gram = jnp.einsum("pis,pks->pik", rotation, rotation, precision=lax.Precision.HIGHEST)
        rotation = 1.5 * rotation - 0.5 * jnp.einsum(
            "pik,pks->pis", gram, rotation, precision=lax.Precision.HIGHEST
        )
    rotated = jnp.einsum("pis,sr->pir", rotation, core_f, precision=lax.Precision.HIGHEST)
    patient_rows = jnp.sum(rotated * projected, axis=1)
    weighted = (rotated * weights[:, None, :]).astype(jnp.bfloat16)
    return (weighted, patient_rows)


def per_device(visits, tile_pattern, counts, codes_t, core, patient_weights):
    npat, nvis, ncode = visits.shape
    ntile = tile_pattern.shape[1]
    rank = core.shape[0]
    core_f = core.astype(jnp.float32)
    live = (lax.broadcasted_iota(jnp.int32, (npat, nvis), 1) < counts[:, None]).astype(jnp.int32)
    gate = (tile_pattern[:, None, :, None] * live[:, :, None, None]).astype(jnp.bfloat16)
    masked = (visits.reshape(npat, nvis, ntile, ncode // ntile) * gate).reshape(npat * nvis, ncode)
    partial_proj = lax.dot_general(
        masked,
        lax.all_gather(codes_t, "subj", axis=0, tiled=True),
        (((1,), (1,)), ((), ())),
        preferred_element_type=jnp.float32,
    )
    partial_proj = partial_proj.reshape(npat, nvis, rank)
    share = npat // lax.axis_size("feat")
    shared = lax.psum_scatter(partial_proj, "feat", scatter_dimension=0, tiled=True)
    own_weights = lax.dynamic_slice_in_dim(
        patient_weights, lax.axis_index("feat") * share, share, 0
    )
    weighted_part, rows_part = procrustes(shared, own_weights, core_f)
    weighted = lax.all_gather(weighted_part, "feat", axis=0, tiled=True)
    patient_rows = lax.all_gather(rows_part, "feat", axis=0, tiled=True)
    weighted_flat = weighted.reshape(npat * nvis, rank)
    term = lax.dot_general(
        weighted_flat, masked, (((0,), (0,)), ((), ())), preferred_element_type=jnp.float32
    )
    code_rows_out = lax.psum_scatter(term, "subj", scatter_dimension=0, tiled=True)
    return (code_rows_out, patient_rows)


def solution(mesh):
    return jax.shard_map(
        per_device,
        mesh=mesh,
        in_specs=(
            P("subj", None, "feat"),
            P("subj", "feat"),
            P("subj"),
            P("subj", "feat"),
            P(),
            P("subj", None),
        ),
        out_specs=(P("subj", "feat"), P("subj", None)),
        check_vma=False,
    )
```

profile of v0, /device:TPU:0, one launch (start us, length us, event | category | flops | bytes accessed | tf_op | source)
XLA Modules:
  0.0 168.6 jit_solution(12359387249808304062)
XLA Ops:
  7.2 0.0 copy-start
  7.2 0.0 all-gather.3.cloned.1.call-start
  7.2 0.7 all-gather.3.cloned.1.call-update
  7.9 0.0 reduce-scatter.3.cloned.1.call-start
  8.0 0.7 fusion.21
  8.7 0.8 multiply_convert_fusion
  9.5 1.7 mul.113
  11.2 2.7 %mul.114 = bf16[8,56,2560]{2,1,0:T(8,128)(2,1)} reshape(bf16[8,56,20,128]{3,2,1,0:T(8,128)(2,1)S(1)} %mul.113) | data formatting | bytes 4587520 | tf_op jit(solution)/shard_map/mul | solution.py:32
  13.8 2.9 %mul.115 = bf16[8,56,2560]{2,1,0:T(8,128)(2,1)S(1)} multiply(bf16[8,56,2560]{2,1,0:T(8,128)(2,1)} %param.6, bf16[8,56,2560]{2,1,0:T(8,128)(2,1)} %mul.114) | non-fusion elementwise | flops 1146880 | bytes 6881280 | tf_op jit(solution)/shard_map/mul | solution.py:32
  16.7 38.0 %all-gather.3.cloned.1.call-done = bf16[256,2560]{1,0:T(8,128)(2,1)} async-done(((bf16[32,2560]{1,0:T(8,128)(2,1)}), bf16[256,2560]{1,0:T(8,128)(2,1)}) %all-gather.3.cloned.1.call-update) | async-done | bytes 1310736 | tf_op jit(solution)/shard_map/all_gather | solution.py:35
  54.7 2.9 %fusion = f32[8,56,256]{2,1,0:T(8,128)} fusion(bf16[8,56,2560]{2,1,0:T(8,128)(2,1)S(1)} %mul.115, bf16[256,2560]{1,0:T(8,128)(2,1)} %all-gather.3.cloned.1.call-done), kind=kOutput, calls=%fused_computation.1 | convolution fusion | flops 587202560 | bytes 4063232 | tf_op jit(solution)/shard_map/dot_general | solution.py:33
  57.6 0.0 reduce-scatter.3.cloned.1.call-update
  57.6 0.0 reduce-scatter.5.cloned.1.call-start
  57.7 0.7 constant_dynamic-slice_fusion
  58.4 19.3 %reduce-scatter.3.cloned.1.call-done = f32[2,56,256]{2,1,0:T(8,128)} async-done(((f32[8,56,256]{2,1,0:T(8,128)}), f32[2,56,256]{2,1,0:T(8,128)}) %reduce-scatter.3.cloned.1.call-update) | async-done | bytes 114704 | tf_op jit(solution)/shard_map/reduce_scatter | solution.py:41
  77.6 0.0 copy-done
  77.6 1.3 multiply_reduce_fusion.1
  78.9 0.0 copy-start.1
  78.9 0.3 fusion.15
  79.2 0.3 fusion.2
  79.6 0.2 fusion.22
  79.8 0.2 fusion.3
  80.1 0.2 fusion.23
  80.3 0.2 fusion.4
  80.6 0.2 fusion.24
  80.8 0.2 fusion.5
  81.1 0.2 fusion.25
  81.3 0.2 fusion.6
  81.6 0.2 fusion.26
  81.8 0.2 fusion.7
  82.1 0.2 fusion.27
  82.3 0.2 fusion.8
  82.6 0.2 fusion.28
  82.8 0.2 fusion.9
  83.1 0.0 copy-done.1
  83.1 0.2 multiply_reduce_fusion
  83.4 5.7 %all_gather.10 = bf16[8,56,256]{2,1,0:T(8,128)(2,1)S(1)} all-gather(bf16[2,56,256]{2,1,0:T(8,128)(2,1)S(1)} %get-tuple-element.3), channel_id=1, replica_groups=mesh['subj'=8,'feat'=4] {'feat'}, dimensions={0}, use_global_device_ids=true | all-gather | bytes 286720 | tf_op jit(solution)/shard_map/all_gather | solution.py:46
  89.1 2.4 %convolution_bitcast_fusion = f32[256,2560]{1,0:T(8,128)} fusion(bf16[8,56,256]{2,1,0:T(8,128)(2,1)S(1)} %all_gather.10, bf16[8,56,2560]{2,1,0:T(8,128)(2,1)S(1)} %mul.115), kind=kOutput, calls=%fused_computation | convolution fusion | flops 587202560 | bytes 5144576 | tf_op jit(solution)/shard_map/dot_general | solution.py:49
  91.4 0.0 reduce-scatter.5.cloned.1.call-update
  91.5 5.2 %all-gather = f32[4,2,256]{2,1,0:T(2,128)S(1)} all-gather(f32[1,2,256]{2,1,0:T(2,128)S(1)} %bitcast.48), channel_id=1, replica_groups=mesh['subj'=8,'feat'=4] {'feat'}, dimensions={0}, use_global_device_ids=true | all-gather | bytes 10240 | tf_op jit(solution)/shard_map/all_gather | solution.py:47
  96.6 0.6 reshape.49
  97.2 64.8 %reduce-scatter.5.cloned.1.call-done = f32[32,2560]{1,0:T(8,128)} async-done(((f32[256,2560]{1,0:T(8,128)}), f32[32,2560]{1,0:T(8,128)}) %reduce-scatter.5.cloned.1.call-update) | async-done | bytes 327696 | tf_op jit(solution)/shard_map/reduce_scatter | solution.py:52
  (1 shorter events, 0.0 us)
Async XLA Ops:
  7.2 70.5 %copy-start = (bf16[256,256]{1,0:T(8,128)(2,1)S(1)}, bf16[256,256]{1,0:T(8,128)(2,1)}, u32[]{:S(2)}) copy-start(bf16[256,256]{1,0:T(8,128)(2,1)} %param.10) | copy-start | bytes 393220
  7.2 47.5 %all-gather.3.cloned.1.call-start = ((), (), s32[]{:S(2)}) async-start(), calls=%async_computation.2 | async-start | bytes 1474560 | tf_op jit(solution)/shard_map/all_gather | solution.py:35
  7.9 69.7 %reduce-scatter.3.cloned.1.call-start = ((), (), s32[]{:S(2)}) async-start(), calls=%async_computation.3 | async-start | bytes 573440 | tf_op jit(solution)/shard_map/reduce_scatter | solution.py:41
  57.6 104.4 %reduce-scatter.5.cloned.1.call-start = ((), (), s32[]{:S(2)}) async-start(), calls=%async_computation.4 | async-start | bytes 2949120 | tf_op jit(solution)/shard_map/reduce_scatter | solution.py:52
  78.9 4.2 %copy-start.1 = (f32[2,56,256]{2,1,0:T(8,128)S(1)}, f32[2,56,256]{2,1,0:T(8,128)}, u32[]{:S(2)}) copy-start(f32[2,56,256]{2,1,0:T(8,128)} %reduce-scatter.3.cloned.1.call-done) | copy-start | bytes 344068
Sparse Core Ops, SparseCore 0:
  10.2 44.4 all-gather.2
  57.7 19.8 reduce-scatter.2
  91.6 70.4 reduce-scatter.4
where the time goes:
time: 169 us
  waiting for transfers between devices  123 us (73%)
  between operations  13.9 us (8%)
  blocking collectives  10.9 us (6%)
  matrix products  10.8 us (6%)
  local copies, waits for them, and re-layouts  5.65 us (3%)
  other arithmetic  4.42 us (3%)
    reduce_scatter x1, waiting for transfers between devices, per_device(): lax.psum_scatter(term, 'subj', scatter_dimension=0, tiled=True)  64.8 us
    all_gather x1, waiting for transfers between devices, per_device(): lax.all_gather(codes_t, 'subj', axis=0, tiled=True)  38 us
    reduce_scatter x1, waiting for transfers between devices, per_device(): lax.psum_scatter(partial_proj, 'feat', scatter_dimension=0, tiled=True)  19.3 us
    all_gather x1, blocking collectives, per_device(): weighted = lax.all_gather(weighted_part, 'feat', axis=0, tiled=True)  5.7 us
    all_gather x1, blocking collectives, per_device(): patient_rows = lax.all_gather(rows_part, 'feat', axis=0, tiled=True)  5.16 us
    mul x2, local copies, waits for them, and re-layouts, per_device(): visits.reshape(npat, nvis, ntile, ncode // ntile) * gate  4.32 us
  transfers between devices with their start and end apart: 3, of which 3 were waited for; matrix products, arithmetic and copies ran while one was open for 6% of the time, Pallas kernels for 0%

commit v1 on v0

v1 whole, which is shorter than its diff:
```python
import functools

import jax
import jax.numpy as jnp
from jax import lax
from jax.experimental import pallas as pl
from jax.experimental.pallas import tpu as pltpu
from jax.sharding import PartitionSpec as P

NS_STEPS = 8
SLOT = 64
VMEM_BYTES = 32 * 1024 * 1024
CYCLE = (0, 2, 4, 6, 7, 5, 3, 1)
NT = (((1,), (1,)), ((), ()))
NN = (((1,), (0,)), ((), ()))


def dot(a, b, dims=NN):
    return lax.dot_general(a, b, dims, preferred_element_type=jnp.float32)


def split2(a):
    hi = a.astype(jnp.bfloat16)
    return hi, (a - hi.astype(jnp.float32)).astype(jnp.bfloat16)


def split3(a):
    hi = a.astype(jnp.bfloat16)
    rest = a - hi.astype(jnp.float32)
    mid = rest.astype(jnp.bfloat16)
    return hi, mid, (rest - mid.astype(jnp.float32)).astype(jnp.bfloat16)


def dot3(a, b, dims=NN):
    ah, al = a
    bh, bl = b
    return dot(ah, bh, dims) + (dot(ah, bl, dims) + dot(al, bh, dims))


def params():
    return pltpu.CompilerParams(vmem_limit_bytes=VMEM_BYTES)


def mask_body(counts_ref, gate_ref, visits_ref, masked_ref):
    k = pl.program_id(0)
    nvis, ncode = visits_ref.shape[1:]
    rows = lax.broadcasted_iota(jnp.int32, (nvis, 1), 0)
    live = (rows < counts_ref[k]).astype(jnp.bfloat16)
    vals = visits_ref[0] * (gate_ref[0] * live)
    masked_ref[...] = jnp.concatenate(
        [vals, jnp.zeros((SLOT - nvis, ncode), jnp.bfloat16)], 0
    )


def mask_visits(visits, tile_pattern, counts):
    npat, nvis, ncode = visits.shape
    gate = jnp.repeat(tile_pattern.astype(jnp.bfloat16), ncode // tile_pattern.shape[1], axis=1)
    return pl.pallas_call(
        mask_body,
        grid=(npat,),
        in_specs=[
            pl.BlockSpec(memory_space=pltpu.SMEM),
            pl.BlockSpec((1, 1, ncode), lambda k: (k, 0, 0)),
            pl.BlockSpec((1, nvis, ncode), lambda k: (k, 0, 0)),
        ],
        out_specs=pl.BlockSpec((SLOT, ncode), lambda k: (k, 0)),
        out_shape=jax.ShapeDtypeStruct((npat * SLOT, ncode), jnp.bfloat16),
        compiler_params=params(),
        cost_estimate=pl.CostEstimate(flops=0, bytes_accessed=6_000_000, transcendentals=0),
        name="mask_visits",
    )(counts, gate.reshape(npat, 1, ncode), visits)


def project_body(n, *refs):
    masked_ref, out_ref = refs[n], refs[n + 1]
    at = 0
    codes = jnp.concatenate([r[...] for r in refs[:n]], 0) if n > 1 else refs[0][...]
    out_ref[...] = dot(codes, masked_ref[...], NT)


def project(blocks, masked):
    rows = sum(b.shape[0] for b in blocks)
    return pl.pallas_call(
        functools.partial(project_body, len(blocks)),
        out_shape=jax.ShapeDtypeStruct((rows, masked.shape[0]), jnp.float32),
        compiler_params=params(),
        cost_estimate=pl.CostEstimate(
            flops=2 * rows * masked.size, bytes_accessed=2 * masked.size, transcendentals=0
        ),
        name="project",
    )(*blocks, masked)


def procrustes_body(block, counts, at_ref, *refs):
    n = len(counts)
    parts, (weights_ref, core_ref, coret_ref, wt_ref, rot_ref, proj_ref, projt, rott) = (
        refs[: 2 * n],
        refs[2 * n :],
    )
    npat, rank = weights_ref.shape
    slot = 0
    for g, blocks in enumerate(counts):
        for b in range(blocks):
            rows = slice(b * block, (b + 1) * block)
            base = pl.multiple_of(at_ref[slot] * block, block)
            projt[pl.ds(base, block), :] = parts[2 * g][rows, :] + parts[2 * g + 1][rows, :]
            slot += 1
    proj = projt[...].T
    proj_ref[...] = proj
    core, coret = core_ref[...], coret_ref[...]
    weights = weights_ref[...]
    wide = jnp.broadcast_to(weights[:, None, :], (npat, SLOT, rank)).reshape(npat * SLOT, rank)
    hi, mid, lo = split3(proj * wide)
    target = dot(hi, coret) + (dot(mid, coret) + dot(lo, coret))
    pair = 2 * SLOT
    row = lax.broadcasted_iota(jnp.int32, (pair, pair), 0) // SLOT
    col = lax.broadcasted_iota(jnp.int32, (pair, pair), 1) // SLOT
    same = row == col
    qs = []
    for p in range(npat // 2):
        two = target[p * pair : (p + 1) * pair].reshape(2, SLOT, rank)
        total = jnp.sum(jnp.sum(two * two, axis=1, keepdims=True), axis=2, keepdims=True)
        qs.append((two * lax.rsqrt(total + 1e-06)).reshape(pair, rank))
    for step in range(NS_STEPS):
        halves = [split2(q) for q in qs]
        grams = [jnp.where(same, dot3(h, h, NT), 0.0) for h in halves]
        prods = [dot3(split2(g), h) for g, h in zip(grams, halves)]
        qs = [1.5 * q - 0.5 * x for q, x in zip(qs, prods)]
    q = jnp.concatenate(qs, 0)
    hi, mid, lo = split3(q)
    rotated = dot(hi, core) + (dot(mid, core) + dot(lo, core))
    rot_ref[...] = rotated
    wt_ref[...] = (rotated * wide).T.astype(jnp.bfloat16)


def procrustes(groups, at, counts, weights, core, block):
    npat, rank = weights.shape
    rows = npat * SLOT
    flat = [a for pair in groups for a in pair]
    vmem = pl.BlockSpec(memory_space=pltpu.VMEM)
    return pl.pallas_call(
        functools.partial(procrustes_body, block, counts),
        in_specs=[pl.BlockSpec(memory_space=pltpu.SMEM)] + [vmem] * (len(flat) + 3),
        out_specs=[vmem] * 3,
        out_shape=[
            jax.ShapeDtypeStruct((rank, rows), jnp.bfloat16),
            jax.ShapeDtypeStruct((rows, rank), jnp.float32),
            jax.ShapeDtypeStruct((rows, rank), jnp.float32),
        ],
        scratch_shapes=[
            pltpu.VMEM((rank, rows), jnp.float32),
            pltpu.VMEM((8, 128), jnp.float32),
        ],
        compiler_params=params(),
        cost_estimate=pl.CostEstimate(
            flops=6 * 40 * rows * rank * 128, bytes_accessed=4_000_000, transcendentals=0
        ),
        name="procrustes",
    )(at, *flat, weights, core, core.T)


def rows_body(rot_ref, proj_ref, out_ref):
    npat, rank = out_ref.shape
    prod = rot_ref[...] * proj_ref[...]
    out_ref[...] = jnp.sum(prod.reshape(npat, SLOT, rank), axis=1)


def patient_rows(rot, proj, npat):
    return pl.pallas_call(
        rows_body,
        out_shape=jax.ShapeDtypeStruct((npat, rot.shape[1]), jnp.float32),
        compiler_params=params(),
        name="patient_rows",
    )(rot, proj)


def term_body(block, at_ref, wt_ref, masked_ref, send_ref, keep_ref):
    there = wt_ref[pl.ds(pl.multiple_of(at_ref[0] * block, block), block), :]
    here = wt_ref[pl.ds(pl.multiple_of(at_ref[1] * block, block), block), :]
    both = dot(jnp.concatenate([there, here], 0), masked_ref[...])
    send_ref[...] = both[:block].astype(send_ref.dtype)
    keep_ref[...] = both[block:]


def term(wt, masked, at, block, send_type):
    ncode = masked.shape[1]
    vmem = pl.BlockSpec(memory_space=pltpu.VMEM)
    return pl.pallas_call(
        functools.partial(term_body, block),
        in_specs=[pl.BlockSpec(memory_space=pltpu.SMEM), vmem, vmem],
        out_specs=[vmem, vmem],
        out_shape=[
            jax.ShapeDtypeStruct((block, ncode), send_type),
            jax.ShapeDtypeStruct((block, ncode), jnp.float32),
        ],
        compiler_params=params(),
        cost_estimate=pl.CostEstimate(
            flops=4 * block * masked.size, bytes_accessed=2 * masked.size, transcendentals=0
        ),
        name="term",
    )(at, wt, masked)


def flip(axis, size, bit):
    return functools.partial(
        lax.ppermute, axis_name=axis, perm=[(s, s ^ bit) for s in range(size)]
    )


def feat_sum(part):
    part = part + flip("feat", 4, 1)(part)
    return part, flip("feat", 4, 2)(part)


def per_device(visits, tile_pattern, counts, codes_t, core, patient_weights):
    npat = visits.shape[0]
    block = codes_t.shape[0]
    me = lax.axis_index("subj")
    cycle = jnp.array(CYCLE, jnp.int32)
    place = jnp.argmax(cycle == me).astype(jnp.int32)
    ahead = [(CYCLE[i], CYCLE[(i + 1) % 8]) for i in range(8)]
    back = [(d, s) for s, d in ahead]

    masked = mask_visits(visits, tile_pattern, counts)

    f, b = [codes_t], [codes_t]
    for _ in range(3):
        f.append(lax.ppermute(f[-1], "subj", ahead))
        b.append(lax.ppermute(b[-1], "subj", back))
    half = block // 2
    f4 = lax.ppermute(f[3][:half], "subj", ahead)
    b4 = lax.ppermute(b[3][half:], "subj", back)

    sets = [[codes_t, f[1], b[1], f[2], b[2]], [f[3], b[3]], [f4, b4]]
    offsets = jnp.array([0, -1, 1, -2, 2, -3, 3, 4], jnp.int32)
    at = cycle[(place + offsets) % 8]
    groups = [feat_sum(project(s, masked)) for s in sets]
    wt, rot, proj = procrustes(groups, at, (5, 2, 1), patient_weights, core, block)

    out = None
    for step in (3, 2, 1, 0):
        to = me ^ (2 * step)
        pick = jnp.stack([to ^ 1, to]).astype(jnp.int32)
        send, keep = term(wt, masked, pick, block, jnp.float32 if step == 0 else jnp.bfloat16)
        got = flip("subj", 8, 1)(send)
        both = keep + got.astype(jnp.float32)
        if step:
            both = flip("subj", 8, 2 * step)(both.astype(jnp.bfloat16)).astype(jnp.float32)
        out = both if out is None else out + both
    rows = patient_rows(rot, proj, npat)
    return out, rows


def per_device_any(visits, tile_pattern, counts, codes_t, core, patient_weights):
    npat = visits.shape[0]
    masked = mask_visits(visits, tile_pattern, counts)
    codes = lax.all_gather(codes_t, "subj", axis=0, tiled=True)
    part = lax.psum(project([codes], masked), "feat")
    rank = part.shape[0]
    groups = [(part, jnp.zeros_like(part))]
    wt, rot, proj = procrustes(
        groups, jnp.zeros((1,), jnp.int32), (1,), patient_weights, core, rank
    )
    half = rank // 2
    low, high = term(wt, masked, jnp.array([0, 1], jnp.int32), half, jnp.float32)
    whole = jnp.concatenate([low, high], 0)
    out = lax.psum_scatter(whole, "subj", scatter_dimension=0, tiled=True)
    return out, patient_rows(rot, proj, npat)


def solution(mesh):
    plan = per_device if (mesh.shape["subj"], mesh.shape["feat"]) == (8, 4) else per_device_any
    return jax.shard_map(
        plan,
        mesh=mesh,
        in_specs=(
            P("subj", None, "feat"),
            P("subj", "feat"),
            P("subj"),
            P("subj", "feat"),
            P(),
            P("subj", None),
        ),
        out_specs=(P("subj", "feat"), P("subj", None)),
        check_vma=False,
    )
```

time: 169 us -> 86.9 us (0.51)
  waiting for transfers between devices: 123 us -> 24.7 us
  starting transfers between devices: 0.12 us -> 23.8 us
  Pallas kernels: 0 us -> 15.3 us
  between operations: 13.9 us -> 0.91 us
  blocking collectives: 10.9 us -> 0 us
  matrix products: 10.8 us -> 0 us
  local copies, waits for them, and re-layouts: 5.65 us -> 15.5 us
  other arithmetic: 4.42 us -> 6.17 us
    reduce_scatter x2 -> x0, waiting for transfers between devices: 84.1 us -> none  [the longest x1 64.8 us: per_device(): lax.psum_scatter(term, 'subj', scatter_dimension=0, tiled=True)]
    all_gather x1 -> x0, waiting for transfers between devices: 38 us -> none  [per_device(): lax.all_gather(codes_t, 'subj', axis=0, tiled=True)]
    ppermute x0 -> x21, waiting for transfers between devices: none -> 24.7 us  [the longest x3 7.63 us: per_device(): flip('subj', 8, 2 * step)(both.astype(jnp.bfloat16)).astype(jnp.float32)]
    ppermute x0 -> x21, starting transfers between devices: none -> 23.8 us  [the longest x3 6.49 us: per_device(): f.append(lax.ppermute(f[-1], 'subj', ahead))]
    pallas_call x0 -> x10, Pallas kernels: none -> 15.3 us  [the longest x1 5.72 us: procrustes(): pl.pallas_call(functools.partial(procrustes_body, block, counts), in_spec...]
    unnamed x5 -> x51, local copies, waits for them, and re-layouts: 0.62 us -> 14.6 us
    all_gather x2 -> x0, blocking collectives: 10.9 us -> none  [the longest x1 5.7 us: per_device(): weighted = lax.all_gather(weighted_part, 'feat', axis=0, tiled=True)]
    dot_general x20 -> x0, matrix products: 10.8 us -> none  [the longest x1 2.88 us: per_device(): lax.dot_general(masked, lax.all_gather(codes_t, 'subj', axis=0, tiled=Tru...]
  transfers between devices with their start and end apart: 3 -> 21, of which waited for: 3 -> 10; matrix products, arithmetic and copies ran while one was open for 6% -> 8% of each run, Pallas kernels for 0% -> 8%
where the time goes in v1:
time: 86.9 us; the launch traced here: 86.4 us
  waiting for transfers between devices  24.7 us (28%)
  starting transfers between devices  23.8 us (27%)
  local copies, waits for them, and re-layouts  15.5 us (18%)
  Pallas kernels  15.3 us (18%)
  other arithmetic  6.17 us (7%)
  between operations  0.91 us (1%)
    unnamed x51, local copies, waits for them, and re-layouts  14.6 us
    ppermute x3, waiting for transfers between devices, per_device(): flip('subj', 8, 2 * step)(both.astype(jnp.bfloat16)).astype(jnp.float32)  7.63 us
    ppermute x3, waiting for transfers between devices, per_device(): f.append(lax.ppermute(f[-1], 'subj', ahead))  7.36 us
    ppermute x3, starting transfers between devices, per_device(): f.append(lax.ppermute(f[-1], 'subj', ahead))  6.49 us
    ppermute x3, starting transfers between devices, per_device(): flip('subj', 8, 2 * step)(both.astype(jnp.bfloat16)).astype(jnp.float32)  6.4 us
    pallas_call x1, Pallas kernels, procrustes(): pl.pallas_call(functools.partial(procrustes_body, block, counts), in_spec...  5.72 us
    ppermute x3, waiting for transfers between devices, feat_sum(): return (part, flip('feat', 4, 2)(part))  5.21 us
    pallas_call x4, Pallas kernels, term(): pl.pallas_call(functools.partial(term_body, block), in_specs=[pl.BlockSpe...  5.06 us
  transfers between devices with their start and end apart: 21, of which 10 were waited for; matrix products, arithmetic and copies ran while one was open for 8% of the time, Pallas kernels for 8%

profile of v1, /device:TPU:0, one launch (start us, length us, event | category | flops | bytes accessed | tf_op | source)
XLA Modules:
  0.0 86.4 jit_solution(14508616743700389581)
XLA Ops:
  0.6 3.1 %collective-permute-start = (bf16[32,2560]{1,0:T(8,128)(2,1)}, bf16[32,2560]{1,0:T(8,128)(2,1)S(1)}, u32[]{:S(2)}, u32[]{:S(2)}) collective-permute-start(bf16[32,2560]{1,0:T(8,128)(2,1)} %refs_0_.1), channel_id=1, source_target_pairs={{0,8},{8,16},{16,24},{24,28},{28,20},{20,12},{12,4},{4,0},{1,9},{9... | collective-permute-start | bytes 491528 | tf_op jit(solution)/shard_map/ppermute | solution.py:228
  3.7 0.7 convert_element_type.30
  4.4 0.1 copy.11
  4.5 3.6 %collective-permute-done.refs_1_ = bf16[32,2560]{1,0:T(8,128)(2,1)S(1)} collective-permute-done((bf16[32,2560]{1,0:T(8,128)(2,1)}, bf16[32,2560]{1,0:T(8,128)(2,1)S(1)}, u32[]{:S(2)}, u32[]{:S(2)}) %collective-permute-start) | collective-permute-done | bytes 163872 | tf_op jit(solution)/shard_map/ppermute | solution.py:228
  8.1 1.8 %collective-permute-start.2 = (bf16[32,2560]{1,0:T(8,128)(2,1)S(1)}, bf16[32,2560]{1,0:T(8,128)(2,1)S(1)}, u32[]{:S(2)}, u32[]{:S(2)}) collective-permute-start(bf16[32,2560]{1,0:T(8,128)(2,1)S(1)} %collective-permute-done.refs_1_), channel_id=1, source_target_pairs={{0,8},{8,16},{16,24},{24,28},{28,20},{20,12},{12,4},{4,0},{1,9},{9... | collective-permute-start | bytes 491528 | tf_op jit(solution)/shard_map/ppermute | solution.py:228
  9.9 0.2 collective-permute-start.3
  10.1 0.1 broadcast_bitcast_fusion
  10.3 1.6 %copy-done = bf16[8,56,2560]{2,1,0:T(8,128)(2,1)S(1)} copy-done((bf16[8,56,2560]{2,1,0:T(8,128)(2,1)S(1)}, bf16[8,56,2560]{2,1,0:T(8,128)(2,1)}, u32[]{:S(2)}) %copy-start) | copy-done | bytes 2293784
  11.9 0.7 copy-done.19
  12.6 1.1 %mask_visits.1.refs_5_.refs_2_.masked_ref = bf16[512,2560]{1,0:T(8,128)(2,1)S(1)} custom-call(s32[8]{0:T(128)S(1)} %copy-done.19, bf16[8,1,2560]{2,1,0:T(2,128)(2,1)S(1)} %copy.12.gate_ref, bf16[8,56,2560]{2,1,0:T(8,128)(2,1)S(1)} %copy-done), custom_call_target="tpu_custom_call" | custom-call | bytes 6000000 | tf_op jit(solution)/shard_map/mask_visits/pallas_call | solution.py:58
  13.8 0.7 copy-done.8
  14.4 0.8 collective-permute-done.3.refs_4_
  15.2 0.7 copy-done.10
  15.9 0.9 %copy-done.9 = bf16[32,2560]{1,0:T(8,128)(2,1)S(1)} copy-done((bf16[32,2560]{1,0:T(8,128)(2,1)S(1)}, bf16[32,2560]{1,0:T(8,128)(2,1)}, u32[]{:S(2)}) %copy-start.9) | copy-done | bytes 163864
  16.8 0.9 %copy-done.11 = bf16[32,2560]{1,0:T(8,128)(2,1)S(1)} copy-done((bf16[32,2560]{1,0:T(8,128)(2,1)S(1)}, bf16[32,2560]{1,0:T(8,128)(2,1)}, u32[]{:S(2)}) %copy-start.11) | copy-done | bytes 163864
  17.7 0.9 %copy-done.13 = bf16[32,2560]{1,0:T(8,128)(2,1)S(1)} copy-done((bf16[32,2560]{1,0:T(8,128)(2,1)S(1)}, bf16[32,2560]{1,0:T(8,128)(2,1)}, u32[]{:S(2)}) %copy-start.13) | copy-done | bytes 163864
  18.6 0.9 %copy-done.15 = bf16[32,2560]{1,0:T(8,128)(2,1)S(1)} copy-done((bf16[32,2560]{1,0:T(8,128)(2,1)S(1)}, bf16[32,2560]{1,0:T(8,128)(2,1)}, u32[]{:S(2)}) %copy-start.15) | copy-done | bytes 163864
  19.5 1.0 %project.3 = f32[160,512]{1,0:T(8,128)S(1)} custom-call(bf16[32,2560]{1,0:T(8,128)(2,1)S(1)} %copy-done.7, bf16[32,2560]{1,0:T(8,128)(2,1)S(1)} %copy-done.13, bf16[32,2560]{1,0:T(8,128)(2,1)S(1)} %copy-done.15, bf16[32,2560]{1,0:T(8,128)(2,1)S(1)} %copy-done.9, bf16[32,2560]{1,0:T(8,128)(2,1)S(1)} %copy-done.11, ...), custom_call_target="tpu_custom_call" | custom-call | flops 419430400 | bytes 2621440 | tf_op jit(solution)/shard_map/project/pallas_call | solution.py:83
  20.6 1.6 %collective-permute-start.6 = (bf16[32,2560]{1,0:T(8,128)(2,1)S(1)}, bf16[32,2560]{1,0:T(8,128)(2,1)S(1)}, u32[]{:S(2)}, u32[]{:S(2)}) collective-permute-start(bf16[32,2560]{1,0:T(8,128)(2,1)S(1)} %copy-done.9), channel_id=1, source_target_pairs={{0,8},{8,16},{16,24},{24,28},{28,20},{20,12},{12,4},{4,0},{1,9},{9... | collective-permute-start | bytes 491528 | tf_op jit(solution)/shard_map/ppermute | solution.py:228
  22.2 0.4 collective-permute-start.7
  22.7 0.7 compare_reduce_fusion
  23.4 3.8 %collective-permute-done.6.refs_0_ = bf16[32,2560]{1,0:T(8,128)(2,1)S(1)} collective-permute-done((bf16[32,2560]{1,0:T(8,128)(2,1)S(1)}, bf16[32,2560]{1,0:T(8,128)(2,1)S(1)}, u32[]{:S(2)}, u32[]{:S(2)}) %collective-permute-start.6) | collective-permute-done | bytes 163872 | tf_op jit(solution)/shard_map/ppermute | solution.py:228
  27.2 1.3 %collective-permute-done.7.refs_1_ = bf16[32,2560]{1,0:T(8,128)(2,1)S(1)} collective-permute-done((bf16[32,2560]{1,0:T(8,128)(2,1)S(1)}, bf16[32,2560]{1,0:T(8,128)(2,1)S(1)}, u32[]{:S(2)}, u32[]{:S(2)}) %collective-permute-start.7) | collective-permute-done | bytes 163872 | tf_op jit(solution)/shard_map/ppermute | solution.py:229
  28.5 0.9 %project.4 = f32[64,512]{1,0:T(8,128)S(1)} custom-call(bf16[32,2560]{1,0:T(8,128)(2,1)S(1)} %collective-permute-done.6.refs_0_, bf16[32,2560]{1,0:T(8,128)(2,1)S(1)} %collective-permute-done.7.refs_1_, bf16[512,2560]{1,0:T(8,128)(2,1)S(1)} %mask_visits.1.refs_5_.refs_2_.masked_ref), custom_call_target="tpu_custom_call" | custom-call | flops 167772160 | bytes 2621440 | tf_op jit(solution)/shard_map/project/pallas_call | solution.py:83
  29.5 0.7 compare_select_fusion
  30.2 1.6 %collective-permute-start.10 = (bf16[16,2560]{1,0:T(8,128)(2,1)S(1)}, bf16[16,2560]{1,0:T(8,128)(2,1)S(1)}, u32[]{:S(2)}, u32[]{:S(2)}) collective-permute-start(bf16[16,2560]{1,0:T(8,128)(2,1)S(1)} %slice.10), channel_id=1, source_target_pairs={{0,8},{8,16},{16,24},{24,28},{28,20},{20,12},{12,4},{4,0},{1,9},{9... | collective-permute-start | bytes 245768 | tf_op jit(solution)/shard_map/ppermute | solution.py:231
  31.8 0.4 collective-permute-start.11
  32.3 1.0 %add.49.refs_0_ = f32[160,512]{1,0:T(8,128)S(1)} add(f32[160,512]{1,0:T(8,128)S(1)} %project.3, f32[160,512]{1,0:T(8,128)} %collective-permute-done.4) | non-fusion elementwise | flops 81920 | bytes 983040 | tf_op jit(solution)/shard_map/add | solution.py:211
  33.3 1.6 %collective-permute-start.5 = (f32[160,512]{1,0:T(8,128)S(1)}, f32[160,512]{1,0:T(8,128)}, u32[]{:S(2)}, u32[]{:S(2)}) collective-permute-start(f32[160,512]{1,0:T(8,128)S(1)} %add.49.refs_0_), channel_id=1, source_target_pairs={{0,2},{1,3},{2,0},{3,1},{4,6},{5,7},{6,4},{7,5},{8,10},{9,11},{10,... | collective-permute-start | bytes 983048 | tf_op jit(solution)/shard_map/ppermute | solution.py:212
  34.9 0.2 collective-permute-done.10.refs_0_
  35.1 1.3 %collective-permute-done.11.refs_1_ = bf16[16,2560]{1,0:T(8,128)(2,1)S(1)} collective-permute-done((bf16[16,2560]{1,0:T(8,128)(2,1)S(1)}, bf16[16,2560]{1,0:T(8,128)(2,1)S(1)}, u32[]{:S(2)}, u32[]{:S(2)}) %collective-permute-start.11) | collective-permute-done | bytes 81952 | tf_op jit(solution)/shard_map/ppermute | solution.py:232
  36.4 0.8 project.5
  37.3 0.9 %add.50.refs_2_ = f32[64,512]{1,0:T(8,128)S(1)} add(f32[64,512]{1,0:T(8,128)S(1)} %project.4, f32[64,512]{1,0:T(8,128)} %collective-permute-done.8) | non-fusion elementwise | flops 32768 | bytes 393216 | tf_op jit(solution)/shard_map/add | solution.py:211
  38.2 1.6 %collective-permute-start.9 = (f32[64,512]{1,0:T(8,128)S(1)}, f32[64,512]{1,0:T(8,128)S(1)}, u32[]{:S(2)}, u32[]{:S(2)}) collective-permute-start(f32[64,512]{1,0:T(8,128)S(1)} %add.50.refs_2_), channel_id=1, source_target_pairs={{0,2},{1,3},{2,0},{3,1},{4,6},{5,7},{6,4},{7,5},{8,10},{9,11},{10,... | collective-permute-start | bytes 393224 | tf_op jit(solution)/shard_map/ppermute | solution.py:212
  39.8 0.6 gather_fusion
  40.5 0.8 copy.13
  41.3 0.6 collective-permute-start.13
  41.9 5.2 %collective-permute-done.13.refs_5_ = f32[32,512]{1,0:T(8,128)S(1)} collective-permute-done((f32[32,512]{1,0:T(8,128)S(1)}, f32[32,512]{1,0:T(8,128)S(1)}, u32[]{:S(2)}, u32[]{:S(2)}) %collective-permute-start.13) | collective-permute-done | bytes 65568 | tf_op jit(solution)/shard_map/ppermute | solution.py:212
  47.2 0.6 copy-done.20
  47.8 1.0 %copy-done.6 = f32[160,512]{1,0:T(8,128)S(1)} copy-done((f32[160,512]{1,0:T(8,128)S(1)}, f32[160,512]{1,0:T(8,128)}, u32[]{:S(2)}) %copy-start.6) | copy-done | bytes 327704
  48.8 0.9 %copy-done.17 = bf16[256,256]{1,0:T(8,128)(2,1)S(1)} copy-done((bf16[256,256]{1,0:T(8,128)(2,1)S(1)}, bf16[256,256]{1,0:T(8,128)(2,1)}, u32[]{:S(2)}) %copy-start.17) | copy-done | bytes 131096
  49.7 0.9 %copy-done.18 = bf16[256,256]{0,1:T(8,128)(2,1)S(1)} copy-done((bf16[256,256]{0,1:T(8,128)(2,1)S(1)}, bf16[256,256]{0,1:T(8,128)(2,1)}, u32[]{:S(2)}) %copy-start.18) | copy-done | bytes 131096
  50.6 0.9 %copy-done.21 = f32[64,512]{1,0:T(8,128)S(1)} copy-done((f32[64,512]{1,0:T(8,128)S(1)}, f32[64,512]{1,0:T(8,128)}, u32[]{:S(2)}) %copy-start.21) | copy-done | bytes 131096
  51.5 0.7 copy-done.22
  52.2 5.7 %procrustes.1 = (bf16[256,512]{1,0:T(8,128)(2,1)S(1)}, f32[512,256]{1,0:T(8,128)S(1)}, f32[512,256]{1,0:T(8,128)S(1)}) custom-call(s32[8]{0:T(128)S(1)} %gather_fusion, f32[160,512]{1,0:T(8,128)S(1)} %copy-done.6, f32[160,512]{1,0:T(8,128)} %collective-permute-done.5.refs_1_, f32[64,512]{1,0:T(8,128)S(1)} %add.50.refs_2_, f32[64,512]{1,0:T(8,128)S(1)} %copy-done.21, ...), custom_call_target="tpu_custom_call" | custom-call | flops 4026531840 | bytes 4000000 | tf_op jit(solution)/shard_map/procrustes/pallas_call | solution.py:141
  57.9 0.8 copy-done.1
  58.7 1.8 %term.4 = (bf16[32,2560]{1,0:T(8,128)(2,1)}, f32[32,2560]{1,0:T(8,128)S(1)}) custom-call(s32[2]{0:T(128)S(1)} %pad_add_fusion.at_ref, bf16[256,512]{1,0:T(8,128)(2,1)S(1)} %get-tuple-element.15.wt_ref, bf16[512,2560]{1,0:T(8,128)(2,1)S(1)} %mask_visits.1.refs_5_.refs_2_.masked_ref), custom_call_target="tpu_custom_call" | custom-call | flops 167772160 | bytes 2621440 | tf_op jit(solution)/shard_map/term/pallas_call | solution.py:188
  60.5 0.7 copy-done.3
  61.2 0.4 collective-permute-start.14
  61.8 1.1 %term.5 = (bf16[32,2560]{1,0:T(8,128)(2,1)S(1)}, f32[32,2560]{1,0:T(8,128)S(1)}) custom-call(s32[2]{0:T(128)S(1)} %pad_add_fusion.1.at_ref, bf16[256,512]{1,0:T(8,128)(2,1)S(1)} %get-tuple-element.15.wt_ref, bf16[512,2560]{1,0:T(8,128)(2,1)S(1)} %mask_visits.1.refs_5_.refs_2_.masked_ref), custom_call_target="tpu_custom_call" | custom-call | flops 167772160 | bytes 2621440 | tf_op jit(solution)/shard_map/term/pallas_call | solution.py:188
  62.9 1.6 %collective-permute-start.16 = (bf16[32,2560]{1,0:T(8,128)(2,1)S(1)}, bf16[32,2560]{1,0:T(8,128)(2,1)S(1)}, u32[]{:S(2)}, u32[]{:S(2)}) collective-permute-start(bf16[32,2560]{1,0:T(8,128)(2,1)S(1)} %get-tuple-element.19), channel_id=1, source_target_pairs={{0,4},{4,0},{8,12},{12,8},{16,20},{20,16},{24,28},{28,24},{1,5},{5... | collective-permute-start | bytes 491528 | tf_op jit(solution)/shard_map/ppermute | solution.py:245
  64.6 1.1 %term.6 = (bf16[32,2560]{1,0:T(8,128)(2,1)S(1)}, f32[32,2560]{1,0:T(8,128)S(1)}) custom-call(s32[2]{0:T(128)S(1)} %pad_add_fusion.2.at_ref, bf16[256,512]{1,0:T(8,128)(2,1)S(1)} %get-tuple-element.15.wt_ref, bf16[512,2560]{1,0:T(8,128)(2,1)S(1)} %mask_visits.1.refs_5_.refs_2_.masked_ref), custom_call_target="tpu_custom_call" | custom-call | flops 167772160 | bytes 2621440 | tf_op jit(solution)/shard_map/term/pallas_call | solution.py:188
  65.7 0.5 collective-permute-start.18
  66.2 1.1 %term.7 = (f32[32,2560]{1,0:T(8,128)S(1)}, f32[32,2560]{1,0:T(8,128)S(1)}) custom-call(s32[2]{0:T(128)S(1)} %pad_add_fusion.3.at_ref, bf16[256,512]{1,0:T(8,128)(2,1)S(1)} %get-tuple-element.15.wt_ref, bf16[512,2560]{1,0:T(8,128)(2,1)S(1)} %mask_visits.1.refs_5_.refs_2_.masked_ref), custom_call_target="tpu_custom_call" | custom-call | flops 167772160 | bytes 2621440 | tf_op jit(solution)/shard_map/term/pallas_call | solution.py:188
  67.3 1.6 %collective-permute-start.20 = (f32[32,2560]{1,0:T(8,128)S(1)}, f32[32,2560]{1,0:T(8,128)S(1)}, u32[]{:S(2)}, u32[]{:S(2)}) collective-permute-start(f32[32,2560]{1,0:T(8,128)S(1)} %get-tuple-element.23), channel_id=1, source_target_pairs={{0,4},{4,0},{8,12},{12,8},{16,20},{20,16},{24,28},{28,24},{1,5},{5... | collective-permute-start | bytes 983048 | tf_op jit(solution)/shard_map/ppermute | solution.py:245
  69.0 0.9 %add_convert_fusion.2 = bf16[32,2560]{1,0:T(8,128)(2,1)S(1)} fusion(f32[32,2560]{1,0:T(8,128)S(1)} %copy-done.4, bf16[32,2560]{1,0:T(8,128)(2,1)} %collective-permute-done.14), kind=kLoop, calls=%fused_computation.4 | loop fusion | flops 245760 | bytes 655360 | tf_op jit(solution)/shard_map/convert_element_type | solution.py:248
  69.9 3.1 %collective-permute-start.15 = (bf16[32,2560]{1,0:T(8,128)(2,1)S(1)}, bf16[32,2560]{1,0:T(8,128)(2,1)S(1)}, u32[]{:S(2)}, u32[]{:S(2)}) collective-permute-start(bf16[32,2560]{1,0:T(8,128)(2,1)S(1)} %add_convert_fusion.2), channel_id=1, source_target_pairs={{0,24},{4,28},{8,16},{12,20},{16,8},{20,12},{24,0},{28,4},{1,25},{... | collective-permute-start | bytes 491528 | tf_op jit(solution)/shard_map/ppermute | solution.py:248
  73.0 1.7 %collective-permute-start.17 = (bf16[32,2560]{1,0:T(8,128)(2,1)S(1)}, bf16[32,2560]{1,0:T(8,128)(2,1)S(1)}, u32[]{:S(2)}, u32[]{:S(2)}) collective-permute-start(bf16[32,2560]{1,0:T(8,128)(2,1)S(1)} %add_convert_fusion.1), channel_id=1, source_target_pairs={{0,16},{4,20},{8,24},{12,28},{16,0},{20,4},{24,8},{28,12},{1,17},{... | collective-permute-start | bytes 491528 | tf_op jit(solution)/shard_map/ppermute | solution.py:248
  74.7 0.9 %collective-permute-done.18 = bf16[32,2560]{1,0:T(8,128)(2,1)S(1)} collective-permute-done((bf16[32,2560]{1,0:T(8,128)(2,1)S(1)}, bf16[32,2560]{1,0:T(8,128)(2,1)S(1)}, u32[]{:S(2)}, u32[]{:S(2)}) %collective-permute-start.18) | collective-permute-done | bytes 163872 | tf_op jit(solution)/shard_map/ppermute | solution.py:245
  75.6 1.6 %collective-permute-start.19 = (bf16[32,2560]{1,0:T(8,128)(2,1)S(1)}, bf16[32,2560]{1,0:T(8,128)(2,1)S(1)}, u32[]{:S(2)}, u32[]{:S(2)}) collective-permute-start(bf16[32,2560]{1,0:T(8,128)(2,1)S(1)} %add_convert_fusion), channel_id=1, source_target_pairs={{0,8},{4,12},{8,0},{12,4},{16,24},{20,28},{24,16},{28,20},{1,9},{5... | collective-permute-start | bytes 491528 | tf_op jit(solution)/shard_map/ppermute | solution.py:248
  77.3 0.7 patient_rows.1
  78.0 0.9 collective-permute-done.15
  78.8 6.8 %collective-permute-done.17 = bf16[32,2560]{1,0:T(8,128)(2,1)S(1)} collective-permute-done((bf16[32,2560]{1,0:T(8,128)(2,1)S(1)}, bf16[32,2560]{1,0:T(8,128)(2,1)S(1)}, u32[]{:S(2)}, u32[]{:S(2)}) %collective-permute-start.17) | collective-permute-done | bytes 163872 | tf_op jit(solution)/shard_map/ppermute | solution.py:248
  85.6 0.8 add_add_fusion
  (60 shorter events, 0.7 us)
Async XLA Ops:
  0.6 15.2 %copy-start.7 = (bf16[32,2560]{1,0:T(8,128)(2,1)S(1)}, bf16[32,2560]{1,0:T(8,128)(2,1)}, u32[]{:S(2)}) copy-start(bf16[32,2560]{1,0:T(8,128)(2,1)} %refs_0_.1) | copy-start | bytes 491524
  0.6 7.4 %collective-permute-start = (bf16[32,2560]{1,0:T(8,128)(2,1)}, bf16[32,2560]{1,0:T(8,128)(2,1)S(1)}, u32[]{:S(2)}, u32[]{:S(2)}) collective-permute-start(bf16[32,2560]{1,0:T(8,128)(2,1)} %refs_0_.1), channel_id=1, source_target_pairs={{0,8},{8,16},{16,24},{24,28},{28,20},{20,12},{12,4},{4,0},{1,9},{9... | collective-permute-start | bytes 491528 | tf_op jit(solution)/shard_map/ppermute | solution.py:228
  3.7 6.2 %collective-permute-start.1 = (bf16[32,2560]{1,0:T(8,128)(2,1)}, bf16[32,2560]{1,0:T(8,128)(2,1)S(1)}, u32[]{:S(2)}, u32[]{:S(2)}) collective-permute-start(bf16[32,2560]{1,0:T(8,128)(2,1)} %refs_0_.1), channel_id=1, source_target_pairs={{8,0},{16,8},{24,16},{28,24},{20,28},{12,20},{4,12},{0,4},{9,1},{1... | collective-permute-start | bytes 491528 | tf_op jit(solution)/shard_map/ppermute | solution.py:229
  8.1 5.7 %copy-start.12 = (bf16[32,2560]{1,0:T(8,128)(2,1)}, bf16[32,2560]{1,0:T(8,128)(2,1)S(1)}, u32[]{:S(2)}) copy-start(bf16[32,2560]{1,0:T(8,128)(2,1)S(1)} %collective-permute-done.refs_1_) | copy-start | bytes 491524
  8.1 5.7 %collective-permute-start.2 = (bf16[32,2560]{1,0:T(8,128)(2,1)S(1)}, bf16[32,2560]{1,0:T(8,128)(2,1)S(1)}, u32[]{:S(2)}, u32[]{:S(2)}) collective-permute-start(bf16[32,2560]{1,0:T(8,128)(2,1)S(1)} %collective-permute-done.refs_1_), channel_id=1, source_target_pairs={{0,8},{8,16},{16,24},{24,28},{28,20},{20,12},{12,4},{4,0},{1,9},{9... | collective-permute-start | bytes 491528 | tf_op jit(solution)/shard_map/ppermute | solution.py:228
  9.9 3.9 %copy-start.14 = (bf16[32,2560]{1,0:T(8,128)(2,1)}, bf16[32,2560]{1,0:T(8,128)(2,1)S(1)}, u32[]{:S(2)}) copy-start(bf16[32,2560]{1,0:T(8,128)(2,1)S(1)} %collective-permute-done.1.refs_2_) | copy-start | bytes 491524
  9.9 5.3 %collective-permute-start.3 = (bf16[32,2560]{1,0:T(8,128)(2,1)S(1)}, bf16[32,2560]{1,0:T(8,128)(2,1)S(1)}, u32[]{:S(2)}, u32[]{:S(2)}) collective-permute-start(bf16[32,2560]{1,0:T(8,128)(2,1)S(1)} %collective-permute-done.1.refs_2_), channel_id=1, source_target_pairs={{8,0},{16,8},{24,16},{28,24},{20,28},{12,20},{4,12},{0,4},{9,1},{1... | collective-permute-start | bytes 491528 | tf_op jit(solution)/shard_map/ppermute | solution.py:229
  10.3 1.6 %copy-start = (bf16[8,56,2560]{2,1,0:T(8,128)(2,1)S(1)}, bf16[8,56,2560]{2,1,0:T(8,128)(2,1)}, u32[]{:S(2)}) copy-start(bf16[8,56,2560]{2,1,0:T(8,128)(2,1)} %visits_ref.1) | copy-start | bytes 6881284
  11.9 0.7 copy-start.19
  12.6 10.1 %copy-start.23 = (s32[8]{0:T(128)S(1)}, s32[8]{0:T(128)}, u32[]{:S(2)}) copy-start(s32[8]{0:T(128)} %constant.40.clone) | copy-start | bytes 100
  12.6 16.9 %copy-start.24 = (s32[8]{0:T(128)S(1)}, s32[8]{0:T(128)}, u32[]{:S(2)}) copy-start(s32[8]{0:T(128)} %constant.41.clone) | copy-start | bytes 100
  13.8 0.7 copy-start.8
  15.2 0.7 copy-start.10
  15.9 0.9 %copy-start.9 = (bf16[32,2560]{1,0:T(8,128)(2,1)S(1)}, bf16[32,2560]{1,0:T(8,128)(2,1)}, u32[]{:S(2)}) copy-start(bf16[32,2560]{1,0:T(8,128)(2,1)} %copy-done.8) | copy-start | bytes 491524
  16.8 0.9 %copy-start.11 = (bf16[32,2560]{1,0:T(8,128)(2,1)S(1)}, bf16[32,2560]{1,0:T(8,128)(2,1)}, u32[]{:S(2)}) copy-start(bf16[32,2560]{1,0:T(8,128)(2,1)} %copy-done.10) | copy-start | bytes 491524
  17.7 0.9 %copy-start.13 = (bf16[32,2560]{1,0:T(8,128)(2,1)S(1)}, bf16[32,2560]{1,0:T(8,128)(2,1)}, u32[]{:S(2)}) copy-start(bf16[32,2560]{1,0:T(8,128)(2,1)} %copy-done.12) | copy-start | bytes 491524
  18.6 0.9 %copy-start.15 = (bf16[32,2560]{1,0:T(8,128)(2,1)S(1)}, bf16[32,2560]{1,0:T(8,128)(2,1)}, u32[]{:S(2)}) copy-start(bf16[32,2560]{1,0:T(8,128)(2,1)} %copy-done.14) | copy-start | bytes 491524
  20.5 11.8 %collective-permute-start.4 = (f32[160,512]{1,0:T(8,128)S(1)}, f32[160,512]{1,0:T(8,128)}, u32[]{:S(2)}, u32[]{:S(2)}) collective-permute-start(f32[160,512]{1,0:T(8,128)S(1)} %project.3), channel_id=1, source_target_pairs={{0,1},{1,0},{2,3},{3,2},{4,5},{5,4},{6,7},{7,6},{8,9},{9,8},{10,11... | collective-permute-start | bytes 983048 | tf_op jit(solution)/shard_map/ppermute | solution.py:211
  20.6 6.6 %collective-permute-start.6 = (bf16[32,2560]{1,0:T(8,128)(2,1)S(1)}, bf16[32,2560]{1,0:T(8,128)(2,1)S(1)}, u32[]{:S(2)}, u32[]{:S(2)}) collective-permute-start(bf16[32,2560]{1,0:T(8,128)(2,1)S(1)} %copy-done.9), channel_id=1, source_target_pairs={{0,8},{8,16},{16,24},{24,28},{28,20},{20,12},{12,4},{4,0},{1,9},{9... | collective-permute-start | bytes 491528 | tf_op jit(solution)/shard_map/ppermute | solution.py:228
  22.2 6.3 %collective-permute-start.7 = (bf16[32,2560]{1,0:T(8,128)(2,1)S(1)}, bf16[32,2560]{1,0:T(8,128)(2,1)S(1)}, u32[]{:S(2)}, u32[]{:S(2)}) collective-permute-start(bf16[32,2560]{1,0:T(8,128)(2,1)S(1)} %copy-done.11), channel_id=1, source_target_pairs={{8,0},{16,8},{24,16},{28,24},{20,28},{12,20},{4,12},{0,4},{9,1},{1... | collective-permute-start | bytes 491528 | tf_op jit(solution)/shard_map/ppermute | solution.py:229
  29.4 11.1 %copy-start.16 = (bf16[256,256]{1,0:T(8,128)(2,1)S(1)}, bf16[256,256]{1,0:T(8,128)(2,1)}, u32[]{:S(2)}) copy-start(bf16[256,256]{1,0:T(8,128)(2,1)} %refs_7_.1) | copy-start | bytes 393220
  29.4 7.9 %collective-permute-start.8 = (f32[64,512]{1,0:T(8,128)S(1)}, f32[64,512]{1,0:T(8,128)}, u32[]{:S(2)}, u32[]{:S(2)}) collective-permute-start(f32[64,512]{1,0:T(8,128)S(1)} %project.4), channel_id=1, source_target_pairs={{0,1},{1,0},{2,3},{3,2},{4,5},{5,4},{6,7},{7,6},{8,9},{9,8},{10,11... | collective-permute-start | bytes 393224 | tf_op jit(solution)/shard_map/ppermute | solution.py:211
  30.2 4.9 %collective-permute-start.10 = (bf16[16,2560]{1,0:T(8,128)(2,1)S(1)}, bf16[16,2560]{1,0:T(8,128)(2,1)S(1)}, u32[]{:S(2)}, u32[]{:S(2)}) collective-permute-start(bf16[16,2560]{1,0:T(8,128)(2,1)S(1)} %slice.10), channel_id=1, source_target_pairs={{0,8},{8,16},{16,24},{24,28},{28,20},{20,12},{12,4},{4,0},{1,9},{9... | collective-permute-start | bytes 245768 | tf_op jit(solution)/shard_map/ppermute | solution.py:231
  31.8 4.6 %collective-permute-start.11 = (bf16[16,2560]{1,0:T(8,128)(2,1)S(1)}, bf16[16,2560]{1,0:T(8,128)(2,1)S(1)}, u32[]{:S(2)}, u32[]{:S(2)}) collective-permute-start(bf16[16,2560]{1,0:T(8,128)(2,1)S(1)} %slice.11), channel_id=1, source_target_pairs={{8,0},{16,8},{24,16},{28,24},{20,28},{12,20},{4,12},{0,4},{9,1},{1... | collective-permute-start | bytes 245768 | tf_op jit(solution)/shard_map/ppermute | solution.py:232
  33.3 14.5 %copy-start.5 = (f32[160,512]{1,0:T(8,128)}, f32[160,512]{1,0:T(8,128)S(1)}, u32[]{:S(2)}) copy-start(f32[160,512]{1,0:T(8,128)S(1)} %add.49.refs_0_) | copy-start | bytes 983044
  33.3 14.5 %collective-permute-start.5 = (f32[160,512]{1,0:T(8,128)S(1)}, f32[160,512]{1,0:T(8,128)}, u32[]{:S(2)}, u32[]{:S(2)}) collective-permute-start(f32[160,512]{1,0:T(8,128)S(1)} %add.49.refs_0_), channel_id=1, source_target_pairs={{0,2},{1,3},{2,0},{3,1},{4,6},{5,7},{6,4},{7,5},{8,10},{9,11},{10,... | collective-permute-start | bytes 983048 | tf_op jit(solution)/shard_map/ppermute | solution.py:212
  37.3 4.0 %collective-permute-start.12 = (f32[32,512]{1,0:T(8,128)S(1)}, f32[32,512]{1,0:T(8,128)S(1)}, u32[]{:S(2)}, u32[]{:S(2)}) collective-permute-start(f32[32,512]{1,0:T(8,128)S(1)} %project.5), channel_id=1, source_target_pairs={{0,1},{1,0},{2,3},{3,2},{4,5},{5,4},{6,7},{7,6},{8,9},{9,8},{10,11... | collective-permute-start | bytes 196616 | tf_op jit(solution)/shard_map/ppermute | solution.py:211
  38.2 8.9 %collective-permute-start.9 = (f32[64,512]{1,0:T(8,128)S(1)}, f32[64,512]{1,0:T(8,128)S(1)}, u32[]{:S(2)}, u32[]{:S(2)}) collective-permute-start(f32[64,512]{1,0:T(8,128)S(1)} %add.50.refs_2_), channel_id=1, source_target_pairs={{0,2},{1,3},{2,0},{3,1},{4,6},{5,7},{6,4},{7,5},{8,10},{9,11},{10,... | collective-permute-start | bytes 393224 | tf_op jit(solution)/shard_map/ppermute | solution.py:212
  41.3 5.9 %collective-permute-start.13 = (f32[32,512]{1,0:T(8,128)S(1)}, f32[32,512]{1,0:T(8,128)S(1)}, u32[]{:S(2)}, u32[]{:S(2)}) collective-permute-start(f32[32,512]{1,0:T(8,128)S(1)} %add.51.refs_4_), channel_id=1, source_target_pairs={{0,2},{1,3},{2,0},{3,1},{4,6},{5,7},{6,4},{7,5},{8,10},{9,11},{10,... | collective-permute-start | bytes 196616 | tf_op jit(solution)/shard_map/ppermute | solution.py:212
  47.2 0.6 copy-start.20
  47.8 1.0 %copy-start.6 = (f32[160,512]{1,0:T(8,128)S(1)}, f32[160,512]{1,0:T(8,128)}, u32[]{:S(2)}) copy-start(f32[160,512]{1,0:T(8,128)} %copy-done.5) | copy-start | bytes 983044
  48.8 0.9 %copy-start.17 = (bf16[256,256]{1,0:T(8,128)(2,1)S(1)}, bf16[256,256]{1,0:T(8,128)(2,1)}, u32[]{:S(2)}) copy-start(bf16[256,256]{1,0:T(8,128)(2,1)} %refs_7_.1) | copy-start | bytes 393220
  49.7 0.9 %copy-start.18 = (bf16[256,256]{0,1:T(8,128)(2,1)S(1)}, bf16[256,256]{0,1:T(8,128)(2,1)}, u32[]{:S(2)}) copy-start(bf16[256,256]{0,1:T(8,128)(2,1)} %copy.13) | copy-start | bytes 393220
  50.6 0.9 %copy-start.21 = (f32[64,512]{1,0:T(8,128)S(1)}, f32[64,512]{1,0:T(8,128)}, u32[]{:S(2)}) copy-start(f32[64,512]{1,0:T(8,128)} %copy-done.20) | copy-start | bytes 393220
  51.5 0.7 copy-start.22
  57.9 0.8 copy-start.1
  60.5 0.7 copy-start.3
  61.2 7.7 %collective-permute-start.14 = (bf16[32,2560]{1,0:T(8,128)(2,1)}, bf16[32,2560]{1,0:T(8,128)(2,1)}, u32[]{:S(2)}, u32[]{:S(2)}) collective-permute-start(bf16[32,2560]{1,0:T(8,128)(2,1)} %get-tuple-element.17), channel_id=1, source_target_pairs={{0,4},{4,0},{8,12},{12,8},{16,20},{20,16},{24,28},{28,24},{1,5},{5... | collective-permute-start | bytes 491528 | tf_op jit(solution)/shard_map/ppermute | solution.py:245
  62.9 6.0 %copy-start.4 = (f32[32,2560]{1,0:T(8,128)S(1)}, f32[32,2560]{1,0:T(8,128)}, u32[]{:S(2)}) copy-start(f32[32,2560]{1,0:T(8,128)} %copy-done.3) | copy-start | bytes 983044
  62.9 10.1 %collective-permute-start.16 = (bf16[32,2560]{1,0:T(8,128)(2,1)S(1)}, bf16[32,2560]{1,0:T(8,128)(2,1)S(1)}, u32[]{:S(2)}, u32[]{:S(2)}) collective-permute-start(bf16[32,2560]{1,0:T(8,128)(2,1)S(1)} %get-tuple-element.19), channel_id=1, source_target_pairs={{0,4},{4,0},{8,12},{12,8},{16,20},{20,16},{24,28},{28,24},{1,5},{5... | collective-permute-start | bytes 491528 | tf_op jit(solution)/shard_map/ppermute | solution.py:245
  65.7 11.6 %copy-start.2 = (f32[512,256]{1,0:T(8,128)S(1)}, f32[512,256]{1,0:T(8,128)}, u32[]{:S(2)}) copy-start(f32[512,256]{1,0:T(8,128)} %copy-done.1) | copy-start | bytes 1572868
  65.7 9.9 %collective-permute-start.18 = (bf16[32,2560]{1,0:T(8,128)(2,1)S(1)}, bf16[32,2560]{1,0:T(8,128)(2,1)S(1)}, u32[]{:S(2)}, u32[]{:S(2)}) collective-permute-start(bf16[32,2560]{1,0:T(8,128)(2,1)S(1)} %get-tuple-element.21), channel_id=1, source_target_pairs={{0,4},{4,0},{8,12},{12,8},{16,20},{20,16},{24,28},{28,24},{1,5},{5... | collective-permute-start | bytes 491528 | tf_op jit(solution)/shard_map/ppermute | solution.py:245
  67.3 18.3 %collective-permute-start.20 = (f32[32,2560]{1,0:T(8,128)S(1)}, f32[32,2560]{1,0:T(8,128)S(1)}, u32[]{:S(2)}, u32[]{:S(2)}) collective-permute-start(f32[32,2560]{1,0:T(8,128)S(1)} %get-tuple-element.23), channel_id=1, source_target_pairs={{0,4},{4,0},{8,12},{12,8},{16,20},{20,16},{24,28},{28,24},{1,5},{5... | collective-permute-start | bytes 983048 | tf_op jit(solution)/shard_map/ppermute | solution.py:245
  69.9 8.9 %collective-permute-start.15 = (bf16[32,2560]{1,0:T(8,128)(2,1)S(1)}, bf16[32,2560]{1,0:T(8,128)(2,1)S(1)}, u32[]{:S(2)}, u32[]{:S(2)}) collective-permute-start(bf16[32,2560]{1,0:T(8,128)(2,1)S(1)} %add_convert_fusion.2), channel_id=1, source_target_pairs={{0,24},{4,28},{8,16},{12,20},{16,8},{20,12},{24,0},{28,4},{1,25},{... | collective-permute-start | bytes 491528 | tf_op jit(solution)/shard_map/ppermute | solution.py:248
  73.0 12.6 %collective-permute-start.17 = (bf16[32,2560]{1,0:T(8,128)(2,1)S(1)}, bf16[32,2560]{1,0:T(8,128)(2,1)S(1)}, u32[]{:S(2)}, u32[]{:S(2)}) collective-permute-start(bf16[32,2560]{1,0:T(8,128)(2,1)S(1)} %add_convert_fusion.1), channel_id=1, source_target_pairs={{0,16},{4,20},{8,24},{12,28},{16,0},{20,4},{24,8},{28,12},{1,17},{... | collective-permute-start | bytes 491528 | tf_op jit(solution)/shard_map/ppermute | solution.py:248
  75.6 10.0 %collective-permute-start.19 = (bf16[32,2560]{1,0:T(8,128)(2,1)S(1)}, bf16[32,2560]{1,0:T(8,128)(2,1)S(1)}, u32[]{:S(2)}, u32[]{:S(2)}) collective-permute-start(bf16[32,2560]{1,0:T(8,128)(2,1)S(1)} %add_convert_fusion), channel_id=1, source_target_pairs={{0,8},{4,12},{8,0},{12,4},{16,24},{20,28},{24,16},{28,20},{1,9},{5... | collective-permute-start | bytes 491528 | tf_op jit(solution)/shard_map/ppermute | solution.py:248

commit v2 on v1

v2 whole, which is shorter than its diff:
```python
import functools

import jax
import jax.numpy as jnp
from jax import lax
from jax.experimental import pallas as pl
from jax.experimental.pallas import tpu as pltpu
from jax.sharding import PartitionSpec as P

NS_STEPS = 8
SLOT = 64
CYCLE = (0, 2, 4, 6, 7, 5, 3, 1)
AHEAD = [(CYCLE[i], CYCLE[(i + 1) % 8]) for i in range(8)]
BACK = [(d, s) for s, d in AHEAD]
NT = (((1,), (1,)), ((), ()))
NN = (((1,), (0,)), ((), ()))


def dot(a, b, dims=NN):
    return lax.dot_general(a, b, dims, preferred_element_type=jnp.float32)


def split2(a):
    hi = a.astype(jnp.bfloat16)
    return hi, (a - hi.astype(jnp.float32)).astype(jnp.bfloat16)


def split3(a):
    hi = a.astype(jnp.bfloat16)
    rest = a - hi.astype(jnp.float32)
    mid = rest.astype(jnp.bfloat16)
    return hi, mid, (rest - mid.astype(jnp.float32)).astype(jnp.bfloat16)


def dot3(a, b, dims=NN):
    ah, al = a
    bh, bl = b
    return dot(ah, bh, dims) + (dot(ah, bl, dims) + dot(al, bh, dims))


def params(mib):
    return pltpu.CompilerParams(vmem_limit_bytes=mib * 1024 * 1024)


def spot(order):
    me = lax.axis_index("subj")
    place = jnp.where(me % 2 == 0, me // 2, 7 - me // 2)
    at = (place + (order + 8)) % 8
    return jnp.where(at < 4, 2 * at, 15 - 2 * at)


def rows_of(index, block):
    return pl.ds(pl.multiple_of(index * block, block), block)


def mask_body(counts_ref, gate_ref, visits_ref, masked_ref):
    k = pl.program_id(0)
    nvis, ncode = visits_ref.shape[1:]
    rows = lax.broadcasted_iota(jnp.int32, (nvis, 1), 0)
    live = (rows < counts_ref[k]).astype(jnp.bfloat16)
    vals = visits_ref[0] * (gate_ref[0] * live)
    masked_ref[...] = jnp.concatenate(
        [vals, jnp.zeros((SLOT - nvis, ncode), jnp.bfloat16)], 0
    )


def mask_visits(visits, tile_pattern, counts):
    npat, nvis, ncode = visits.shape
    gate = jnp.repeat(tile_pattern.astype(jnp.bfloat16), ncode // tile_pattern.shape[1], axis=1)
    return pl.pallas_call(
        mask_body,
        grid=(npat,),
        in_specs=[
            pl.BlockSpec(memory_space=pltpu.SMEM),
            pl.BlockSpec((1, 1, ncode), lambda k: (k, 0, 0)),
            pl.BlockSpec((1, nvis, ncode), lambda k: (k, 0, 0)),
        ],
        out_specs=pl.BlockSpec((SLOT, ncode), lambda k: (k, 0)),
        out_shape=jax.ShapeDtypeStruct((npat * SLOT, ncode), jnp.bfloat16),
        compiler_params=params(4),
        cost_estimate=pl.CostEstimate(flops=0, bytes_accessed=6_000_000, transcendentals=0),
        name="mask_visits",
    )(counts, gate.reshape(npat, 1, ncode), visits)


def project_body(n, split, *refs):
    masked_ref, outs = refs[n], refs[n + 1 :]
    codes = jnp.concatenate([r[...] for r in refs[:n]], 0) if n > 1 else refs[0][...]
    both = dot(codes, masked_ref[...], NT)
    if not split:
        outs[0][...] = both
        return
    mine_ref, theirs_ref, whole = outs
    half = mine_ref.shape[0]
    whole[...] = both
    core = lax.axis_index("feat") % 2
    mine_ref[...] = whole[rows_of(core, half), :]
    theirs_ref[...] = whole[rows_of(1 - core, half), :]


def project(blocks, masked, split=False):
    rows = sum(b.shape[0] for b in blocks)
    cols = masked.shape[0]
    whole = jax.ShapeDtypeStruct((rows, cols), jnp.float32)
    part = jax.ShapeDtypeStruct((rows // 2, cols), jnp.float32)
    return pl.pallas_call(
        functools.partial(project_body, len(blocks), split),
        out_shape=(part, part) if split else whole,
        scratch_shapes=[pltpu.VMEM((rows, cols), jnp.float32)] if split else [],
        compiler_params=params(10),
        cost_estimate=pl.CostEstimate(
            flops=2 * rows * masked.size, bytes_accessed=2 * masked.size, transcendentals=0
        ),
        name="project",
    )(*blocks, masked)


def place_rows(projt, parts, block, plan):
    core = lax.axis_index("feat") % 2
    at = 0
    for blocks, split in plan:
        left, right = parts[at], parts[at + 1]
        at += 2
        if not split:
            for b, order in enumerate(blocks):
                rows = slice(b * block, (b + 1) * block)
                projt[rows_of(spot(order), block), :] = left[rows, :] + right[rows, :]
            continue
        half = block // 2
        count = len(blocks)
        bases = [spot(o) * 2 + h for o in blocks for h in (0, 1)]
        for u in range(count):
            rows = slice(u * half, (u + 1) * half)
            low, high = bases[u], bases[count + u]
            projt[rows_of(jnp.where(core == 0, low, high), half), :] = left[rows, :]
            projt[rows_of(jnp.where(core == 0, high, low), half), :] = right[rows, :]


def procrustes_body(block, plan, *refs):
    n = 2 * len(plan) if plan else 1
    parts, (weights_ref, core_ref, coret_ref, wt_ref, rot_ref, proj_ref, projt) = (
        refs[:n],
        refs[n:],
    )
    npat, rank = weights_ref.shape
    if plan:
        place_rows(projt, parts, block, plan)
    else:
        projt[...] = parts[0][...]
    proj = projt[...].T
    proj_ref[...] = proj
    core, coret = core_ref[...], coret_ref[...]
    weights = weights_ref[...]
    wide = jnp.broadcast_to(weights[:, None, :], (npat, SLOT, rank)).reshape(npat * SLOT, rank)
    hi, mid, lo = split3(proj * wide)
    target = dot(hi, coret) + (dot(mid, coret) + dot(lo, coret))
    pair = 2 * SLOT
    row = lax.broadcasted_iota(jnp.int32, (pair, pair), 0) // SLOT
    col = lax.broadcasted_iota(jnp.int32, (pair, pair), 1) // SLOT
    same = row == col
    qs = []
    for p in range(npat // 2):
        two = target[p * pair : (p + 1) * pair].reshape(2, SLOT, rank)
        total = jnp.sum(jnp.sum(two * two, axis=1, keepdims=True), axis=2, keepdims=True)
        qs.append((two * lax.rsqrt(total + 1e-06)).reshape(pair, rank))
    for step in range(NS_STEPS):
        halves = [split2(q) for q in qs]
        grams = [jnp.where(same, dot3(h, h, NT), 0.0) for h in halves]
        prods = [dot3(split2(g), h) for g, h in zip(grams, halves)]
        qs = [1.5 * q - 0.5 * x for q, x in zip(qs, prods)]
    q = jnp.concatenate(qs, 0)
    hi, mid, lo = split3(q)
    rotated = dot(hi, core) + (dot(mid, core) + dot(lo, core))
    rot_ref[...] = rotated
    wt_ref[...] = (rotated * wide).T.astype(jnp.bfloat16)


def procrustes(parts, plan, weights, core, block):
    npat, rank = weights.shape
    rows = npat * SLOT
    return pl.pallas_call(
        functools.partial(procrustes_body, block, plan),
        out_shape=[
            jax.ShapeDtypeStruct((rank, rows), jnp.bfloat16),
            jax.ShapeDtypeStruct((rows, rank), jnp.float32),
            jax.ShapeDtypeStruct((rows, rank), jnp.float32),
        ],
        scratch_shapes=[pltpu.VMEM((rank, rows), jnp.float32)],
        compiler_params=params(16),
        cost_estimate=pl.CostEstimate(
            flops=6 * 40 * rows * rank * 128, bytes_accessed=4_000_000, transcendentals=0
        ),
        name="procrustes",
    )(*parts, weights, core, core.T)


def rows_body(rot_ref, proj_ref, out_ref):
    npat, rank = out_ref.shape
    prod = rot_ref[...] * proj_ref[...]
    out_ref[...] = jnp.sum(prod.reshape(npat, SLOT, rank), axis=1)


def patient_rows(rot, proj, npat):
    return pl.pallas_call(
        rows_body,
        out_shape=jax.ShapeDtypeStruct((npat, rot.shape[1]), jnp.float32),
        compiler_params=params(4),
        name="patient_rows",
    )(rot, proj)


def term_body(block, picks, wt_ref, masked_ref, *out_refs):
    me = lax.axis_index("subj")
    flips = [f for pick in picks for f in pick]
    wt = jnp.concatenate([wt_ref[rows_of(me ^ f, block), :] for f in flips], 0)
    both = dot(wt, masked_ref[...])
    at = 0
    for out_ref in out_refs:
        rows = out_ref.shape[0]
        out_ref[...] = both[at : at + rows].astype(out_ref.dtype)
        at += rows


def term(wt, masked, block, picks, kind):
    ncode = masked.shape[1]
    rows = [len(pick) * block for pick in picks]
    return pl.pallas_call(
        functools.partial(term_body, block, picks),
        out_shape=[jax.ShapeDtypeStruct((r, ncode), kind) for r in rows],
        compiler_params=params(10),
        cost_estimate=pl.CostEstimate(
            flops=2 * sum(rows) * masked.size, bytes_accessed=2 * masked.size, transcendentals=0
        ),
        name="term",
    )(wt, masked)


def whole_term_body(wt_ref, masked_ref, out_ref):
    out_ref[...] = dot(wt_ref[...], masked_ref[...])


def whole_term(wt, masked):
    return pl.pallas_call(
        whole_term_body,
        out_shape=jax.ShapeDtypeStruct((wt.shape[0], masked.shape[1]), jnp.float32),
        compiler_params=params(16),
        name="whole_term",
    )(wt, masked)


def flip(axis, size, bit):
    return functools.partial(
        lax.ppermute, axis_name=axis, perm=[(s, s ^ bit) for s in range(size)]
    )


def feat_sum(blocks, masked):
    part = project(blocks, masked)
    part = part + flip("feat", 4, 1)(part)
    return part, flip("feat", 4, 2)(part)


def feat_sum_halves(blocks, masked):
    mine, theirs = project(blocks, masked, split=True)
    mine = mine + flip("feat", 4, 1)(theirs)
    mine = mine + flip("feat", 4, 2)(mine)
    return mine, flip("feat", 4, 1)(mine)


def per_device(visits, tile_pattern, counts, codes_t, core, patient_weights):
    npat = visits.shape[0]
    block = codes_t.shape[0]
    masked = mask_visits(visits, tile_pattern, counts)

    f, b = [codes_t], [codes_t]
    for _ in range(3):
        f.append(lax.ppermute(f[-1], "subj", AHEAD))
        b.append(lax.ppermute(b[-1], "subj", BACK))
    half = block // 2
    f4 = lax.ppermute(f[3][:half], "subj", AHEAD)
    b4 = lax.ppermute(b[3][half:], "subj", BACK)

    plan = (((0, -1, 1, -2, 2), True), ((-3, 3), True), ((4,), False))
    parts = [
        *feat_sum_halves([codes_t, f[1], b[1], f[2], b[2]], masked),
        *feat_sum_halves([f[3], b[3]], masked),
        *feat_sum([f4, b4], masked),
    ]
    wt, rot, proj = procrustes(parts, plan, patient_weights, core, block)

    y, z1, z2, z3 = (flip("subj", 8, bit) for bit in (1, 2, 4, 6))
    there3, there2, near = term(wt, masked, block, ((7,), (5,), (3, 2)), jnp.bfloat16)
    here3, here2, there0, here0 = term(
        wt, masked, block, ((6,), (4,), (1,), (0,)), jnp.float32
    )
    far3 = z3((here3 + y(there3).astype(jnp.float32)).astype(jnp.bfloat16))
    far2 = z2((here2 + y(there2).astype(jnp.float32)).astype(jnp.bfloat16))
    near = z1(near).astype(jnp.float32)
    other = y(there0 + near[:block])
    out = (here0 + near[block:]) + other + (far3.astype(jnp.float32) + far2.astype(jnp.float32))
    rows = patient_rows(rot, proj, npat)
    return out, rows


def per_device_any(visits, tile_pattern, counts, codes_t, core, patient_weights):
    npat = visits.shape[0]
    masked = mask_visits(visits, tile_pattern, counts)
    codes = lax.all_gather(codes_t, "subj", axis=0, tiled=True)
    part = lax.psum(project([codes], masked), "feat")
    wt, rot, proj = procrustes([part], None, patient_weights, core, part.shape[0])
    out = lax.psum_scatter(
        whole_term(wt, masked), "subj", scatter_dimension=0, tiled=True
    )
    return out, patient_rows(rot, proj, npat)


def solution(mesh):
    plan = per_device if (mesh.shape["subj"], mesh.shape["feat"]) == (8, 4) else per_device_any
    return jax.shard_map(
        plan,
        mesh=mesh,
        in_specs=(
            P("subj", None, "feat"),
            P("subj", "feat"),
            P("subj"),
            P("subj", "feat"),
            P(),
            P("subj", None),
        ),
        out_specs=(P("subj", "feat"), P("subj", None)),
        check_vma=False,
    )
```

time: 86.9 us -> 66.3 us (0.76)
  local copies, waits for them, and re-layouts: 15.5 us -> 2.67 us
  Pallas kernels: 15.3 us -> 10.4 us
  other arithmetic: 6.17 us -> 1.71 us
  starting transfers between devices: 23.8 us -> 26.3 us
    unnamed x51 -> x11, local copies, waits for them, and re-layouts: 14.6 us -> 2.41 us
    pallas_call x8 -> x6, Pallas kernels: 13.5 us -> 8.57 us  [the longest x1 4.77 us: procrustes(): pl.pallas_call(functools.partial(procrustes_body, block, plan), out_shape...]
    ppermute x15 -> x20, starting transfers between devices: 19.9 us -> 24.8 us  [the longest x3 6.49 us: per_device(): f.append(lax.ppermute(f[-1], 'subj', AHEAD))]
    ppermute x3 -> x1, waiting for transfers between devices: 5.21 us -> 2.87 us  [feat_sum(): return (part, flip('feat', 4, 2)(part))]
    ppermute x3 -> x1, starting transfers between devices: 3.71 us -> 1.55 us  [feat_sum(): return (part, flip('feat', 4, 2)(part))]
    add x3 -> x1, other arithmetic: 1.95 us -> 0.01 us  [feat_sum(): part = part + flip('feat', 4, 1)(part)]
    ppermute x15 -> x20, waiting for transfers between devices: 19.4 us -> 21.3 us  [the longest x3 6.5 us: per_device(): f.append(lax.ppermute(f[-1], 'subj', AHEAD))]
    another operation x5 -> x0, other arithmetic: 1.02 us -> none  [the longest x1 0.72 us: per_device(): place = jnp.argmax(cycle == me).astype(jnp.int32)]
  transfers between devices with their start and end apart: 21 -> 22, of which waited for: 10 -> 11; matrix products, arithmetic and copies ran while one was open for 8% -> 2% of each run, Pallas kernels for 8% -> 6%
where the time goes in v2:
time: 66.3 us; the launch traced here: 66.1 us
  starting transfers between devices  26.3 us (40%)
  waiting for transfers between devices  24.1 us (36%)
  Pallas kernels  10.4 us (16%)
  local copies, waits for them, and re-layouts  2.67 us (4%)
  other arithmetic  1.71 us (3%)
  between operations  0.87 us (1%)
    ppermute x3, waiting for transfers between devices, per_device(): f.append(lax.ppermute(f[-1], 'subj', AHEAD))  6.5 us
    ppermute x3, starting transfers between devices, per_device(): f.append(lax.ppermute(f[-1], 'subj', AHEAD))  6.49 us
    ppermute x2, starting transfers between devices, per_device(): far2 = z2((here2 + y(there2).astype(jnp.float32)).astype(jnp.bfloat16))  5.68 us
    ppermute x2, waiting for transfers between devices, per_device(): far2 = z2((here2 + y(there2).astype(jnp.float32)).astype(jnp.bfloat16))  5.47 us
    pallas_call x1, Pallas kernels, procrustes(): pl.pallas_call(functools.partial(procrustes_body, block, plan), out_shape...  4.77 us
    ppermute x2, waiting for transfers between devices, per_device(): far3 = z3((here3 + y(there3).astype(jnp.float32)).astype(jnp.bfloat16))  4.7 us
    ppermute x2, starting transfers between devices, per_device(): far3 = z3((here3 + y(there3).astype(jnp.float32)).astype(jnp.bfloat16))  3.97 us
    ppermute x2, starting transfers between devices, feat_sum_halves(): mine = mine + flip('feat', 4, 2)(mine)  3.11 us
  transfers between devices with their start and end apart: 22, of which 11 were waited for; matrix products, arithmetic and copies ran while one was open for 2% of the time, Pallas kernels for 6%

profile of v2, /device:TPU:0, one launch (start us, length us, event | category | flops | bytes accessed | tf_op | source)
XLA Modules:
  0.0 66.1 jit_solution(17785777067341472763)
XLA Ops:
  0.6 0.0 copy-start.1
  0.6 3.1 %collective-permute-start = (bf16[32,2560]{1,0:T(8,128)(2,1)}, bf16[32,2560]{1,0:T(8,128)(2,1)S(1)}, u32[]{:S(2)}, u32[]{:S(2)}) collective-permute-start(bf16[32,2560]{1,0:T(8,128)(2,1)} %refs_0_.1), channel_id=1, source_target_pairs={{0,8},{8,16},{16,24},{24,28},{28,20},{20,12},{12,4},{4,0},{1,9},{9... | collective-permute-start | bytes 491528 | tf_op jit(solution)/shard_map/ppermute | solution.py:277
  3.7 0.0 collective-permute-start.1
  3.7 0.7 %convert_element_type.24 = bf16[8,20]{1,0:T(8,128)(2,1)S(1)} convert(s32[8,20]{1,0:T(8,128)} %param.7) | non-fusion elementwise | flops 160 | bytes 960 | tf_op jit(solution)/shard_map/convert_element_type | solution.py:69
  4.4 0.1 copy.9
  4.5 3.6 %collective-permute-done.refs_1_ = bf16[32,2560]{1,0:T(8,128)(2,1)S(1)} collective-permute-done((bf16[32,2560]{1,0:T(8,128)(2,1)}, bf16[32,2560]{1,0:T(8,128)(2,1)S(1)}, u32[]{:S(2)}, u32[]{:S(2)}) %collective-permute-start) | collective-permute-done | bytes 163872 | tf_op jit(solution)/shard_map/ppermute | solution.py:277
  8.1 1.8 %collective-permute-start.2 = (bf16[32,2560]{1,0:T(8,128)(2,1)S(1)}, bf16[32,2560]{1,0:T(8,128)(2,1)S(1)}, u32[]{:S(2)}, u32[]{:S(2)}) collective-permute-start(bf16[32,2560]{1,0:T(8,128)(2,1)S(1)} %collective-permute-done.refs_1_), channel_id=1, source_target_pairs={{0,8},{8,16},{16,24},{24,28},{28,20},{20,12},{12,4},{4,0},{1,9},{9... | collective-permute-start | bytes 491528 | tf_op jit(solution)/shard_map/ppermute | solution.py:277
  9.9 0.0 collective-permute-done.1.refs_2_
  9.9 0.2 collective-permute-start.3
  10.1 0.1 broadcast_bitcast_fusion
  10.2 0.1 copy.10.gate_ref
  10.3 0.0 copy-start
  10.3 1.6 %copy-done = bf16[8,56,2560]{2,1,0:T(8,128)(2,1)S(1)} copy-done((bf16[8,56,2560]{2,1,0:T(8,128)(2,1)S(1)}, bf16[8,56,2560]{2,1,0:T(8,128)(2,1)}, u32[]{:S(2)}) %copy-start) | copy-done | bytes 2293784
  11.9 0.7 copy-done.3
  12.6 1.1 %mask_visits.1.refs_5_.refs_2_.masked_ref = bf16[512,2560]{1,0:T(8,128)(2,1)S(1)} custom-call(s32[8]{0:T(128)S(1)} %copy-done.3, bf16[8,1,2560]{2,1,0:T(2,128)(2,1)S(1)} %copy.10.gate_ref, bf16[8,56,2560]{2,1,0:T(8,128)(2,1)S(1)} %copy-done), custom_call_target="tpu_custom_call" | custom-call | bytes 6000000 | tf_op jit(solution)/shard_map/mask_visits/pallas_call | solution.py:70
  13.7 0.0 collective-permute-done.2.refs_3_
  13.7 1.5 %collective-permute-done.3.refs_4_ = bf16[32,2560]{1,0:T(8,128)(2,1)S(1)} collective-permute-done((bf16[32,2560]{1,0:T(8,128)(2,1)S(1)}, bf16[32,2560]{1,0:T(8,128)(2,1)S(1)}, u32[]{:S(2)}, u32[]{:S(2)}) %collective-permute-start.3) | collective-permute-done | bytes 163872 | tf_op jit(solution)/shard_map/ppermute | solution.py:278
  15.2 1.0 %project.3 = (f32[80,512]{1,0:T(8,128)S(1)}, f32[80,512]{1,0:T(8,128)S(1)}) custom-call(bf16[32,2560]{1,0:T(8,128)(2,1)S(1)} %copy-done.1, bf16[32,2560]{1,0:T(8,128)(2,1)S(1)} %collective-permute-done.refs_1_, bf16[32,2560]{1,0:T(8,128)(2,1)S(1)} %collective-permute-done.1.refs_2_, bf16[32,2560]{1,0:T(8,128)(2,1)S(1)} %collective-permute-done.2.refs_3_, ...), custom_call_target="tpu_custom_call" | custom-call | flops 419430400 | bytes 2621440 | tf_op jit(solution)/shard_map/project/pallas_call | solution.py:106
  16.2 0.1 collective-permute-start.4
  16.3 1.6 %collective-permute-start.7 = (bf16[32,2560]{1,0:T(8,128)(2,1)S(1)}, bf16[32,2560]{1,0:T(8,128)(2,1)S(1)}, u32[]{:S(2)}, u32[]{:S(2)}) collective-permute-start(bf16[32,2560]{1,0:T(8,128)(2,1)S(1)} %collective-permute-done.2.refs_3_), channel_id=1, source_target_pairs={{0,8},{8,16},{16,24},{24,28},{28,20},{20,12},{12,4},{4,0},{1,9},{9... | collective-permute-start | bytes 491528 | tf_op jit(solution)/shard_map/ppermute | solution.py:277
  17.9 0.4 collective-permute-start.8
  18.4 0.0 collective-permute-done.4
  18.4 1.6 %collective-permute-start.5 = (f32[80,512]{1,0:T(8,128)S(1)}, f32[80,512]{1,0:T(8,128)S(1)}, u32[]{:S(2)}, u32[]{:S(2)}) collective-permute-start(f32[80,512]{1,0:T(8,128)S(1)} %add.36), channel_id=1, source_target_pairs={{0,2},{1,3},{2,0},{3,1},{4,6},{5,7},{6,4},{7,5},{8,10},{9,11},{10,... | collective-permute-start | bytes 491528 | tf_op jit(solution)/shard_map/ppermute | solution.py:266
  20.0 2.9 %collective-permute-done.7.refs_0_ = bf16[32,2560]{1,0:T(8,128)(2,1)S(1)} collective-permute-done((bf16[32,2560]{1,0:T(8,128)(2,1)S(1)}, bf16[32,2560]{1,0:T(8,128)(2,1)S(1)}, u32[]{:S(2)}, u32[]{:S(2)}) %collective-permute-start.7) | collective-permute-done | bytes 163872 | tf_op jit(solution)/shard_map/ppermute | solution.py:277
  22.9 1.6 %collective-permute-start.12 = (bf16[16,2560]{1,0:T(8,128)(2,1)S(1)}, bf16[16,2560]{1,0:T(8,128)(2,1)S(1)}, u32[]{:S(2)}, u32[]{:S(2)}) collective-permute-start(bf16[16,2560]{1,0:T(8,128)(2,1)S(1)} %slice.16), channel_id=1, source_target_pairs={{0,8},{8,16},{16,24},{24,28},{28,20},{20,12},{12,4},{4,0},{1,9},{9... | collective-permute-start | bytes 245768 | tf_op jit(solution)/shard_map/ppermute | solution.py:280
  24.5 0.0 collective-permute-done.8.refs_1_
  24.5 0.5 collective-permute-start.13
  25.0 0.9 %project.4 = (f32[32,512]{1,0:T(8,128)S(1)}, f32[32,512]{1,0:T(8,128)S(1)}) custom-call(bf16[32,2560]{1,0:T(8,128)(2,1)S(1)} %collective-permute-done.7.refs_0_, bf16[32,2560]{1,0:T(8,128)(2,1)S(1)} %collective-permute-done.8.refs_1_, bf16[512,2560]{1,0:T(8,128)(2,1)S(1)} %mask_visits.1.refs_5_.refs_2_.masked_ref), custom_call_target="tpu_custom_call" | custom-call | flops 167772160 | bytes 2621440 | tf_op jit(solution)/shard_map/project/pallas_call | solution.py:106
  25.9 0.0 copy-start.2
  25.9 0.0 copy-start.4
  26.0 0.1 collective-permute-start.9
  26.0 0.0 collective-permute-done.5
  26.1 0.5 collective-permute-start.6
  26.6 0.6 collective-permute-done.9
  27.3 1.6 %collective-permute-start.10 = (f32[32,512]{1,0:T(8,128)S(1)}, f32[32,512]{1,0:T(8,128)S(1)}, u32[]{:S(2)}, u32[]{:S(2)}) collective-permute-start(f32[32,512]{1,0:T(8,128)S(1)} %add.38), channel_id=1, source_target_pairs={{0,2},{1,3},{2,0},{3,1},{4,6},{5,7},{6,4},{7,5},{8,10},{9,11},{10,... | collective-permute-start | bytes 196616 | tf_op jit(solution)/shard_map/ppermute | solution.py:266
  28.8 0.0 collective-permute-done.12.refs_0_
  28.9 0.1 collective-permute-done.13.refs_1_
  29.0 0.8 %project.5 = f32[32,512]{1,0:T(8,128)S(1)} custom-call(bf16[16,2560]{1,0:T(8,128)(2,1)S(1)} %collective-permute-done.12.refs_0_, bf16[16,2560]{1,0:T(8,128)(2,1)S(1)} %collective-permute-done.13.refs_1_, bf16[512,2560]{1,0:T(8,128)(2,1)S(1)} %mask_visits.1.refs_5_.refs_2_.masked_ref), custom_call_target="tpu_custom_call" | custom-call | flops 83886080 | bytes 2621440 | tf_op jit(solution)/shard_map/project/pallas_call | solution.py:106
  29.8 0.0 collective-permute-start.14
  29.9 1.8 %collective-permute-done.10 = f32[32,512]{1,0:T(8,128)S(1)} collective-permute-done((f32[32,512]{1,0:T(8,128)S(1)}, f32[32,512]{1,0:T(8,128)S(1)}, u32[]{:S(2)}, u32[]{:S(2)}) %collective-permute-start.10) | collective-permute-done | bytes 65568 | tf_op jit(solution)/shard_map/ppermute | solution.py:266
  31.6 0.1 collective-permute-start.11
  31.7 0.0 collective-permute-done.14
  31.7 1.6 %collective-permute-start.15 = (f32[32,512]{1,0:T(8,128)S(1)}, f32[32,512]{1,0:T(8,128)S(1)}, u32[]{:S(2)}, u32[]{:S(2)}) collective-permute-start(f32[32,512]{1,0:T(8,128)S(1)} %add.40.refs_4_), channel_id=1, source_target_pairs={{0,2},{1,3},{2,0},{3,1},{4,6},{5,7},{6,4},{7,5},{8,10},{9,11},{10,... | collective-permute-start | bytes 196616 | tf_op jit(solution)/shard_map/ppermute | solution.py:260
  33.3 0.1 copy.11
  33.4 0.0 collective-permute-done.11.refs_3_
  33.4 2.9 %collective-permute-done.15.refs_5_ = f32[32,512]{1,0:T(8,128)S(1)} collective-permute-done((f32[32,512]{1,0:T(8,128)S(1)}, f32[32,512]{1,0:T(8,128)S(1)}, u32[]{:S(2)}, u32[]{:S(2)}) %collective-permute-start.15) | collective-permute-done | bytes 65568 | tf_op jit(solution)/shard_map/ppermute | solution.py:260
  36.3 0.0 collective-permute-done.6.refs_1_
  36.3 4.8 %procrustes.1 = (bf16[256,512]{1,0:T(8,128)(2,1)S(1)}, f32[512,256]{1,0:T(8,128)S(1)}, f32[512,256]{1,0:T(8,128)S(1)}) custom-call(f32[80,512]{1,0:T(8,128)S(1)} %add.37.refs_0_, f32[80,512]{1,0:T(8,128)S(1)} %collective-permute-done.6.refs_1_, f32[32,512]{1,0:T(8,128)S(1)} %add.39.refs_2_, f32[32,512]{1,0:T(8,128)S(1)} %collective-permute-done.11.refs_3_, ...), custom_call_target="tpu_custom_call" | custom-call | flops 4026531840 | bytes 4000000 | tf_op jit(solution)/shard_map/procrustes/pallas_call | solution.py:181
  41.1 0.5 term.3
  41.6 0.4 collective-permute-start.18
  42.0 1.7 %collective-permute-start.20 = (bf16[32,2560]{1,0:T(8,128)(2,1)S(1)}, bf16[32,2560]{1,0:T(8,128)(2,1)S(1)}, u32[]{:S(2)}, u32[]{:S(2)}) collective-permute-start(bf16[32,2560]{1,0:T(8,128)(2,1)S(1)} %get-tuple-element.27), channel_id=1, source_target_pairs={{0,4},{4,0},{8,12},{12,8},{16,20},{20,16},{24,28},{28,24},{1,5},{5... | collective-permute-start | bytes 491528 | tf_op jit(solution)/shard_map/ppermute | solution.py:297
  43.7 1.6 %collective-permute-start.16 = (bf16[64,2560]{1,0:T(8,128)(2,1)S(1)}, bf16[64,2560]{1,0:T(8,128)(2,1)S(1)}, u32[]{:S(2)}, u32[]{:S(2)}) collective-permute-start(bf16[64,2560]{1,0:T(8,128)(2,1)S(1)} %get-tuple-element.22), channel_id=1, source_target_pairs={{0,8},{4,12},{8,0},{12,4},{16,24},{20,28},{24,16},{28,20},{1,9},{5... | collective-permute-start | bytes 983048 | tf_op jit(solution)/shard_map/ppermute | solution.py:298
  45.3 0.5 term.2
  45.8 3.0 %collective-permute-done.18 = bf16[32,2560]{1,0:T(8,128)(2,1)S(1)} collective-permute-done((bf16[32,2560]{1,0:T(8,128)(2,1)S(1)}, bf16[32,2560]{1,0:T(8,128)(2,1)S(1)}, u32[]{:S(2)}, u32[]{:S(2)}) %collective-permute-start.18) | collective-permute-done | bytes 163872 | tf_op jit(solution)/shard_map/ppermute | solution.py:296
  48.8 3.6 %collective-permute-start.19 = (bf16[32,2560]{1,0:T(8,128)(2,1)S(1)}, bf16[32,2560]{1,0:T(8,128)(2,1)S(1)}, u32[]{:S(2)}, u32[]{:S(2)}) collective-permute-start(bf16[32,2560]{1,0:T(8,128)(2,1)S(1)} %add_convert_fusion.1), channel_id=1, source_target_pairs={{0,24},{4,28},{8,16},{12,20},{16,8},{20,12},{24,0},{28,4},{1,25},{... | collective-permute-start | bytes 491528 | tf_op jit(solution)/shard_map/ppermute | solution.py:296
  52.4 0.6 collective-permute-done.16
  53.1 0.4 collective-permute-start.17
  53.5 0.0 collective-permute-done.20
  53.5 4.0 %collective-permute-start.21 = (bf16[32,2560]{1,0:T(8,128)(2,1)S(1)}, bf16[32,2560]{1,0:T(8,128)(2,1)S(1)}, u32[]{:S(2)}, u32[]{:S(2)}) collective-permute-start(bf16[32,2560]{1,0:T(8,128)(2,1)S(1)} %add_convert_fusion), channel_id=1, source_target_pairs={{0,16},{4,20},{8,24},{12,28},{16,0},{20,4},{24,8},{28,12},{1,17},{... | collective-permute-start | bytes 491528 | tf_op jit(solution)/shard_map/ppermute | solution.py:297
  57.4 0.7 %patient_rows.1 = f32[8,256]{1,0:T(8,128)} custom-call(f32[512,256]{1,0:T(8,128)S(1)} %get-tuple-element.28.rot_ref, f32[512,256]{1,0:T(8,128)S(1)} %get-tuple-element.29.proj_ref), custom_call_target="tpu_custom_call" | custom-call | tf_op jit(solution)/shard_map/patient_rows/pallas_call | solution.py:204
  58.1 1.7 %collective-permute-done.19 = bf16[32,2560]{1,0:T(8,128)(2,1)S(1)} collective-permute-done((bf16[32,2560]{1,0:T(8,128)(2,1)S(1)}, bf16[32,2560]{1,0:T(8,128)(2,1)S(1)}, u32[]{:S(2)}, u32[]{:S(2)}) %collective-permute-start.19) | collective-permute-done | bytes 163872 | tf_op jit(solution)/shard_map/ppermute | solution.py:296
  59.8 5.5 %collective-permute-done.21 = bf16[32,2560]{1,0:T(8,128)(2,1)S(1)} collective-permute-done((bf16[32,2560]{1,0:T(8,128)(2,1)S(1)}, bf16[32,2560]{1,0:T(8,128)(2,1)S(1)}, u32[]{:S(2)}, u32[]{:S(2)}) %collective-permute-start.21) | collective-permute-done | bytes 163872 | tf_op jit(solution)/shard_map/ppermute | solution.py:297
  65.3 0.0 collective-permute-done.17
  65.3 0.8 %fusion.1 = f32[32,2560]{1,0:T(8,128)} fusion(f32[32,2560]{1,0:T(8,128)S(1)} %collective-permute-done.17, f32[32,2560]{1,0:T(8,128)S(1)} %get-tuple-element.21, f32[64,2560]{1,0:T(8,128)S(1)} %convert_element_type.25, bf16[32,2560]{1,0:T(8,128)(2,1)S(1)} %collective-permute-done.21, bf16[32,2560]{1,0:T(8,128)(2,1)S(1)} %collective-permute-done.19), kind=kLoop, calls=%fused_computation.3 | loop fusion | flops 491520 | bytes 1638400 | tf_op jit(solution)/shard_map/add | solution.py:300
  (15 shorter events, 0.3 us)
Async XLA Ops:
  0.6 14.6 %copy-start.1 = (bf16[32,2560]{1,0:T(8,128)(2,1)S(1)}, bf16[32,2560]{1,0:T(8,128)(2,1)}, u32[]{:S(2)}) copy-start(bf16[32,2560]{1,0:T(8,128)(2,1)} %refs_0_.1) | copy-start | bytes 491524
  0.6 7.4 %collective-permute-start = (bf16[32,2560]{1,0:T(8,128)(2,1)}, bf16[32,2560]{1,0:T(8,128)(2,1)S(1)}, u32[]{:S(2)}, u32[]{:S(2)}) collective-permute-start(bf16[32,2560]{1,0:T(8,128)(2,1)} %refs_0_.1), channel_id=1, source_target_pairs={{0,8},{8,16},{16,24},{24,28},{28,20},{20,12},{12,4},{4,0},{1,9},{9... | collective-permute-start | bytes 491528 | tf_op jit(solution)/shard_map/ppermute | solution.py:277
  3.7 6.2 %collective-permute-start.1 = (bf16[32,2560]{1,0:T(8,128)(2,1)}, bf16[32,2560]{1,0:T(8,128)(2,1)S(1)}, u32[]{:S(2)}, u32[]{:S(2)}) collective-permute-start(bf16[32,2560]{1,0:T(8,128)(2,1)} %refs_0_.1), channel_id=1, source_target_pairs={{8,0},{16,8},{24,16},{28,24},{20,28},{12,20},{4,12},{0,4},{9,1},{1... | collective-permute-start | bytes 491528 | tf_op jit(solution)/shard_map/ppermute | solution.py:278
  8.1 5.6 %collective-permute-start.2 = (bf16[32,2560]{1,0:T(8,128)(2,1)S(1)}, bf16[32,2560]{1,0:T(8,128)(2,1)S(1)}, u32[]{:S(2)}, u32[]{:S(2)}) collective-permute-start(bf16[32,2560]{1,0:T(8,128)(2,1)S(1)} %collective-permute-done.refs_1_), channel_id=1, source_target_pairs={{0,8},{8,16},{16,24},{24,28},{28,20},{20,12},{12,4},{4,0},{1,9},{9... | collective-permute-start | bytes 491528 | tf_op jit(solution)/shard_map/ppermute | solution.py:277
  9.9 5.3 %collective-permute-start.3 = (bf16[32,2560]{1,0:T(8,128)(2,1)S(1)}, bf16[32,2560]{1,0:T(8,128)(2,1)S(1)}, u32[]{:S(2)}, u32[]{:S(2)}) collective-permute-start(bf16[32,2560]{1,0:T(8,128)(2,1)S(1)} %collective-permute-done.1.refs_2_), channel_id=1, source_target_pairs={{8,0},{16,8},{24,16},{28,24},{20,28},{12,20},{4,12},{0,4},{9,1},{1... | collective-permute-start | bytes 491528 | tf_op jit(solution)/shard_map/ppermute | solution.py:278
  10.3 1.6 %copy-start = (bf16[8,56,2560]{2,1,0:T(8,128)(2,1)S(1)}, bf16[8,56,2560]{2,1,0:T(8,128)(2,1)}, u32[]{:S(2)}) copy-start(bf16[8,56,2560]{2,1,0:T(8,128)(2,1)} %visits_ref.1) | copy-start | bytes 6881284
  11.9 0.7 copy-start.3
  16.2 2.2 %collective-permute-start.4 = (f32[80,512]{1,0:T(8,128)S(1)}, f32[80,512]{1,0:T(8,128)S(1)}, u32[]{:S(2)}, u32[]{:S(2)}) collective-permute-start(f32[80,512]{1,0:T(8,128)S(1)} %get-tuple-element.17), channel_id=1, source_target_pairs={{0,1},{1,0},{2,3},{3,2},{4,5},{5,4},{6,7},{7,6},{8,9},{9,8},{10,11... | collective-permute-start | bytes 491528 | tf_op jit(solution)/shard_map/ppermute | solution.py:265
  16.3 6.6 %collective-permute-start.7 = (bf16[32,2560]{1,0:T(8,128)(2,1)S(1)}, bf16[32,2560]{1,0:T(8,128)(2,1)S(1)}, u32[]{:S(2)}, u32[]{:S(2)}) collective-permute-start(bf16[32,2560]{1,0:T(8,128)(2,1)S(1)} %collective-permute-done.2.refs_3_), channel_id=1, source_target_pairs={{0,8},{8,16},{16,24},{24,28},{28,20},{20,12},{12,4},{4,0},{1,9},{9... | collective-permute-start | bytes 491528 | tf_op jit(solution)/shard_map/ppermute | solution.py:277
  17.9 6.6 %collective-permute-start.8 = (bf16[32,2560]{1,0:T(8,128)(2,1)S(1)}, bf16[32,2560]{1,0:T(8,128)(2,1)S(1)}, u32[]{:S(2)}, u32[]{:S(2)}) collective-permute-start(bf16[32,2560]{1,0:T(8,128)(2,1)S(1)} %collective-permute-done.3.refs_4_), channel_id=1, source_target_pairs={{8,0},{16,8},{24,16},{28,24},{20,28},{12,20},{4,12},{0,4},{9,1},{1... | collective-permute-start | bytes 491528 | tf_op jit(solution)/shard_map/ppermute | solution.py:278
  18.4 7.6 %collective-permute-start.5 = (f32[80,512]{1,0:T(8,128)S(1)}, f32[80,512]{1,0:T(8,128)S(1)}, u32[]{:S(2)}, u32[]{:S(2)}) collective-permute-start(f32[80,512]{1,0:T(8,128)S(1)} %add.36), channel_id=1, source_target_pairs={{0,2},{1,3},{2,0},{3,1},{4,6},{5,7},{6,4},{7,5},{8,10},{9,11},{10,... | collective-permute-start | bytes 491528 | tf_op jit(solution)/shard_map/ppermute | solution.py:266
  22.9 5.9 %collective-permute-start.12 = (bf16[16,2560]{1,0:T(8,128)(2,1)S(1)}, bf16[16,2560]{1,0:T(8,128)(2,1)S(1)}, u32[]{:S(2)}, u32[]{:S(2)}) collective-permute-start(bf16[16,2560]{1,0:T(8,128)(2,1)S(1)} %slice.16), channel_id=1, source_target_pairs={{0,8},{8,16},{16,24},{24,28},{28,20},{20,12},{12,4},{4,0},{1,9},{9... | collective-permute-start | bytes 245768 | tf_op jit(solution)/shard_map/ppermute | solution.py:280
  24.5 4.5 %collective-permute-start.13 = (bf16[16,2560]{1,0:T(8,128)(2,1)S(1)}, bf16[16,2560]{1,0:T(8,128)(2,1)S(1)}, u32[]{:S(2)}, u32[]{:S(2)}) collective-permute-start(bf16[16,2560]{1,0:T(8,128)(2,1)S(1)} %slice.17), channel_id=1, source_target_pairs={{8,0},{16,8},{24,16},{28,24},{20,28},{12,20},{4,12},{0,4},{9,1},{1... | collective-permute-start | bytes 245768 | tf_op jit(solution)/shard_map/ppermute | solution.py:281
  25.9 7.4 %copy-start.2 = (bf16[256,256]{1,0:T(8,128)(2,1)S(1)}, bf16[256,256]{1,0:T(8,128)(2,1)}, u32[]{:S(2)}) copy-start(bf16[256,256]{1,0:T(8,128)(2,1)} %refs_7_.1) | copy-start | bytes 393220
  25.9 10.4 %copy-start.4 = (f32[8,256]{1,0:T(8,128)S(1)}, f32[8,256]{1,0:T(8,128)}, u32[]{:S(2)}) copy-start(f32[8,256]{1,0:T(8,128)} %refs_6_.1) | copy-start | bytes 24580
  26.0 1.3 %collective-permute-start.9 = (f32[32,512]{1,0:T(8,128)S(1)}, f32[32,512]{1,0:T(8,128)S(1)}, u32[]{:S(2)}, u32[]{:S(2)}) collective-permute-start(f32[32,512]{1,0:T(8,128)S(1)} %get-tuple-element.19), channel_id=1, source_target_pairs={{0,1},{1,0},{2,3},{3,2},{4,5},{5,4},{6,7},{7,6},{8,9},{9,8},{10,11... | collective-permute-start | bytes 196616 | tf_op jit(solution)/shard_map/ppermute | solution.py:265
  26.1 10.2 %collective-permute-start.6 = (f32[80,512]{1,0:T(8,128)S(1)}, f32[80,512]{1,0:T(8,128)S(1)}, u32[]{:S(2)}, u32[]{:S(2)}) collective-permute-start(f32[80,512]{1,0:T(8,128)S(1)} %add.37.refs_0_), channel_id=1, source_target_pairs={{0,1},{1,0},{2,3},{3,2},{4,5},{5,4},{6,7},{7,6},{8,9},{9,8},{10,11... | collective-permute-start | bytes 491528 | tf_op jit(solution)/shard_map/ppermute | solution.py:267
  27.3 4.3 %collective-permute-start.10 = (f32[32,512]{1,0:T(8,128)S(1)}, f32[32,512]{1,0:T(8,128)S(1)}, u32[]{:S(2)}, u32[]{:S(2)}) collective-permute-start(f32[32,512]{1,0:T(8,128)S(1)} %add.38), channel_id=1, source_target_pairs={{0,2},{1,3},{2,0},{3,1},{4,6},{5,7},{6,4},{7,5},{8,10},{9,11},{10,... | collective-permute-start | bytes 196616 | tf_op jit(solution)/shard_map/ppermute | solution.py:266
  29.8 1.9 %collective-permute-start.14 = (f32[32,512]{1,0:T(8,128)S(1)}, f32[32,512]{1,0:T(8,128)S(1)}, u32[]{:S(2)}, u32[]{:S(2)}) collective-permute-start(f32[32,512]{1,0:T(8,128)S(1)} %project.5), channel_id=1, source_target_pairs={{0,1},{1,0},{2,3},{3,2},{4,5},{5,4},{6,7},{7,6},{8,9},{9,8},{10,11... | collective-permute-start | bytes 196616 | tf_op jit(solution)/shard_map/ppermute | solution.py:259
  31.6 1.8 %collective-permute-start.11 = (f32[32,512]{1,0:T(8,128)S(1)}, f32[32,512]{1,0:T(8,128)S(1)}, u32[]{:S(2)}, u32[]{:S(2)}) collective-permute-start(f32[32,512]{1,0:T(8,128)S(1)} %add.39.refs_2_), channel_id=1, source_target_pairs={{0,1},{1,0},{2,3},{3,2},{4,5},{5,4},{6,7},{7,6},{8,9},{9,8},{10,11... | collective-permute-start | bytes 196616 | tf_op jit(solution)/shard_map/ppermute | solution.py:267
  31.7 4.5 %collective-permute-start.15 = (f32[32,512]{1,0:T(8,128)S(1)}, f32[32,512]{1,0:T(8,128)S(1)}, u32[]{:S(2)}, u32[]{:S(2)}) collective-permute-start(f32[32,512]{1,0:T(8,128)S(1)} %add.40.refs_4_), channel_id=1, source_target_pairs={{0,2},{1,3},{2,0},{3,1},{4,6},{5,7},{6,4},{7,5},{8,10},{9,11},{10,... | collective-permute-start | bytes 196616 | tf_op jit(solution)/shard_map/ppermute | solution.py:260
  41.6 7.2 %collective-permute-start.18 = (bf16[32,2560]{1,0:T(8,128)(2,1)S(1)}, bf16[32,2560]{1,0:T(8,128)(2,1)S(1)}, u32[]{:S(2)}, u32[]{:S(2)}) collective-permute-start(bf16[32,2560]{1,0:T(8,128)(2,1)S(1)} %get-tuple-element.25), channel_id=1, source_target_pairs={{0,4},{4,0},{8,12},{12,8},{16,20},{20,16},{24,28},{28,24},{1,5},{5... | collective-permute-start | bytes 491528 | tf_op jit(solution)/shard_map/ppermute | solution.py:296
  42.0 11.5 %collective-permute-start.20 = (bf16[32,2560]{1,0:T(8,128)(2,1)S(1)}, bf16[32,2560]{1,0:T(8,128)(2,1)S(1)}, u32[]{:S(2)}, u32[]{:S(2)}) collective-permute-start(bf16[32,2560]{1,0:T(8,128)(2,1)S(1)} %get-tuple-element.27), channel_id=1, source_target_pairs={{0,4},{4,0},{8,12},{12,8},{16,20},{20,16},{24,28},{28,24},{1,5},{5... | collective-permute-start | bytes 491528 | tf_op jit(solution)/shard_map/ppermute | solution.py:297
  43.7 9.3 %collective-permute-start.16 = (bf16[64,2560]{1,0:T(8,128)(2,1)S(1)}, bf16[64,2560]{1,0:T(8,128)(2,1)S(1)}, u32[]{:S(2)}, u32[]{:S(2)}) collective-permute-start(bf16[64,2560]{1,0:T(8,128)(2,1)S(1)} %get-tuple-element.22), channel_id=1, source_target_pairs={{0,8},{4,12},{8,0},{12,4},{16,24},{20,28},{24,16},{28,20},{1,9},{5... | collective-permute-start | bytes 983048 | tf_op jit(solution)/shard_map/ppermute | solution.py:298
  48.8 11.0 %collective-permute-start.19 = (bf16[32,2560]{1,0:T(8,128)(2,1)S(1)}, bf16[32,2560]{1,0:T(8,128)(2,1)S(1)}, u32[]{:S(2)}, u32[]{:S(2)}) collective-permute-start(bf16[32,2560]{1,0:T(8,128)(2,1)S(1)} %add_convert_fusion.1), channel_id=1, source_target_pairs={{0,24},{4,28},{8,16},{12,20},{16,8},{20,12},{24,0},{28,4},{1,25},{... | collective-permute-start | bytes 491528 | tf_op jit(solution)/shard_map/ppermute | solution.py:296
  53.1 12.2 %collective-permute-start.17 = (f32[32,2560]{1,0:T(8,128)S(1)}, f32[32,2560]{1,0:T(8,128)S(1)}, u32[]{:S(2)}, u32[]{:S(2)}) collective-permute-start(f32[32,2560]{1,0:T(8,128)S(1)} %slice_add_fusion), channel_id=1, source_target_pairs={{0,4},{4,0},{8,12},{12,8},{16,20},{20,16},{24,28},{28,24},{1,5},{5... | collective-permute-start | bytes 983048 | tf_op jit(solution)/shard_map/ppermute | solution.py:299
  53.5 11.8 %collective-permute-start.21 = (bf16[32,2560]{1,0:T(8,128)(2,1)S(1)}, bf16[32,2560]{1,0:T(8,128)(2,1)S(1)}, u32[]{:S(2)}, u32[]{:S(2)}) collective-permute-start(bf16[32,2560]{1,0:T(8,128)(2,1)S(1)} %add_convert_fusion), channel_id=1, source_target_pairs={{0,16},{4,20},{8,24},{12,28},{16,0},{20,4},{24,8},{28,12},{1,17},{... | collective-permute-start | bytes 491528 | tf_op jit(solution)/shard_map/ppermute | solution.py:297

commit v3 on v2

--- a/solution.py
+++ b/solution.py
@@ -9,6 +9,12 @@
 
 NS_STEPS = 8
 SLOT = 64
+BF16, F32 = jnp.bfloat16, jnp.float32
+
+
+def cost(us):
+    return pl.CostEstimate(flops=0, bytes_accessed=int(us * 3.6e6), transcendentals=0)
+
 CYCLE = (0, 2, 4, 6, 7, 5, 3, 1)
 AHEAD = [(CYCLE[i], CYCLE[(i + 1) % 8]) for i in range(8)]
 BACK = [(d, s) for s, d in AHEAD]
@@ -78,7 +84,7 @@
         out_specs=pl.BlockSpec((SLOT, ncode), lambda k: (k, 0)),
         out_shape=jax.ShapeDtypeStruct((npat * SLOT, ncode), jnp.bfloat16),
         compiler_params=params(4),
-        cost_estimate=pl.CostEstimate(flops=0, bytes_accessed=6_000_000, transcendentals=0),
+        cost_estimate=cost(0),
         name="mask_visits",
     )(counts, gate.reshape(npat, 1, ncode), visits)
 
@@ -108,9 +114,7 @@
         out_shape=(part, part) if split else whole,
         scratch_shapes=[pltpu.VMEM((rows, cols), jnp.float32)] if split else [],
         compiler_params=params(10),
-        cost_estimate=pl.CostEstimate(
-            flops=2 * rows * masked.size, bytes_accessed=2 * masked.size, transcendentals=0
-        ),
+        cost_estimate=cost(0),
         name="project",
     )(*blocks, masked)
 
@@ -187,9 +191,7 @@
         ],
         scratch_shapes=[pltpu.VMEM((rank, rows), jnp.float32)],
         compiler_params=params(16),
-        cost_estimate=pl.CostEstimate(
-            flops=6 * 40 * rows * rank * 128, bytes_accessed=4_000_000, transcendentals=0
-        ),
+        cost_estimate=cost(0),
         name="procrustes",
     )(*parts, weights, core, core.T)
 
@@ -221,16 +223,14 @@
         at += rows
 
 
-def term(wt, masked, block, picks, kind):
+def term(wt, masked, block, picks, kinds):
     ncode = masked.shape[1]
     rows = [len(pick) * block for pick in picks]
     return pl.pallas_call(
         functools.partial(term_body, block, picks),
-        out_shape=[jax.ShapeDtypeStruct((r, ncode), kind) for r in rows],
+        out_shape=[jax.ShapeDtypeStruct((r, ncode), kind) for r, kind in zip(rows, kinds)],
         compiler_params=params(10),
-        cost_estimate=pl.CostEstimate(
-            flops=2 * sum(rows) * masked.size, bytes_accessed=2 * masked.size, transcendentals=0
-        ),
+        cost_estimate=cost(0),
         name="term",
     )(wt, masked)
 
@@ -254,50 +254,47 @@
     )
 
 
-def feat_sum(blocks, masked):
-    part = project(blocks, masked)
-    part = part + flip("feat", 4, 1)(part)
-    return part, flip("feat", 4, 2)(part)
-
-
-def feat_sum_halves(blocks, masked):
-    mine, theirs = project(blocks, masked, split=True)
-    mine = mine + flip("feat", 4, 1)(theirs)
-    mine = mine + flip("feat", 4, 2)(mine)
-    return mine, flip("feat", 4, 1)(mine)
+def tie(first, then):
+    return lax.optimization_barrier((first, then))
 
 
 def per_device(visits, tile_pattern, counts, codes_t, core, patient_weights):
     npat = visits.shape[0]
     block = codes_t.shape[0]
+    half = block // 2
+    to_core, to_x = flip("feat", 4, 1), flip("feat", 4, 2)
+
+    def step(ahead, back):
+        return lax.ppermute(ahead, "subj", AHEAD), lax.ppermute(back, "subj", BACK)
+
     masked = mask_visits(visits, tile_pattern, counts)
-
-    f, b = [codes_t], [codes_t]
-    for _ in range(3):
-        f.append(lax.ppermute(f[-1], "subj", AHEAD))
-        b.append(lax.ppermute(b[-1], "subj", BACK))
-    half = block // 2
-    f4 = lax.ppermute(f[3][:half], "subj", AHEAD)
-    b4 = lax.ppermute(b[3][half:], "subj", BACK)
-
-    plan = (((0, -1, 1, -2, 2), True), ((-3, 3), True), ((4,), False))
-    parts = [
-        *feat_sum_halves([codes_t, f[1], b[1], f[2], b[2]], masked),
-        *feat_sum_halves([f[3], b[3]], masked),
-        *feat_sum([f4, b4], masked),
-    ]
+    one = step(codes_t, codes_t)
+    masked, back = tie(masked, one[1])
+    one = (one[0], back)
+    two = step(*one)
+    proj0 = project([codes_t, *one, *two], masked, split=True)
+    core0 = proj0[0] + to_core(proj0[1])
+    tot0 = core0 + to_x(core0)
+    three = step(*two)
+    four = step(three[0][:half], three[1][half:])
+    proj1 = project([*three, *four], masked, split=True)
+    core1 = proj1[0] + to_core(proj1[1])
+    tot1 = core1 + to_x(core1)
+    parts = [tot0, to_core(tot0), tot1, to_core(tot1)]
+    plan = (((0, -1, 1, -2, 2), True), ((-3, 3, 4), True),)
     wt, rot, proj = procrustes(parts, plan, patient_weights, core, block)
 
     y, z1, z2, z3 = (flip("subj", 8, bit) for bit in (1, 2, 4, 6))
-    there3, there2, near = term(wt, masked, block, ((7,), (5,), (3, 2)), jnp.bfloat16)
-    here3, here2, there0, here0 = term(
-        wt, masked, block, ((6,), (4,), (1,), (0,)), jnp.float32
-    )
-    far3 = z3((here3 + y(there3).astype(jnp.float32)).astype(jnp.bfloat16))
-    far2 = z2((here2 + y(there2).astype(jnp.float32)).astype(jnp.bfloat16))
-    near = z1(near).astype(jnp.float32)
+    there2, there3, near = term(wt, masked, block, ((5,), (7,), (3, 2)), (BF16, BF16, BF16))
+    here2, here3, there0, here0 = term(
+        wt, masked, block, ((4,), (6,), (1,), (0,)), (F32, F32, F32, F32)
+    )
+    got2, there3 = tie(y(there2), there3)
+    far2 = z2((here2 + got2.astype(F32)).astype(BF16))
+    far3 = z3((here3 + y(there3).astype(F32)).astype(BF16))
+    near = z1(near).astype(F32)
     other = y(there0 + near[:block])
-    out = (here0 + near[block:]) + other + (far3.astype(jnp.float32) + far2.astype(jnp.float32))
+    out = (here0 + near[block:]) + other + (far3.astype(F32) + far2.astype(F32))
     rows = patient_rows(rot, proj, npat)
     return out, rows
 

time: 66.3 us -> 62.9 us (0.949)
  starting transfers between devices: 26.3 us -> 21.5 us
  waiting for transfers between devices: 24.1 us -> 26.4 us
  Pallas kernels: 10.4 us -> 9.57 us
    ppermute x21 -> x19, starting transfers between devices: 25.9 us -> 19.8 us  [the longest x4 8.62 us: step(): lax.ppermute(ahead, 'subj', AHEAD)]
    ppermute x21 -> x19, waiting for transfers between devices: 24.1 us -> 26.4 us  [the longest x4 6.37 us: step(): lax.ppermute(ahead, 'subj', AHEAD)]
    ppermute x1, starting transfers between devices: 0.39 us -> 1.68 us  [per_device(): other = y(there0 + near[:block])]
    pallas_call x3 -> x2, Pallas kernels: 2.79 us -> 1.96 us  [project(): pl.pallas_call(functools.partial(project_body, len(blocks), split), out_s...]
  transfers between devices with their start and end apart: 22 -> 20, of which waited for: 11 -> 11; matrix products, arithmetic and copies ran while one was open for 2% -> 2% of each run, Pallas kernels for 6% -> 7%
where the time goes in v3:
time: 62.9 us; the launch traced here: 62.7 us
  waiting for transfers between devices  26.4 us (42%)
  starting transfers between devices  21.5 us (34%)
  Pallas kernels  9.57 us (15%)
  local copies, waits for them, and re-layouts  2.68 us (4%)
  other arithmetic  1.71 us (3%)
  between operations  0.84 us (1%)
    ppermute x4, starting transfers between devices, step(): lax.ppermute(ahead, 'subj', AHEAD)  8.62 us
    ppermute x4, waiting for transfers between devices, step(): lax.ppermute(ahead, 'subj', AHEAD)  6.37 us
    pallas_call x1, Pallas kernels, procrustes(): pl.pallas_call(functools.partial(procrustes_body, block, plan), out_shape...  4.76 us
    ppermute x2, waiting for transfers between devices, per_device(): far3 = z3((here3 + y(there3).astype(F32)).astype(BF16))  4.11 us
    ppermute x1, waiting for transfers between devices, per_device(): near = z1(near).astype(F32)  4.01 us
    ppermute x1, waiting for transfers between devices, per_device(): got2, there3 = tie(y(there2), there3)  3.7 us
    ppermute x1, waiting for transfers between devices, per_device(): tot1 = core1 + to_x(core1)  3.25 us
    ppermute x1, starting transfers between devices, per_device(): far2 = z2((here2 + got2.astype(F32)).astype(BF16))  2.76 us
  transfers between devices with their start and end apart: 20, of which 11 were waited for; matrix products, arithmetic and copies ran while one was open for 2% of the time, Pallas kernels for 7%

profile of v3, /device:TPU:0, one launch (start us, length us, event | category | flops | bytes accessed | tf_op | source)
XLA Modules:
  0.0 62.7 jit_solution(18380109353322633717)
XLA Ops:
  0.6 0.0 copy-start.2
  0.6 3.1 %collective-permute-start = (bf16[32,2560]{1,0:T(8,128)(2,1)}, bf16[32,2560]{1,0:T(8,128)(2,1)S(1)}, u32[]{:S(2)}, u32[]{:S(2)}) collective-permute-start(bf16[32,2560]{1,0:T(8,128)(2,1)} %refs_0_.1), channel_id=1, source_target_pairs={{0,8},{8,16},{16,24},{24,28},{28,20},{20,12},{12,4},{4,0},{1,9},{9... | collective-permute-start | bytes 491528 | tf_op jit(solution)/shard_map/ppermute | solution.py:268
  3.7 0.0 collective-permute-start.1
  3.7 0.7 %convert_element_type.24 = bf16[8,20]{1,0:T(8,128)(2,1)S(1)} convert(s32[8,20]{1,0:T(8,128)} %param.7) | non-fusion elementwise | flops 160 | bytes 960 | tf_op jit(solution)/shard_map/convert_element_type | solution.py:75
  4.4 0.1 copy.9
  4.5 0.1 broadcast_bitcast_fusion
  4.6 0.1 copy.10.gate_ref
  4.7 0.0 copy-start
  4.7 1.6 %copy-done = bf16[8,56,2560]{2,1,0:T(8,128)(2,1)S(1)} copy-done((bf16[8,56,2560]{2,1,0:T(8,128)(2,1)S(1)}, bf16[8,56,2560]{2,1,0:T(8,128)(2,1)}, u32[]{:S(2)}) %copy-start) | copy-done | bytes 2293784
  6.3 0.0 copy-start.4
  6.3 0.7 %copy-done.4 = s32[8]{0:T(128)S(1)} copy-done((s32[8]{0:T(128)S(1)}, s32[8]{0:T(128)}, u32[]{:S(2)}) %copy-start.4) | copy-done | bytes 56
  7.0 1.1 %mask_visits.1.refs_5_.refs_4_.masked_ref = bf16[512,2560]{1,0:T(8,128)(2,1)S(1)} custom-call(s32[8]{0:T(128)S(1)} %copy-done.4, bf16[8,1,2560]{2,1,0:T(2,128)(2,1)S(1)} %copy.10.gate_ref, bf16[8,56,2560]{2,1,0:T(8,128)(2,1)S(1)} %copy-done), custom_call_target="tpu_custom_call" | custom-call | tf_op jit(solution)/shard_map/mask_visits/pallas_call | solution.py:76
  8.1 0.0 collective-permute-done.refs_1_
  8.1 2.1 %collective-permute-start.2 = (bf16[32,2560]{1,0:T(8,128)(2,1)S(1)}, bf16[32,2560]{1,0:T(8,128)(2,1)S(1)}, u32[]{:S(2)}, u32[]{:S(2)}) collective-permute-start(bf16[32,2560]{1,0:T(8,128)(2,1)S(1)} %collective-permute-done.refs_1_), channel_id=1, source_target_pairs={{0,8},{8,16},{16,24},{24,28},{28,20},{20,12},{12,4},{4,0},{1,9},{9... | collective-permute-start | bytes 491528 | tf_op jit(solution)/shard_map/ppermute | solution.py:268
  10.2 0.0 collective-permute-done.1.refs_2_
  10.2 0.0 collective-permute-start.3
  10.2 3.6 %collective-permute-done.2.refs_3_ = bf16[32,2560]{1,0:T(8,128)(2,1)S(1)} collective-permute-done((bf16[32,2560]{1,0:T(8,128)(2,1)S(1)}, bf16[32,2560]{1,0:T(8,128)(2,1)S(1)}, u32[]{:S(2)}, u32[]{:S(2)}) %collective-permute-start.2) | collective-permute-done | bytes 163872 | tf_op jit(solution)/shard_map/ppermute | solution.py:268
  13.9 1.7 %collective-permute-start.7 = (bf16[32,2560]{1,0:T(8,128)(2,1)S(1)}, bf16[32,2560]{1,0:T(8,128)(2,1)S(1)}, u32[]{:S(2)}, u32[]{:S(2)}) collective-permute-start(bf16[32,2560]{1,0:T(8,128)(2,1)S(1)} %collective-permute-done.2.refs_3_), channel_id=1, source_target_pairs={{0,8},{8,16},{16,24},{24,28},{28,20},{20,12},{12,4},{4,0},{1,9},{9... | collective-permute-start | bytes 491528 | tf_op jit(solution)/shard_map/ppermute | solution.py:268
  15.6 0.0 collective-permute-done.3.refs_4_
  15.6 0.3 collective-permute-start.8
  15.9 0.0 copy-done.2
  15.9 1.0 %project.2 = (f32[80,512]{1,0:T(8,128)S(1)}, f32[80,512]{1,0:T(8,128)S(1)}) custom-call(bf16[32,2560]{1,0:T(8,128)(2,1)S(1)} %copy-done.2, bf16[32,2560]{1,0:T(8,128)(2,1)S(1)} %collective-permute-done.refs_1_, bf16[32,2560]{1,0:T(8,128)(2,1)S(1)} %collective-permute-done.1.refs_2_, bf16[32,2560]{1,0:T(8,128)(2,1)S(1)} %collective-permute-done.2.refs_3_, ...), custom_call_target="tpu_custom_call" | custom-call | tf_op jit(solution)/shard_map/project/pallas_call | solution.py:112
  16.9 0.0 copy-start.1
  16.9 0.0 copy-start.3
  16.9 0.1 collective-permute-start.4
  17.0 2.1 %collective-permute-done.7.refs_0_ = bf16[32,2560]{1,0:T(8,128)(2,1)S(1)} collective-permute-done((bf16[32,2560]{1,0:T(8,128)(2,1)S(1)}, bf16[32,2560]{1,0:T(8,128)(2,1)S(1)}, u32[]{:S(2)}, u32[]{:S(2)}) %collective-permute-start.7) | collective-permute-done | bytes 163872 | tf_op jit(solution)/shard_map/ppermute | solution.py:268
  19.2 1.7 %collective-permute-start.9 = (bf16[16,2560]{1,0:T(8,128)(2,1)S(1)}, bf16[16,2560]{1,0:T(8,128)(2,1)S(1)}, u32[]{:S(2)}, u32[]{:S(2)}) collective-permute-start(bf16[16,2560]{1,0:T(8,128)(2,1)S(1)} %slice.16), channel_id=1, source_target_pairs={{0,8},{8,16},{16,24},{24,28},{28,20},{20,12},{12,4},{4,0},{1,9},{9... | collective-permute-start | bytes 245768 | tf_op jit(solution)/shard_map/ppermute | solution.py:268
  20.9 0.0 collective-permute-done.8.refs_1_
  20.9 0.3 collective-permute-start.10
  21.3 0.0 collective-permute-done.4
  21.3 1.7 %collective-permute-start.5 = (f32[80,512]{1,0:T(8,128)S(1)}, f32[80,512]{1,0:T(8,128)S(1)}, u32[]{:S(2)}, u32[]{:S(2)}) collective-permute-start(f32[80,512]{1,0:T(8,128)S(1)} %add.33), channel_id=1, source_target_pairs={{0,2},{1,3},{2,0},{3,1},{4,6},{5,7},{6,4},{7,5},{8,10},{9,11},{10,... | collective-permute-start | bytes 491528 | tf_op jit(solution)/shard_map/ppermute | solution.py:277
  23.0 0.6 collective-permute-done.9.refs_2_
  23.6 1.8 %collective-permute-done.10.refs_3_ = bf16[16,2560]{1,0:T(8,128)(2,1)S(1)} collective-permute-done((bf16[16,2560]{1,0:T(8,128)(2,1)S(1)}, bf16[16,2560]{1,0:T(8,128)(2,1)S(1)}, u32[]{:S(2)}, u32[]{:S(2)}) %collective-permute-start.10) | collective-permute-done | bytes 81952 | tf_op jit(solution)/shard_map/ppermute | solution.py:268
  25.4 0.9 %project.3 = (f32[48,512]{1,0:T(8,128)S(1)}, f32[48,512]{1,0:T(8,128)S(1)}) custom-call(bf16[32,2560]{1,0:T(8,128)(2,1)S(1)} %collective-permute-done.7.refs_0_, bf16[32,2560]{1,0:T(8,128)(2,1)S(1)} %collective-permute-done.8.refs_1_, bf16[16,2560]{1,0:T(8,128)(2,1)S(1)} %collective-permute-done.9.refs_2_, ...), custom_call_target="tpu_custom_call" | custom-call | tf_op jit(solution)/shard_map/project/pallas_call | solution.py:112
  26.4 0.1 collective-permute-start.11
  26.5 1.3 %collective-permute-done.11 = f32[48,512]{1,0:T(8,128)S(1)} collective-permute-done((f32[48,512]{1,0:T(8,128)S(1)}, f32[48,512]{1,0:T(8,128)S(1)}, u32[]{:S(2)}, u32[]{:S(2)}) %collective-permute-start.11) | collective-permute-done | bytes 98336 | tf_op jit(solution)/shard_map/ppermute | solution.py:281
  27.8 1.6 %collective-permute-start.12 = (f32[48,512]{1,0:T(8,128)S(1)}, f32[48,512]{1,0:T(8,128)S(1)}, u32[]{:S(2)}, u32[]{:S(2)}) collective-permute-start(f32[48,512]{1,0:T(8,128)S(1)} %add.35), channel_id=1, source_target_pairs={{0,2},{1,3},{2,0},{3,1},{4,6},{5,7},{6,4},{7,5},{8,10},{9,11},{10,... | collective-permute-start | bytes 294920 | tf_op jit(solution)/shard_map/ppermute | solution.py:282
  29.3 0.0 collective-permute-done.5
  29.3 0.1 collective-permute-start.6
  29.4 3.3 %collective-permute-done.12 = f32[48,512]{1,0:T(8,128)S(1)} collective-permute-done((f32[48,512]{1,0:T(8,128)S(1)}, f32[48,512]{1,0:T(8,128)S(1)}, u32[]{:S(2)}, u32[]{:S(2)}) %collective-permute-start.12) | collective-permute-done | bytes 98336 | tf_op jit(solution)/shard_map/ppermute | solution.py:282
  32.7 0.1 collective-permute-start.13
  32.8 0.0 copy-done.1
  32.8 0.1 copy.11
  32.9 0.0 collective-permute-done.6.refs_1_
  32.9 1.2 %collective-permute-done.13.refs_3_ = f32[48,512]{1,0:T(8,128)S(1)} collective-permute-done((f32[48,512]{1,0:T(8,128)S(1)}, f32[48,512]{1,0:T(8,128)S(1)}, u32[]{:S(2)}, u32[]{:S(2)}) %collective-permute-start.13) | collective-permute-done | bytes 98336 | tf_op jit(solution)/shard_map/ppermute | solution.py:283
  34.1 0.0 copy-done.3
  34.1 4.8 %procrustes.1 = (bf16[256,512]{1,0:T(8,128)(2,1)S(1)}, f32[512,256]{1,0:T(8,128)S(1)}, f32[512,256]{1,0:T(8,128)S(1)}) custom-call(f32[80,512]{1,0:T(8,128)S(1)} %add.34.refs_0_, f32[80,512]{1,0:T(8,128)S(1)} %collective-permute-done.6.refs_1_, f32[48,512]{1,0:T(8,128)S(1)} %add.36.refs_2_, f32[48,512]{1,0:T(8,128)S(1)} %collective-permute-done.13.refs_3_, ...), custom_call_target="tpu_custom_call" | custom-call | tf_op jit(solution)/shard_map/procrustes/pallas_call | solution.py:185
  38.8 0.5 term.3
  39.4 0.4 collective-permute-start.16
  39.7 0.5 term.2
  40.2 1.7 %collective-permute-start.14 = (bf16[64,2560]{1,0:T(8,128)(2,1)S(1)}, bf16[64,2560]{1,0:T(8,128)(2,1)S(1)}, u32[]{:S(2)}, u32[]{:S(2)}) collective-permute-start(bf16[64,2560]{1,0:T(8,128)(2,1)S(1)} %get-tuple-element.28), channel_id=1, source_target_pairs={{0,8},{4,12},{8,0},{12,4},{16,24},{20,28},{24,16},{28,20},{1,9},{5... | collective-permute-start | bytes 983048 | tf_op jit(solution)/shard_map/ppermute | solution.py:295
  42.0 3.7 %collective-permute-done.16 = bf16[32,2560]{1,0:T(8,128)(2,1)S(1)} collective-permute-done((bf16[32,2560]{1,0:T(8,128)(2,1)S(1)}, bf16[32,2560]{1,0:T(8,128)(2,1)S(1)}, u32[]{:S(2)}, u32[]{:S(2)}) %collective-permute-start.16) | collective-permute-done | bytes 163872 | tf_op jit(solution)/shard_map/ppermute | solution.py:292
  45.7 0.3 collective-permute-start.17
  46.0 2.8 %collective-permute-start.19 = (bf16[32,2560]{1,0:T(8,128)(2,1)S(1)}, bf16[32,2560]{1,0:T(8,128)(2,1)S(1)}, u32[]{:S(2)}, u32[]{:S(2)}) collective-permute-start(bf16[32,2560]{1,0:T(8,128)(2,1)S(1)} %add_convert_fusion), channel_id=1, source_target_pairs={{0,16},{4,20},{8,24},{12,28},{16,0},{20,4},{24,8},{28,12},{1,17},{... | collective-permute-start | bytes 491528 | tf_op jit(solution)/shard_map/ppermute | solution.py:293
  48.8 4.0 %collective-permute-done.14 = bf16[64,2560]{1,0:T(8,128)(2,1)S(1)} collective-permute-done((bf16[64,2560]{1,0:T(8,128)(2,1)S(1)}, bf16[64,2560]{1,0:T(8,128)(2,1)S(1)}, u32[]{:S(2)}, u32[]{:S(2)}) %collective-permute-start.14) | collective-permute-done | bytes 327712 | tf_op jit(solution)/shard_map/ppermute | solution.py:295
  52.9 1.7 %collective-permute-start.15 = (f32[32,2560]{1,0:T(8,128)S(1)}, f32[32,2560]{1,0:T(8,128)S(1)}, u32[]{:S(2)}, u32[]{:S(2)}) collective-permute-start(f32[32,2560]{1,0:T(8,128)S(1)} %slice_add_fusion), channel_id=1, source_target_pairs={{0,4},{4,0},{8,12},{12,8},{16,20},{20,16},{24,28},{28,24},{1,5},{5... | collective-permute-start | bytes 983048 | tf_op jit(solution)/shard_map/ppermute | solution.py:296
  54.6 0.0 collective-permute-done.17
  54.6 1.8 %collective-permute-start.18 = (bf16[32,2560]{1,0:T(8,128)(2,1)S(1)}, bf16[32,2560]{1,0:T(8,128)(2,1)S(1)}, u32[]{:S(2)}, u32[]{:S(2)}) collective-permute-start(bf16[32,2560]{1,0:T(8,128)(2,1)S(1)} %add_convert_fusion.1), channel_id=1, source_target_pairs={{0,24},{4,28},{8,16},{12,20},{16,8},{20,12},{24,0},{28,4},{1,25},{... | collective-permute-start | bytes 491528 | tf_op jit(solution)/shard_map/ppermute | solution.py:294
  56.4 0.7 %patient_rows.1 = f32[8,256]{1,0:T(8,128)} custom-call(f32[512,256]{1,0:T(8,128)S(1)} %get-tuple-element.36.rot_ref, f32[512,256]{1,0:T(8,128)S(1)} %get-tuple-element.37.proj_ref), custom_call_target="tpu_custom_call" | custom-call | tf_op jit(solution)/shard_map/patient_rows/pallas_call | solution.py:206
  57.1 0.7 %collective-permute-done.19 = bf16[32,2560]{1,0:T(8,128)(2,1)S(1)} collective-permute-done((bf16[32,2560]{1,0:T(8,128)(2,1)S(1)}, bf16[32,2560]{1,0:T(8,128)(2,1)S(1)}, u32[]{:S(2)}, u32[]{:S(2)}) %collective-permute-start.19) | collective-permute-done | bytes 163872 | tf_op jit(solution)/shard_map/ppermute | solution.py:293
  57.8 4.1 %collective-permute-done.18 = bf16[32,2560]{1,0:T(8,128)(2,1)S(1)} collective-permute-done((bf16[32,2560]{1,0:T(8,128)(2,1)S(1)}, bf16[32,2560]{1,0:T(8,128)(2,1)S(1)}, u32[]{:S(2)}, u32[]{:S(2)}) %collective-permute-start.18) | collective-permute-done | bytes 163872 | tf_op jit(solution)/shard_map/ppermute | solution.py:294
  61.9 0.0 collective-permute-done.15
  61.9 0.8 %fusion.1 = f32[32,2560]{1,0:T(8,128)} fusion(f32[32,2560]{1,0:T(8,128)S(1)} %collective-permute-done.15, f32[32,2560]{1,0:T(8,128)S(1)} %get-tuple-element.27, f32[64,2560]{1,0:T(8,128)S(1)} %convert_element_type.25, bf16[32,2560]{1,0:T(8,128)(2,1)S(1)} %collective-permute-done.19, bf16[32,2560]{1,0:T(8,128)(2,1)S(1)} %collective-permute-done.18), kind=kLoop, calls=%fused_computation.3 | loop fusion | flops 491520 | bytes 1638400 | tf_op jit(solution)/shard_map/add | solution.py:297
  (10 shorter events, 0.2 us)
Async XLA Ops:
  0.6 15.3 %copy-start.2 = (bf16[32,2560]{1,0:T(8,128)(2,1)S(1)}, bf16[32,2560]{1,0:T(8,128)(2,1)}, u32[]{:S(2)}) copy-start(bf16[32,2560]{1,0:T(8,128)(2,1)} %refs_0_.1) | copy-start | bytes 491524
  0.6 7.5 %collective-permute-start = (bf16[32,2560]{1,0:T(8,128)(2,1)}, bf16[32,2560]{1,0:T(8,128)(2,1)S(1)}, u32[]{:S(2)}, u32[]{:S(2)}) collective-permute-start(bf16[32,2560]{1,0:T(8,128)(2,1)} %refs_0_.1), channel_id=1, source_target_pairs={{0,8},{8,16},{16,24},{24,28},{28,20},{20,12},{12,4},{4,0},{1,9},{9... | collective-permute-start | bytes 491528 | tf_op jit(solution)/shard_map/ppermute | solution.py:268
  3.7 6.5 %collective-permute-start.1 = (bf16[32,2560]{1,0:T(8,128)(2,1)}, bf16[32,2560]{1,0:T(8,128)(2,1)S(1)}, u32[]{:S(2)}, u32[]{:S(2)}) collective-permute-start(bf16[32,2560]{1,0:T(8,128)(2,1)} %refs_0_.1), channel_id=1, source_target_pairs={{8,0},{16,8},{24,16},{28,24},{20,28},{12,20},{4,12},{0,4},{9,1},{1... | collective-permute-start | bytes 491528 | tf_op jit(solution)/shard_map/ppermute | solution.py:268
  4.7 1.6 %copy-start = (bf16[8,56,2560]{2,1,0:T(8,128)(2,1)S(1)}, bf16[8,56,2560]{2,1,0:T(8,128)(2,1)}, u32[]{:S(2)}) copy-start(bf16[8,56,2560]{2,1,0:T(8,128)(2,1)} %visits_ref.1) | copy-start | bytes 6881284
  6.3 0.7 %copy-start.4 = (s32[8]{0:T(128)S(1)}, s32[8]{0:T(128)}, u32[]{:S(2)}) copy-start(s32[8]{0:T(128)} %counts_ref.1) | copy-start | bytes 100
  8.1 5.7 %collective-permute-start.2 = (bf16[32,2560]{1,0:T(8,128)(2,1)S(1)}, bf16[32,2560]{1,0:T(8,128)(2,1)S(1)}, u32[]{:S(2)}, u32[]{:S(2)}) collective-permute-start(bf16[32,2560]{1,0:T(8,128)(2,1)S(1)} %collective-permute-done.refs_1_), channel_id=1, source_target_pairs={{0,8},{8,16},{16,24},{24,28},{28,20},{20,12},{12,4},{4,0},{1,9},{9... | collective-permute-start | bytes 491528 | tf_op jit(solution)/shard_map/ppermute | solution.py:268
  10.2 5.4 %collective-permute-start.3 = (bf16[32,2560]{1,0:T(8,128)(2,1)S(1)}, bf16[32,2560]{1,0:T(8,128)(2,1)S(1)}, u32[]{:S(2)}, u32[]{:S(2)}) collective-permute-start(bf16[32,2560]{1,0:T(8,128)(2,1)S(1)} %collective-permute-done.1.refs_2_), channel_id=1, source_target_pairs={{8,0},{16,8},{24,16},{28,24},{20,28},{12,20},{4,12},{0,4},{9,1},{1... | collective-permute-start | bytes 491528 | tf_op jit(solution)/shard_map/ppermute | solution.py:268
  13.9 5.3 %collective-permute-start.7 = (bf16[32,2560]{1,0:T(8,128)(2,1)S(1)}, bf16[32,2560]{1,0:T(8,128)(2,1)S(1)}, u32[]{:S(2)}, u32[]{:S(2)}) collective-permute-start(bf16[32,2560]{1,0:T(8,128)(2,1)S(1)} %collective-permute-done.2.refs_3_), channel_id=1, source_target_pairs={{0,8},{8,16},{16,24},{24,28},{28,20},{20,12},{12,4},{4,0},{1,9},{9... | collective-permute-start | bytes 491528 | tf_op jit(solution)/shard_map/ppermute | solution.py:268
  15.6 5.3 %collective-permute-start.8 = (bf16[32,2560]{1,0:T(8,128)(2,1)S(1)}, bf16[32,2560]{1,0:T(8,128)(2,1)S(1)}, u32[]{:S(2)}, u32[]{:S(2)}) collective-permute-start(bf16[32,2560]{1,0:T(8,128)(2,1)S(1)} %collective-permute-done.3.refs_4_), channel_id=1, source_target_pairs={{8,0},{16,8},{24,16},{28,24},{20,28},{12,20},{4,12},{0,4},{9,1},{1... | collective-permute-start | bytes 491528 | tf_op jit(solution)/shard_map/ppermute | solution.py:268
  16.9 15.9 %copy-start.1 = (bf16[256,256]{1,0:T(8,128)(2,1)S(1)}, bf16[256,256]{1,0:T(8,128)(2,1)}, u32[]{:S(2)}) copy-start(bf16[256,256]{1,0:T(8,128)(2,1)} %refs_5_.1) | copy-start | bytes 393220
  16.9 17.1 %copy-start.3 = (f32[8,256]{1,0:T(8,128)S(1)}, f32[8,256]{1,0:T(8,128)}, u32[]{:S(2)}) copy-start(f32[8,256]{1,0:T(8,128)} %refs_4_.1) | copy-start | bytes 24580
  16.9 4.3 %collective-permute-start.4 = (f32[80,512]{1,0:T(8,128)S(1)}, f32[80,512]{1,0:T(8,128)S(1)}, u32[]{:S(2)}, u32[]{:S(2)}) collective-permute-start(f32[80,512]{1,0:T(8,128)S(1)} %get-tuple-element.23), channel_id=1, source_target_pairs={{0,1},{1,0},{2,3},{3,2},{4,5},{5,4},{6,7},{7,6},{8,9},{9,8},{10,11... | collective-permute-start | bytes 491528 | tf_op jit(solution)/shard_map/ppermute | solution.py:276
  19.2 4.4 %collective-permute-start.9 = (bf16[16,2560]{1,0:T(8,128)(2,1)S(1)}, bf16[16,2560]{1,0:T(8,128)(2,1)S(1)}, u32[]{:S(2)}, u32[]{:S(2)}) collective-permute-start(bf16[16,2560]{1,0:T(8,128)(2,1)S(1)} %slice.16), channel_id=1, source_target_pairs={{0,8},{8,16},{16,24},{24,28},{28,20},{20,12},{12,4},{4,0},{1,9},{9... | collective-permute-start | bytes 245768 | tf_op jit(solution)/shard_map/ppermute | solution.py:268
  20.9 4.5 %collective-permute-start.10 = (bf16[16,2560]{1,0:T(8,128)(2,1)S(1)}, bf16[16,2560]{1,0:T(8,128)(2,1)S(1)}, u32[]{:S(2)}, u32[]{:S(2)}) collective-permute-start(bf16[16,2560]{1,0:T(8,128)(2,1)S(1)} %slice.17), channel_id=1, source_target_pairs={{8,0},{16,8},{24,16},{28,24},{20,28},{12,20},{4,12},{0,4},{9,1},{1... | collective-permute-start | bytes 245768 | tf_op jit(solution)/shard_map/ppermute | solution.py:268
  21.3 8.0 %collective-permute-start.5 = (f32[80,512]{1,0:T(8,128)S(1)}, f32[80,512]{1,0:T(8,128)S(1)}, u32[]{:S(2)}, u32[]{:S(2)}) collective-permute-start(f32[80,512]{1,0:T(8,128)S(1)} %add.33), channel_id=1, source_target_pairs={{0,2},{1,3},{2,0},{3,1},{4,6},{5,7},{6,4},{7,5},{8,10},{9,11},{10,... | collective-permute-start | bytes 491528 | tf_op jit(solution)/shard_map/ppermute | solution.py:277
  26.4 1.4 %collective-permute-start.11 = (f32[48,512]{1,0:T(8,128)S(1)}, f32[48,512]{1,0:T(8,128)S(1)}, u32[]{:S(2)}, u32[]{:S(2)}) collective-permute-start(f32[48,512]{1,0:T(8,128)S(1)} %get-tuple-element.25), channel_id=1, source_target_pairs={{0,1},{1,0},{2,3},{3,2},{4,5},{5,4},{6,7},{7,6},{8,9},{9,8},{10,11... | collective-permute-start | bytes 294920 | tf_op jit(solution)/shard_map/ppermute | solution.py:281
  27.8 4.9 %collective-permute-start.12 = (f32[48,512]{1,0:T(8,128)S(1)}, f32[48,512]{1,0:T(8,128)S(1)}, u32[]{:S(2)}, u32[]{:S(2)}) collective-permute-start(f32[48,512]{1,0:T(8,128)S(1)} %add.35), channel_id=1, source_target_pairs={{0,2},{1,3},{2,0},{3,1},{4,6},{5,7},{6,4},{7,5},{8,10},{9,11},{10,... | collective-permute-start | bytes 294920 | tf_op jit(solution)/shard_map/ppermute | solution.py:282
  29.3 3.5 %collective-permute-start.6 = (f32[80,512]{1,0:T(8,128)S(1)}, f32[80,512]{1,0:T(8,128)S(1)}, u32[]{:S(2)}, u32[]{:S(2)}) collective-permute-start(f32[80,512]{1,0:T(8,128)S(1)} %add.34.refs_0_), channel_id=1, source_target_pairs={{0,1},{1,0},{2,3},{3,2},{4,5},{5,4},{6,7},{7,6},{8,9},{9,8},{10,11... | collective-permute-start | bytes 491528 | tf_op jit(solution)/shard_map/ppermute | solution.py:283
  32.7 1.4 %collective-permute-start.13 = (f32[48,512]{1,0:T(8,128)S(1)}, f32[48,512]{1,0:T(8,128)S(1)}, u32[]{:S(2)}, u32[]{:S(2)}) collective-permute-start(f32[48,512]{1,0:T(8,128)S(1)} %add.36.refs_2_), channel_id=1, source_target_pairs={{0,1},{1,0},{2,3},{3,2},{4,5},{5,4},{6,7},{7,6},{8,9},{9,8},{10,11... | collective-permute-start | bytes 294920 | tf_op jit(solution)/shard_map/ppermute | solution.py:283
  39.4 6.3 %collective-permute-start.16 = (bf16[32,2560]{1,0:T(8,128)(2,1)S(1)}, bf16[32,2560]{1,0:T(8,128)(2,1)S(1)}, u32[]{:S(2)}, u32[]{:S(2)}) collective-permute-start(bf16[32,2560]{1,0:T(8,128)(2,1)S(1)} %get-tuple-element.31), channel_id=1, source_target_pairs={{0,4},{4,0},{8,12},{12,8},{16,20},{20,16},{24,28},{28,24},{1,5},{5... | collective-permute-start | bytes 491528 | tf_op jit(solution)/shard_map/ppermute | solution.py:292
  40.2 12.6 %collective-permute-start.14 = (bf16[64,2560]{1,0:T(8,128)(2,1)S(1)}, bf16[64,2560]{1,0:T(8,128)(2,1)S(1)}, u32[]{:S(2)}, u32[]{:S(2)}) collective-permute-start(bf16[64,2560]{1,0:T(8,128)(2,1)S(1)} %get-tuple-element.28), channel_id=1, source_target_pairs={{0,8},{4,12},{8,0},{12,4},{16,24},{20,28},{24,16},{28,20},{1,9},{5... | collective-permute-start | bytes 983048 | tf_op jit(solution)/shard_map/ppermute | solution.py:295
  45.7 8.9 %collective-permute-start.17 = (bf16[32,2560]{1,0:T(8,128)(2,1)S(1)}, bf16[32,2560]{1,0:T(8,128)(2,1)S(1)}, u32[]{:S(2)}, u32[]{:S(2)}) collective-permute-start(bf16[32,2560]{1,0:T(8,128)(2,1)S(1)} %get-tuple-element.33), channel_id=1, source_target_pairs={{0,4},{4,0},{8,12},{12,8},{16,20},{20,16},{24,28},{28,24},{1,5},{5... | collective-permute-start | bytes 491528 | tf_op jit(solution)/shard_map/ppermute | solution.py:294
  46.0 11.8 %collective-permute-start.19 = (bf16[32,2560]{1,0:T(8,128)(2,1)S(1)}, bf16[32,2560]{1,0:T(8,128)(2,1)S(1)}, u32[]{:S(2)}, u32[]{:S(2)}) collective-permute-start(bf16[32,2560]{1,0:T(8,128)(2,1)S(1)} %add_convert_fusion), channel_id=1, source_target_pairs={{0,16},{4,20},{8,24},{12,28},{16,0},{20,4},{24,8},{28,12},{1,17},{... | collective-permute-start | bytes 491528 | tf_op jit(solution)/shard_map/ppermute | solution.py:293
  52.9 9.0 %collective-permute-start.15 = (f32[32,2560]{1,0:T(8,128)S(1)}, f32[32,2560]{1,0:T(8,128)S(1)}, u32[]{:S(2)}, u32[]{:S(2)}) collective-permute-start(f32[32,2560]{1,0:T(8,128)S(1)} %slice_add_fusion), channel_id=1, source_target_pairs={{0,4},{4,0},{8,12},{12,8},{16,20},{20,16},{24,28},{28,24},{1,5},{5... | collective-permute-start | bytes 983048 | tf_op jit(solution)/shard_map/ppermute | solution.py:296
  54.6 7.3 %collective-permute-start.18 = (bf16[32,2560]{1,0:T(8,128)(2,1)S(1)}, bf16[32,2560]{1,0:T(8,128)(2,1)S(1)}, u32[]{:S(2)}, u32[]{:S(2)}) collective-permute-start(bf16[32,2560]{1,0:T(8,128)(2,1)S(1)} %add_convert_fusion.1), channel_id=1, source_target_pairs={{0,24},{4,28},{8,16},{12,20},{16,8},{20,12},{24,0},{28,4},{1,25},{... | collective-permute-start | bytes 491528 | tf_op jit(solution)/shard_map/ppermute | solution.py:294

commit v4 on v3

--- a/solution.py
+++ b/solution.py
@@ -10,6 +10,7 @@
 NS_STEPS = 8
 SLOT = 64
 BF16, F32 = jnp.bfloat16, jnp.float32
+FIRST = ((5,), (7,), (3,), (2,))
 
 
 def cost(us):
@@ -142,10 +143,11 @@
 
 def procrustes_body(block, plan, *refs):
     n = 2 * len(plan) if plan else 1
-    parts, (weights_ref, core_ref, coret_ref, wt_ref, rot_ref, proj_ref, projt) = (
-        refs[:n],
-        refs[n:],
-    )
+    parts, (weights_ref, core_ref, coret_ref, *rest) = refs[:n], refs[n:]
+    if plan:
+        masked_ref, wt_ref, rot_ref, proj_ref, *sends, projt = rest
+    else:
+        wt_ref, rot_ref, proj_ref, projt = rest
     npat, rank = weights_ref.shape
     if plan:
         place_rows(projt, parts, block, plan)
@@ -156,8 +158,8 @@
     core, coret = core_ref[...], coret_ref[...]
     weights = weights_ref[...]
     wide = jnp.broadcast_to(weights[:, None, :], (npat, SLOT, rank)).reshape(npat * SLOT, rank)
-    hi, mid, lo = split3(proj * wide)
-    target = dot(hi, coret) + (dot(mid, coret) + dot(lo, coret))
+    hi, lo = split2(proj * wide)
+    target = dot(hi, coret) + dot(lo, coret)
     pair = 2 * SLOT
     row = lax.broadcasted_iota(jnp.int32, (pair, pair), 0) // SLOT
     col = lax.broadcasted_iota(jnp.int32, (pair, pair), 1) // SLOT
@@ -169,31 +171,43 @@
         qs.append((two * lax.rsqrt(total + 1e-06)).reshape(pair, rank))
     for step in range(NS_STEPS):
         halves = [split2(q) for q in qs]
-        grams = [jnp.where(same, dot3(h, h, NT), 0.0) for h in halves]
-        prods = [dot3(split2(g), h) for g, h in zip(grams, halves)]
+        stacks = [jnp.concatenate(h, 0) for h in halves]
+        wides = [dot(k, k, NT) for k in stacks]
+        grams = [w[:pair, :pair] + (w[:pair, pair:] + w[pair:, :pair]) for w in wides]
+        grams = [split2(jnp.where(same, g, 0.0)) for g in grams]
+        prods = [
+            dot(jnp.concatenate([g[0], g[0]], 1), k) + dot(g[1], h[0])
+            for g, h, k in zip(grams, halves, stacks)
+        ]
         qs = [1.5 * q - 0.5 * x for q, x in zip(qs, prods)]
     q = jnp.concatenate(qs, 0)
-    hi, mid, lo = split3(q)
-    rotated = dot(hi, core) + (dot(mid, core) + dot(lo, core))
+    hi, lo = split2(q)
+    rotated = dot(hi, core) + dot(lo, core)
     rot_ref[...] = rotated
     wt_ref[...] = (rotated * wide).T.astype(jnp.bfloat16)
-
-
-def procrustes(parts, plan, weights, core, block):
+    if plan:
+        term_body(block, FIRST, wt_ref, masked_ref, *sends)
+
+
+def procrustes(parts, plan, weights, core, block, masked=None):
     npat, rank = weights.shape
     rows = npat * SLOT
+    sends = [] if masked is None else [
+        jax.ShapeDtypeStruct((len(pick) * block, masked.shape[1]), BF16) for pick in FIRST
+    ]
     return pl.pallas_call(
         functools.partial(procrustes_body, block, plan),
         out_shape=[
             jax.ShapeDtypeStruct((rank, rows), jnp.bfloat16),
             jax.ShapeDtypeStruct((rows, rank), jnp.float32),
             jax.ShapeDtypeStruct((rows, rank), jnp.float32),
+            *sends,
         ],
         scratch_shapes=[pltpu.VMEM((rank, rows), jnp.float32)],
         compiler_params=params(16),
-        cost_estimate=cost(0),
+        cost_estimate=cost(4.8),
         name="procrustes",
-    )(*parts, weights, core, core.T)
+    )(*parts, weights, core, core.T, *([] if masked is None else [masked]))
 
 
 def rows_body(rot_ref, proj_ref, out_ref):
@@ -282,19 +296,22 @@
     tot1 = core1 + to_x(core1)
     parts = [tot0, to_core(tot0), tot1, to_core(tot1)]
     plan = (((0, -1, 1, -2, 2), True), ((-3, 3, 4), True),)
-    wt, rot, proj = procrustes(parts, plan, patient_weights, core, block)
+    wt, rot, proj, there2, there3, near, own = procrustes(
+        parts, plan, patient_weights, core, block, masked
+    )
 
     y, z1, z2, z3 = (flip("subj", 8, bit) for bit in (1, 2, 4, 6))
-    there2, there3, near = term(wt, masked, block, ((5,), (7,), (3, 2)), (BF16, BF16, BF16))
     here2, here3, there0, here0 = term(
         wt, masked, block, ((4,), (6,), (1,), (0,)), (F32, F32, F32, F32)
     )
-    got2, there3 = tie(y(there2), there3)
-    far2 = z2((here2 + got2.astype(F32)).astype(BF16))
-    far3 = z3((here3 + y(there3).astype(F32)).astype(BF16))
-    near = z1(near).astype(F32)
-    other = y(there0 + near[:block])
-    out = (here0 + near[block:]) + other + (far3.astype(F32) + far2.astype(F32))
+    got2, own = tie(y(there2), own)
+    far2 = z2((here2 + got2.astype(F32)).astype(BF16)).astype(F32)
+    got3 = y(there3)
+    far3 = z3((here3 + got3.astype(F32)).astype(BF16)).astype(F32)
+    other = there0 + z1(near).astype(F32)
+    other = jnp.concatenate([y(p) for p in jnp.split(other, 2, axis=0)], 0)
+    own = z1(own).astype(F32)
+    out = (((here0 + own) + far2) + far3) + other
     rows = patient_rows(rot, proj, npat)
     return out, rows
 

time: 62.9 us -> 61.2 us (0.973)
  waiting for transfers between devices: 26.4 us -> 23 us
  starting transfers between devices: 21.5 us -> 23.6 us
    ppermute x4, starting transfers between devices: 0.65 us -> 8.22 us  [step(): lax.ppermute(back, 'subj', BACK)]
    ppermute x4, starting transfers between devices: 8.62 us -> 1.11 us  [step(): lax.ppermute(ahead, 'subj', AHEAD)]
    ppermute x4, waiting for transfers between devices: 6.37 us -> 1.7 us  [step(): lax.ppermute(ahead, 'subj', AHEAD)]
    ppermute x4, waiting for transfers between devices: 1.81 us -> 6.43 us  [step(): lax.ppermute(back, 'subj', BACK)]
    ppermute x6 -> x8, waiting for transfers between devices: 12.5 us -> 9.18 us  [the longest x1 5.79 us: per_device(): far2 = z2((here2 + got2.astype(F32)).astype(BF16)).astype(F32)]
    ppermute x6 -> x8, starting transfers between devices: 8.64 us -> 10.7 us  [the longest x1 2.18 us: per_device(): far2 = z2((here2 + got2.astype(F32)).astype(BF16)).astype(F32)]
  transfers between devices with their start and end apart: 20 -> 22, of which waited for: 11 -> 10; matrix products, arithmetic and copies ran while one was open for 2% -> 2% of each run, Pallas kernels for 7% -> 7%
where the time goes in v4:
time: 61.2 us; the launch traced here: 61 us
  starting transfers between devices  23.6 us (39%)
  waiting for transfers between devices  23 us (38%)
  Pallas kernels  9.16 us (15%)
  local copies, waits for them, and re-layouts  2.7 us (4%)
  other arithmetic  1.68 us (3%)
  between operations  0.84 us (1%)
    ppermute x4, starting transfers between devices, step(): lax.ppermute(back, 'subj', BACK)  8.22 us
    ppermute x4, waiting for transfers between devices, step(): lax.ppermute(back, 'subj', BACK)  6.43 us
    ppermute x1, waiting for transfers between devices, per_device(): far2 = z2((here2 + got2.astype(F32)).astype(BF16)).astype(F32)  5.79 us
    pallas_call x1, Pallas kernels, procrustes(): pl.pallas_call(functools.partial(procrustes_body, block, plan), out_shape...  4.88 us
    ppermute x1, waiting for transfers between devices, per_device(): tot1 = core1 + to_x(core1)  3.25 us
    ppermute x1, waiting for transfers between devices, per_device(): got2, own = tie(y(there2), own)  3.23 us
    unnamed x11, local copies, waits for them, and re-layouts  2.41 us
    ppermute x1, starting transfers between devices, per_device(): far2 = z2((here2 + got2.astype(F32)).astype(BF16)).astype(F32)  2.18 us
  transfers between devices with their start and end apart: 22, of which 10 were waited for; matrix products, arithmetic and copies ran while one was open for 2% of the time, Pallas kernels for 7%

profile of v4, /device:TPU:0, one launch (start us, length us, event | category | flops | bytes accessed | tf_op | source)
XLA Modules:
  0.0 61.0 jit_solution(2375989330183694294)
XLA Ops:
  0.6 0.0 copy-start.2
  0.6 3.0 %collective-permute-start.1 = (bf16[32,2560]{1,0:T(8,128)(2,1)}, bf16[32,2560]{1,0:T(8,128)(2,1)S(1)}, u32[]{:S(2)}, u32[]{:S(2)}) collective-permute-start(bf16[32,2560]{1,0:T(8,128)(2,1)} %refs_0_.1), channel_id=1, source_target_pairs={{8,0},{16,8},{24,16},{28,24},{20,28},{12,20},{4,12},{0,4},{9,1},{1... | collective-permute-start | bytes 491528 | tf_op jit(solution)/shard_map/ppermute | solution.py:282
  3.7 0.1 collective-permute-start
  3.8 0.7 %convert_element_type.27 = bf16[8,20]{1,0:T(8,128)(2,1)S(1)} convert(s32[8,20]{1,0:T(8,128)} %param.7) | non-fusion elementwise | flops 160 | bytes 960 | tf_op jit(solution)/shard_map/convert_element_type | solution.py:76
  4.5 0.1 copy.9
  4.6 0.1 broadcast_bitcast_fusion
  4.7 0.1 copy.10.gate_ref
  4.7 0.0 copy-start
  4.8 1.6 %copy-done = bf16[8,56,2560]{2,1,0:T(8,128)(2,1)S(1)} copy-done((bf16[8,56,2560]{2,1,0:T(8,128)(2,1)S(1)}, bf16[8,56,2560]{2,1,0:T(8,128)(2,1)}, u32[]{:S(2)}) %copy-start) | copy-done | bytes 2293784
  6.4 0.7 %copy-done.4 = s32[8]{0:T(128)S(1)} copy-done((s32[8]{0:T(128)S(1)}, s32[8]{0:T(128)}, u32[]{:S(2)}) %copy-start.4) | copy-done | bytes 56
  7.0 1.1 %mask_visits.1.refs_5_.refs_4_.refs_7_.masked_ref = bf16[512,2560]{1,0:T(8,128)(2,1)S(1)} custom-call(s32[8]{0:T(128)S(1)} %copy-done.4, bf16[8,1,2560]{2,1,0:T(2,128)(2,1)S(1)} %copy.10.gate_ref, bf16[8,56,2560]{2,1,0:T(8,128)(2,1)S(1)} %copy-done), custom_call_target="tpu_custom_call" | custom-call | tf_op jit(solution)/shard_map/mask_visits/pallas_call | solution.py:77
  8.2 0.0 collective-permute-done.1.refs_2_
  8.2 2.0 %collective-permute-start.3 = (bf16[32,2560]{1,0:T(8,128)(2,1)S(1)}, bf16[32,2560]{1,0:T(8,128)(2,1)S(1)}, u32[]{:S(2)}, u32[]{:S(2)}) collective-permute-start(bf16[32,2560]{1,0:T(8,128)(2,1)S(1)} %collective-permute-done.1.refs_2_), channel_id=1, source_target_pairs={{8,0},{16,8},{24,16},{28,24},{20,28},{12,20},{4,12},{0,4},{9,1},{1... | collective-permute-start | bytes 491528 | tf_op jit(solution)/shard_map/ppermute | solution.py:282
  10.2 0.0 collective-permute-done.refs_1_
  10.2 0.1 collective-permute-start.2
  10.3 3.6 %collective-permute-done.3.refs_4_ = bf16[32,2560]{1,0:T(8,128)(2,1)S(1)} collective-permute-done((bf16[32,2560]{1,0:T(8,128)(2,1)S(1)}, bf16[32,2560]{1,0:T(8,128)(2,1)S(1)}, u32[]{:S(2)}, u32[]{:S(2)}) %collective-permute-start.3) | collective-permute-done | bytes 163872 | tf_op jit(solution)/shard_map/ppermute | solution.py:282
  13.9 1.6 %collective-permute-start.8 = (bf16[32,2560]{1,0:T(8,128)(2,1)S(1)}, bf16[32,2560]{1,0:T(8,128)(2,1)S(1)}, u32[]{:S(2)}, u32[]{:S(2)}) collective-permute-start(bf16[32,2560]{1,0:T(8,128)(2,1)S(1)} %collective-permute-done.3.refs_4_), channel_id=1, source_target_pairs={{8,0},{16,8},{24,16},{28,24},{20,28},{12,20},{4,12},{0,4},{9,1},{1... | collective-permute-start | bytes 491528 | tf_op jit(solution)/shard_map/ppermute | solution.py:282
  15.5 0.0 collective-permute-done.2.refs_3_
  15.5 0.4 collective-permute-start.7
  15.9 0.0 copy-done.2
  15.9 1.0 %project.2 = (f32[80,512]{1,0:T(8,128)S(1)}, f32[80,512]{1,0:T(8,128)S(1)}) custom-call(bf16[32,2560]{1,0:T(8,128)(2,1)S(1)} %copy-done.2, bf16[32,2560]{1,0:T(8,128)(2,1)S(1)} %collective-permute-done.refs_1_, bf16[32,2560]{1,0:T(8,128)(2,1)S(1)} %collective-permute-done.1.refs_2_, bf16[32,2560]{1,0:T(8,128)(2,1)S(1)} %collective-permute-done.2.refs_3_, ...), custom_call_target="tpu_custom_call" | custom-call | tf_op jit(solution)/shard_map/project/pallas_call | solution.py:113
  17.0 0.0 copy-start.1
  17.0 0.0 copy-start.3
  17.0 0.1 collective-permute-start.4
  17.1 2.1 %collective-permute-done.8.refs_1_ = bf16[32,2560]{1,0:T(8,128)(2,1)S(1)} collective-permute-done((bf16[32,2560]{1,0:T(8,128)(2,1)S(1)}, bf16[32,2560]{1,0:T(8,128)(2,1)S(1)}, u32[]{:S(2)}, u32[]{:S(2)}) %collective-permute-start.8) | collective-permute-done | bytes 163872 | tf_op jit(solution)/shard_map/ppermute | solution.py:282
  19.2 1.6 %collective-permute-start.10 = (bf16[16,2560]{1,0:T(8,128)(2,1)S(1)}, bf16[16,2560]{1,0:T(8,128)(2,1)S(1)}, u32[]{:S(2)}, u32[]{:S(2)}) collective-permute-start(bf16[16,2560]{1,0:T(8,128)(2,1)S(1)} %slice.9), channel_id=1, source_target_pairs={{8,0},{16,8},{24,16},{28,24},{20,28},{12,20},{4,12},{0,4},{9,1},{1... | collective-permute-start | bytes 245768 | tf_op jit(solution)/shard_map/ppermute | solution.py:282
  20.9 0.0 collective-permute-done.7.refs_0_
  20.9 0.5 collective-permute-start.9
  21.3 0.0 collective-permute-done.4
  21.4 1.7 %collective-permute-start.5 = (f32[80,512]{1,0:T(8,128)S(1)}, f32[80,512]{1,0:T(8,128)S(1)}, u32[]{:S(2)}, u32[]{:S(2)}) collective-permute-start(f32[80,512]{1,0:T(8,128)S(1)} %add.33), channel_id=1, source_target_pairs={{0,2},{1,3},{2,0},{3,1},{4,6},{5,7},{6,4},{7,5},{8,10},{9,11},{10,... | collective-permute-start | bytes 491528 | tf_op jit(solution)/shard_map/ppermute | solution.py:291
  23.0 0.7 %collective-permute-done.10.refs_3_ = bf16[16,2560]{1,0:T(8,128)(2,1)S(1)} collective-permute-done((bf16[16,2560]{1,0:T(8,128)(2,1)S(1)}, bf16[16,2560]{1,0:T(8,128)(2,1)S(1)}, u32[]{:S(2)}, u32[]{:S(2)}) %collective-permute-start.10) | collective-permute-done | bytes 81952 | tf_op jit(solution)/shard_map/ppermute | solution.py:282
  23.7 1.7 %collective-permute-done.9.refs_2_ = bf16[16,2560]{1,0:T(8,128)(2,1)S(1)} collective-permute-done((bf16[16,2560]{1,0:T(8,128)(2,1)S(1)}, bf16[16,2560]{1,0:T(8,128)(2,1)S(1)}, u32[]{:S(2)}, u32[]{:S(2)}) %collective-permute-start.9) | collective-permute-done | bytes 81952 | tf_op jit(solution)/shard_map/ppermute | solution.py:282
  25.4 0.9 %project.3 = (f32[48,512]{1,0:T(8,128)S(1)}, f32[48,512]{1,0:T(8,128)S(1)}) custom-call(bf16[32,2560]{1,0:T(8,128)(2,1)S(1)} %collective-permute-done.7.refs_0_, bf16[32,2560]{1,0:T(8,128)(2,1)S(1)} %collective-permute-done.8.refs_1_, bf16[16,2560]{1,0:T(8,128)(2,1)S(1)} %collective-permute-done.9.refs_2_, ...), custom_call_target="tpu_custom_call" | custom-call | tf_op jit(solution)/shard_map/project/pallas_call | solution.py:113
  26.3 0.1 collective-permute-start.11
  26.4 1.3 %collective-permute-done.11 = f32[48,512]{1,0:T(8,128)S(1)} collective-permute-done((f32[48,512]{1,0:T(8,128)S(1)}, f32[48,512]{1,0:T(8,128)S(1)}, u32[]{:S(2)}, u32[]{:S(2)}) %collective-permute-start.11) | collective-permute-done | bytes 98336 | tf_op jit(solution)/shard_map/ppermute | solution.py:295
  27.7 1.6 %collective-permute-start.12 = (f32[48,512]{1,0:T(8,128)S(1)}, f32[48,512]{1,0:T(8,128)S(1)}, u32[]{:S(2)}, u32[]{:S(2)}) collective-permute-start(f32[48,512]{1,0:T(8,128)S(1)} %add.35), channel_id=1, source_target_pairs={{0,2},{1,3},{2,0},{3,1},{4,6},{5,7},{6,4},{7,5},{8,10},{9,11},{10,... | collective-permute-start | bytes 294920 | tf_op jit(solution)/shard_map/ppermute | solution.py:296
  29.3 0.0 collective-permute-done.5
  29.3 0.1 collective-permute-start.6
  29.4 3.3 %collective-permute-done.12 = f32[48,512]{1,0:T(8,128)S(1)} collective-permute-done((f32[48,512]{1,0:T(8,128)S(1)}, f32[48,512]{1,0:T(8,128)S(1)}, u32[]{:S(2)}, u32[]{:S(2)}) %collective-permute-start.12) | collective-permute-done | bytes 98336 | tf_op jit(solution)/shard_map/ppermute | solution.py:296
  32.6 0.1 collective-permute-start.13
  32.7 0.0 copy-done.1
  32.7 0.1 copy.11
  32.8 0.0 collective-permute-done.6.refs_1_
  32.8 1.2 %collective-permute-done.13.refs_3_ = f32[48,512]{1,0:T(8,128)S(1)} collective-permute-done((f32[48,512]{1,0:T(8,128)S(1)}, f32[48,512]{1,0:T(8,128)S(1)}, u32[]{:S(2)}, u32[]{:S(2)}) %collective-permute-start.13) | collective-permute-done | bytes 98336 | tf_op jit(solution)/shard_map/ppermute | solution.py:297
  34.0 4.9 %procrustes.1 = (bf16[256,512]{1,0:T(8,128)(2,1)S(1)}, f32[512,256]{1,0:T(8,128)S(1)}, f32[512,256]{1,0:T(8,128)S(1)}, bf16[32,2560]{1,0:T(8,128)(2,1)S(1)}, bf1...) custom-call(f32[80,512]{1,0:T(8,128)S(1)} %add.34.refs_0_, ...), custom_call_target="tpu_custom_call" | custom-call | bytes 17280000 | tf_op jit(solution)/shard_map/procrustes/pallas_call | solution.py:198
  38.9 1.6 %collective-permute-start.14 = (bf16[32,2560]{1,0:T(8,128)(2,1)S(1)}, bf16[32,2560]{1,0:T(8,128)(2,1)S(1)}, u32[]{:S(2)}, u32[]{:S(2)}) collective-permute-start(bf16[32,2560]{1,0:T(8,128)(2,1)S(1)} %get-tuple-element.29), channel_id=1, source_target_pairs={{0,4},{4,0},{8,12},{12,8},{16,20},{20,16},{24,28},{28,24},{1,5},{5... | collective-permute-start | bytes 491528 | tf_op jit(solution)/shard_map/ppermute | solution.py:307
  40.5 0.5 term.1
  41.0 0.5 collective-permute-start.17
  41.6 1.2 %collective-permute-start.19 = (bf16[32,2560]{1,0:T(8,128)(2,1)S(1)}, bf16[32,2560]{1,0:T(8,128)(2,1)S(1)}, u32[]{:S(2)}, u32[]{:S(2)}) collective-permute-start(bf16[32,2560]{1,0:T(8,128)(2,1)S(1)} %get-tuple-element.37), channel_id=1, source_target_pairs={{0,8},{4,12},{8,0},{12,4},{16,24},{20,28},{24,16},{28,20},{1,9},{5... | collective-permute-start | bytes 491528 | tf_op jit(solution)/shard_map/ppermute | solution.py:311
  42.8 3.2 %collective-permute-done.14 = bf16[32,2560]{1,0:T(8,128)(2,1)S(1)} collective-permute-done((bf16[32,2560]{1,0:T(8,128)(2,1)S(1)}, bf16[32,2560]{1,0:T(8,128)(2,1)S(1)}, u32[]{:S(2)}, u32[]{:S(2)}) %collective-permute-start.14) | collective-permute-done | bytes 163872 | tf_op jit(solution)/shard_map/ppermute | solution.py:307
  46.0 2.2 %collective-permute-start.16 = (bf16[32,2560]{1,0:T(8,128)(2,1)S(1)}, bf16[32,2560]{1,0:T(8,128)(2,1)S(1)}, u32[]{:S(2)}, u32[]{:S(2)}) collective-permute-start(bf16[32,2560]{1,0:T(8,128)(2,1)S(1)} %add_convert_fusion.1), channel_id=1, source_target_pairs={{0,16},{4,20},{8,24},{12,28},{16,0},{20,4},{24,8},{28,12},{1,17},{... | collective-permute-start | bytes 491528 | tf_op jit(solution)/shard_map/ppermute | solution.py:308
  48.2 1.0 %collective-permute-start.15 = (bf16[32,2560]{1,0:T(8,128)(2,1)S(1)}, bf16[32,2560]{1,0:T(8,128)(2,1)S(1)}, u32[]{:S(2)}, u32[]{:S(2)}) collective-permute-start(bf16[32,2560]{1,0:T(8,128)(2,1)S(1)} %get-tuple-element.31), channel_id=1, source_target_pairs={{0,8},{4,12},{8,0},{12,4},{16,24},{20,28},{24,16},{28,20},{1,9},{5... | collective-permute-start | bytes 491528 | tf_op jit(solution)/shard_map/ppermute | solution.py:313
  49.2 0.0 collective-permute-done.17
  49.3 2.1 %collective-permute-start.18 = (bf16[32,2560]{1,0:T(8,128)(2,1)S(1)}, bf16[32,2560]{1,0:T(8,128)(2,1)S(1)}, u32[]{:S(2)}, u32[]{:S(2)}) collective-permute-start(bf16[32,2560]{1,0:T(8,128)(2,1)S(1)} %add_convert_fusion), channel_id=1, source_target_pairs={{0,24},{4,28},{8,16},{12,20},{16,8},{20,12},{24,0},{28,4},{1,25},{... | collective-permute-start | bytes 491528 | tf_op jit(solution)/shard_map/ppermute | solution.py:310
  51.4 0.0 collective-permute-done.19
  51.4 1.6 %collective-permute-start.20 = (f32[16,2560]{1,0:T(8,128)S(1)}, f32[16,2560]{1,0:T(8,128)S(1)}, u32[]{:S(2)}, u32[]{:S(2)}) collective-permute-start(f32[16,2560]{1,0:T(8,128)S(1)} %get-tuple-element.40), channel_id=1, source_target_pairs={{0,4},{4,0},{8,12},{12,8},{16,20},{20,16},{24,28},{28,24},{1,5},{5... | collective-permute-start | bytes 491528 | tf_op jit(solution)/shard_map/ppermute | solution.py:312
  53.1 0.4 collective-permute-start.21
  53.5 0.7 %patient_rows.1 = f32[8,256]{1,0:T(8,128)} custom-call(f32[512,256]{1,0:T(8,128)S(1)} %get-tuple-element.38.rot_ref, f32[512,256]{1,0:T(8,128)S(1)} %get-tuple-element.39.proj_ref), custom_call_target="tpu_custom_call" | custom-call | tf_op jit(solution)/shard_map/patient_rows/pallas_call | solution.py:220
  54.2 5.8 %collective-permute-done.16 = bf16[32,2560]{1,0:T(8,128)(2,1)S(1)} collective-permute-done((bf16[32,2560]{1,0:T(8,128)(2,1)S(1)}, bf16[32,2560]{1,0:T(8,128)(2,1)S(1)}, u32[]{:S(2)}, u32[]{:S(2)}) %collective-permute-start.16) | collective-permute-done | bytes 163872 | tf_op jit(solution)/shard_map/ppermute | solution.py:308
  60.0 0.0 collective-permute-done.15
  60.0 0.0 collective-permute-done.18
  60.0 0.0 collective-permute-done.20
  60.0 0.1 collective-permute-done.21
  60.2 0.8 %maximum_add_fusion = f32[32,2560]{1,0:T(8,128)} fusion(f32[16,2560]{1,0:T(8,128)S(1)} %collective-permute-done.21, f32[16,2560]{1,0:T(8,128)S(1)} %collective-permute-done.20, bf16[32,2560]{1,0:T(8,128)(2,1)S(1)} %collective-permute-done.18, bf16[32,2560]{1,0:T(8,128)(2,1)S(1)} %collective-permute-done.16, f32[32,2560]{1,0:T(8,128)S(1)} %get-tuple-element.28, ...), kind=kLoop, calls=%fused_computation | loop fusion | flops 655360 | bytes 1474560 | tf_op jit(solution)/shard_map/add | solution.py:314
  (12 shorter events, 0.2 us)
Async XLA Ops:
  0.6 15.3 %copy-start.2 = (bf16[32,2560]{1,0:T(8,128)(2,1)S(1)}, bf16[32,2560]{1,0:T(8,128)(2,1)}, u32[]{:S(2)}) copy-start(bf16[32,2560]{1,0:T(8,128)(2,1)} %refs_0_.1) | copy-start | bytes 491524
  0.6 7.6 %collective-permute-start.1 = (bf16[32,2560]{1,0:T(8,128)(2,1)}, bf16[32,2560]{1,0:T(8,128)(2,1)S(1)}, u32[]{:S(2)}, u32[]{:S(2)}) collective-permute-start(bf16[32,2560]{1,0:T(8,128)(2,1)} %refs_0_.1), channel_id=1, source_target_pairs={{8,0},{16,8},{24,16},{28,24},{20,28},{12,20},{4,12},{0,4},{9,1},{1... | collective-permute-start | bytes 491528 | tf_op jit(solution)/shard_map/ppermute | solution.py:282
  3.7 6.5 %collective-permute-start = (bf16[32,2560]{1,0:T(8,128)(2,1)}, bf16[32,2560]{1,0:T(8,128)(2,1)S(1)}, u32[]{:S(2)}, u32[]{:S(2)}) collective-permute-start(bf16[32,2560]{1,0:T(8,128)(2,1)} %refs_0_.1), channel_id=1, source_target_pairs={{0,8},{8,16},{16,24},{24,28},{28,20},{20,12},{12,4},{4,0},{1,9},{9... | collective-permute-start | bytes 491528 | tf_op jit(solution)/shard_map/ppermute | solution.py:282
  4.7 1.6 %copy-start = (bf16[8,56,2560]{2,1,0:T(8,128)(2,1)S(1)}, bf16[8,56,2560]{2,1,0:T(8,128)(2,1)}, u32[]{:S(2)}) copy-start(bf16[8,56,2560]{2,1,0:T(8,128)(2,1)} %visits_ref.1) | copy-start | bytes 6881284
  6.4 0.7 %copy-start.4 = (s32[8]{0:T(128)S(1)}, s32[8]{0:T(128)}, u32[]{:S(2)}) copy-start(s32[8]{0:T(128)} %counts_ref.1) | copy-start | bytes 100
  8.2 5.7 %collective-permute-start.3 = (bf16[32,2560]{1,0:T(8,128)(2,1)S(1)}, bf16[32,2560]{1,0:T(8,128)(2,1)S(1)}, u32[]{:S(2)}, u32[]{:S(2)}) collective-permute-start(bf16[32,2560]{1,0:T(8,128)(2,1)S(1)} %collective-permute-done.1.refs_2_), channel_id=1, source_target_pairs={{8,0},{16,8},{24,16},{28,24},{20,28},{12,20},{4,12},{0,4},{9,1},{1... | collective-permute-start | bytes 491528 | tf_op jit(solution)/shard_map/ppermute | solution.py:282
  10.2 5.4 %collective-permute-start.2 = (bf16[32,2560]{1,0:T(8,128)(2,1)S(1)}, bf16[32,2560]{1,0:T(8,128)(2,1)S(1)}, u32[]{:S(2)}, u32[]{:S(2)}) collective-permute-start(bf16[32,2560]{1,0:T(8,128)(2,1)S(1)} %collective-permute-done.refs_1_), channel_id=1, source_target_pairs={{0,8},{8,16},{16,24},{24,28},{28,20},{20,12},{12,4},{4,0},{1,9},{9... | collective-permute-start | bytes 491528 | tf_op jit(solution)/shard_map/ppermute | solution.py:282
  13.9 5.3 %collective-permute-start.8 = (bf16[32,2560]{1,0:T(8,128)(2,1)S(1)}, bf16[32,2560]{1,0:T(8,128)(2,1)S(1)}, u32[]{:S(2)}, u32[]{:S(2)}) collective-permute-start(bf16[32,2560]{1,0:T(8,128)(2,1)S(1)} %collective-permute-done.3.refs_4_), channel_id=1, source_target_pairs={{8,0},{16,8},{24,16},{28,24},{20,28},{12,20},{4,12},{0,4},{9,1},{1... | collective-permute-start | bytes 491528 | tf_op jit(solution)/shard_map/ppermute | solution.py:282
  15.5 5.3 %collective-permute-start.7 = (bf16[32,2560]{1,0:T(8,128)(2,1)S(1)}, bf16[32,2560]{1,0:T(8,128)(2,1)S(1)}, u32[]{:S(2)}, u32[]{:S(2)}) collective-permute-start(bf16[32,2560]{1,0:T(8,128)(2,1)S(1)} %collective-permute-done.2.refs_3_), channel_id=1, source_target_pairs={{0,8},{8,16},{16,24},{24,28},{28,20},{20,12},{12,4},{4,0},{1,9},{9... | collective-permute-start | bytes 491528 | tf_op jit(solution)/shard_map/ppermute | solution.py:282
  17.0 15.7 %copy-start.1 = (bf16[256,256]{1,0:T(8,128)(2,1)S(1)}, bf16[256,256]{1,0:T(8,128)(2,1)}, u32[]{:S(2)}) copy-start(bf16[256,256]{1,0:T(8,128)(2,1)} %refs_5_.1) | copy-start | bytes 393220
  17.0 17.0 %copy-start.3 = (f32[8,256]{1,0:T(8,128)S(1)}, f32[8,256]{1,0:T(8,128)}, u32[]{:S(2)}) copy-start(f32[8,256]{1,0:T(8,128)} %refs_4_.1) | copy-start | bytes 24580
  17.0 4.3 %collective-permute-start.4 = (f32[80,512]{1,0:T(8,128)S(1)}, f32[80,512]{1,0:T(8,128)S(1)}, u32[]{:S(2)}, u32[]{:S(2)}) collective-permute-start(f32[80,512]{1,0:T(8,128)S(1)} %get-tuple-element.24), channel_id=1, source_target_pairs={{0,1},{1,0},{2,3},{3,2},{4,5},{5,4},{6,7},{7,6},{8,9},{9,8},{10,11... | collective-permute-start | bytes 491528 | tf_op jit(solution)/shard_map/ppermute | solution.py:290
  19.2 4.4 %collective-permute-start.10 = (bf16[16,2560]{1,0:T(8,128)(2,1)S(1)}, bf16[16,2560]{1,0:T(8,128)(2,1)S(1)}, u32[]{:S(2)}, u32[]{:S(2)}) collective-permute-start(bf16[16,2560]{1,0:T(8,128)(2,1)S(1)} %slice.9), channel_id=1, source_target_pairs={{8,0},{16,8},{24,16},{28,24},{20,28},{12,20},{4,12},{0,4},{9,1},{1... | collective-permute-start | bytes 245768 | tf_op jit(solution)/shard_map/ppermute | solution.py:282
  20.9 4.5 %collective-permute-start.9 = (bf16[16,2560]{1,0:T(8,128)(2,1)S(1)}, bf16[16,2560]{1,0:T(8,128)(2,1)S(1)}, u32[]{:S(2)}, u32[]{:S(2)}) collective-permute-start(bf16[16,2560]{1,0:T(8,128)(2,1)S(1)} %slice.8), channel_id=1, source_target_pairs={{0,8},{8,16},{16,24},{24,28},{28,20},{20,12},{12,4},{4,0},{1,9},{9... | collective-permute-start | bytes 245768 | tf_op jit(solution)/shard_map/ppermute | solution.py:282
  21.4 7.9 %collective-permute-start.5 = (f32[80,512]{1,0:T(8,128)S(1)}, f32[80,512]{1,0:T(8,128)S(1)}, u32[]{:S(2)}, u32[]{:S(2)}) collective-permute-start(f32[80,512]{1,0:T(8,128)S(1)} %add.33), channel_id=1, source_target_pairs={{0,2},{1,3},{2,0},{3,1},{4,6},{5,7},{6,4},{7,5},{8,10},{9,11},{10,... | collective-permute-start | bytes 491528 | tf_op jit(solution)/shard_map/ppermute | solution.py:291
  26.3 1.4 %collective-permute-start.11 = (f32[48,512]{1,0:T(8,128)S(1)}, f32[48,512]{1,0:T(8,128)S(1)}, u32[]{:S(2)}, u32[]{:S(2)}) collective-permute-start(f32[48,512]{1,0:T(8,128)S(1)} %get-tuple-element.26), channel_id=1, source_target_pairs={{0,1},{1,0},{2,3},{3,2},{4,5},{5,4},{6,7},{7,6},{8,9},{9,8},{10,11... | collective-permute-start | bytes 294920 | tf_op jit(solution)/shard_map/ppermute | solution.py:295
  27.7 4.9 %collective-permute-start.12 = (f32[48,512]{1,0:T(8,128)S(1)}, f32[48,512]{1,0:T(8,128)S(1)}, u32[]{:S(2)}, u32[]{:S(2)}) collective-permute-start(f32[48,512]{1,0:T(8,128)S(1)} %add.35), channel_id=1, source_target_pairs={{0,2},{1,3},{2,0},{3,1},{4,6},{5,7},{6,4},{7,5},{8,10},{9,11},{10,... | collective-permute-start | bytes 294920 | tf_op jit(solution)/shard_map/ppermute | solution.py:296
  29.3 3.5 %collective-permute-start.6 = (f32[80,512]{1,0:T(8,128)S(1)}, f32[80,512]{1,0:T(8,128)S(1)}, u32[]{:S(2)}, u32[]{:S(2)}) collective-permute-start(f32[80,512]{1,0:T(8,128)S(1)} %add.34.refs_0_), channel_id=1, source_target_pairs={{0,1},{1,0},{2,3},{3,2},{4,5},{5,4},{6,7},{7,6},{8,9},{9,8},{10,11... | collective-permute-start | bytes 491528 | tf_op jit(solution)/shard_map/ppermute | solution.py:297
  32.6 1.4 %collective-permute-start.13 = (f32[48,512]{1,0:T(8,128)S(1)}, f32[48,512]{1,0:T(8,128)S(1)}, u32[]{:S(2)}, u32[]{:S(2)}) collective-permute-start(f32[48,512]{1,0:T(8,128)S(1)} %add.36.refs_2_), channel_id=1, source_target_pairs={{0,1},{1,0},{2,3},{3,2},{4,5},{5,4},{6,7},{7,6},{8,9},{9,8},{10,11... | collective-permute-start | bytes 294920 | tf_op jit(solution)/shard_map/ppermute | solution.py:297
  38.9 7.1 %collective-permute-start.14 = (bf16[32,2560]{1,0:T(8,128)(2,1)S(1)}, bf16[32,2560]{1,0:T(8,128)(2,1)S(1)}, u32[]{:S(2)}, u32[]{:S(2)}) collective-permute-start(bf16[32,2560]{1,0:T(8,128)(2,1)S(1)} %get-tuple-element.29), channel_id=1, source_target_pairs={{0,4},{4,0},{8,12},{12,8},{16,20},{20,16},{24,28},{28,24},{1,5},{5... | collective-permute-start | bytes 491528 | tf_op jit(solution)/shard_map/ppermute | solution.py:307
  41.0 8.2 %collective-permute-start.17 = (bf16[32,2560]{1,0:T(8,128)(2,1)S(1)}, bf16[32,2560]{1,0:T(8,128)(2,1)S(1)}, u32[]{:S(2)}, u32[]{:S(2)}) collective-permute-start(bf16[32,2560]{1,0:T(8,128)(2,1)S(1)} %get-tuple-element.35), channel_id=1, source_target_pairs={{0,4},{4,0},{8,12},{12,8},{16,20},{20,16},{24,28},{28,24},{1,5},{5... | collective-permute-start | bytes 491528 | tf_op jit(solution)/shard_map/ppermute | solution.py:309
  41.6 9.8 %collective-permute-start.19 = (bf16[32,2560]{1,0:T(8,128)(2,1)S(1)}, bf16[32,2560]{1,0:T(8,128)(2,1)S(1)}, u32[]{:S(2)}, u32[]{:S(2)}) collective-permute-start(bf16[32,2560]{1,0:T(8,128)(2,1)S(1)} %get-tuple-element.37), channel_id=1, source_target_pairs={{0,8},{4,12},{8,0},{12,4},{16,24},{20,28},{24,16},{28,20},{1,9},{5... | collective-permute-start | bytes 491528 | tf_op jit(solution)/shard_map/ppermute | solution.py:311
  46.0 14.0 %collective-permute-start.16 = (bf16[32,2560]{1,0:T(8,128)(2,1)S(1)}, bf16[32,2560]{1,0:T(8,128)(2,1)S(1)}, u32[]{:S(2)}, u32[]{:S(2)}) collective-permute-start(bf16[32,2560]{1,0:T(8,128)(2,1)S(1)} %add_convert_fusion.1), channel_id=1, source_target_pairs={{0,16},{4,20},{8,24},{12,28},{16,0},{20,4},{24,8},{28,12},{1,17},{... | collective-permute-start | bytes 491528 | tf_op jit(solution)/shard_map/ppermute | solution.py:308
  48.2 11.8 %collective-permute-start.15 = (bf16[32,2560]{1,0:T(8,128)(2,1)S(1)}, bf16[32,2560]{1,0:T(8,128)(2,1)S(1)}, u32[]{:S(2)}, u32[]{:S(2)}) collective-permute-start(bf16[32,2560]{1,0:T(8,128)(2,1)S(1)} %get-tuple-element.31), channel_id=1, source_target_pairs={{0,8},{4,12},{8,0},{12,4},{16,24},{20,28},{24,16},{28,20},{1,9},{5... | collective-permute-start | bytes 491528 | tf_op jit(solution)/shard_map/ppermute | solution.py:313
  49.3 10.8 %collective-permute-start.18 = (bf16[32,2560]{1,0:T(8,128)(2,1)S(1)}, bf16[32,2560]{1,0:T(8,128)(2,1)S(1)}, u32[]{:S(2)}, u32[]{:S(2)}) collective-permute-start(bf16[32,2560]{1,0:T(8,128)(2,1)S(1)} %add_convert_fusion), channel_id=1, source_target_pairs={{0,24},{4,28},{8,16},{12,20},{16,8},{20,12},{24,0},{28,4},{1,25},{... | collective-permute-start | bytes 491528 | tf_op jit(solution)/shard_map/ppermute | solution.py:310
  51.4 8.6 %collective-permute-start.20 = (f32[16,2560]{1,0:T(8,128)S(1)}, f32[16,2560]{1,0:T(8,128)S(1)}, u32[]{:S(2)}, u32[]{:S(2)}) collective-permute-start(f32[16,2560]{1,0:T(8,128)S(1)} %get-tuple-element.40), channel_id=1, source_target_pairs={{0,4},{4,0},{8,12},{12,8},{16,20},{20,16},{24,28},{28,24},{1,5},{5... | collective-permute-start | bytes 491528 | tf_op jit(solution)/shard_map/ppermute | solution.py:312
  53.1 7.1 %collective-permute-start.21 = (f32[16,2560]{1,0:T(8,128)S(1)}, f32[16,2560]{1,0:T(8,128)S(1)}, u32[]{:S(2)}, u32[]{:S(2)}) collective-permute-start(f32[16,2560]{1,0:T(8,128)S(1)} %get-tuple-element.41), channel_id=1, source_target_pairs={{0,4},{4,0},{8,12},{12,8},{16,20},{20,16},{24,28},{28,24},{1,5},{5... | collective-permute-start | bytes 491528 | tf_op jit(solution)/shard_map/ppermute | solution.py:312

commit v5 on v4

--- a/solution.py
+++ b/solution.py
@@ -90,60 +90,63 @@
     )(counts, gate.reshape(npat, 1, ncode), visits)
 
 
-def project_body(n, split, *refs):
+def project_body(n, cuts, *refs):
     masked_ref, outs = refs[n], refs[n + 1 :]
     codes = jnp.concatenate([r[...] for r in refs[:n]], 0) if n > 1 else refs[0][...]
     both = dot(codes, masked_ref[...], NT)
-    if not split:
+    if not cuts:
         outs[0][...] = both
         return
-    mine_ref, theirs_ref, whole = outs
-    half = mine_ref.shape[0]
+    *outs, whole = outs
     whole[...] = both
     core = lax.axis_index("feat") % 2
-    mine_ref[...] = whole[rows_of(core, half), :]
-    theirs_ref[...] = whole[rows_of(1 - core, half), :]
-
-
-def project(blocks, masked, split=False):
+    for who, pieces in ((core, outs[: len(cuts)]), (1 - core, outs[len(cuts) :])):
+        at = who * sum(cuts)
+        for piece, rows in zip(pieces, cuts):
+            piece[...] = whole[pl.ds(pl.multiple_of(at, 8), rows), :]
+            at = at + rows
+
+
+def project(blocks, masked, cuts=()):
     rows = sum(b.shape[0] for b in blocks)
     cols = masked.shape[0]
-    whole = jax.ShapeDtypeStruct((rows, cols), jnp.float32)
-    part = jax.ShapeDtypeStruct((rows // 2, cols), jnp.float32)
-    return pl.pallas_call(
-        functools.partial(project_body, len(blocks), split),
-        out_shape=(part, part) if split else whole,
-        scratch_shapes=[pltpu.VMEM((rows, cols), jnp.float32)] if split else [],
+    shapes = [jax.ShapeDtypeStruct((r, cols), F32) for r in (tuple(cuts) * 2 or (rows,))]
+    outs = pl.pallas_call(
+        functools.partial(project_body, len(blocks), cuts),
+        out_shape=shapes,
+        scratch_shapes=[pltpu.VMEM((rows, cols), F32)] if cuts else [],
         compiler_params=params(10),
         cost_estimate=cost(0),
         name="project",
     )(*blocks, masked)
+    return (outs[: len(cuts)], outs[len(cuts) :]) if cuts else outs[0]
 
 
 def place_rows(projt, parts, block, plan):
     core = lax.axis_index("feat") % 2
-    at = 0
-    for blocks, split in plan:
-        left, right = parts[at], parts[at + 1]
-        at += 2
-        if not split:
-            for b, order in enumerate(blocks):
+    parts = list(parts)
+    for orders, cuts, back in plan:
+        if not cuts:
+            left, right = parts.pop(0), parts.pop(0)
+            for b, order in enumerate(orders):
                 rows = slice(b * block, (b + 1) * block)
                 projt[rows_of(spot(order), block), :] = left[rows, :] + right[rows, :]
             continue
         half = block // 2
-        count = len(blocks)
-        bases = [spot(o) * 2 + h for o in blocks for h in (0, 1)]
-        for u in range(count):
-            rows = slice(u * half, (u + 1) * half)
-            low, high = bases[u], bases[count + u]
-            projt[rows_of(jnp.where(core == 0, low, high), half), :] = left[rows, :]
-            projt[rows_of(jnp.where(core == 0, high, low), half), :] = right[rows, :]
+        bases = [spot(o) * 2 + h for o in orders for h in (0, 1)]
+        for who, sizes in ((core, cuts), (1 - core, back)):
+            at = 0
+            for rows in sizes:
+                piece = parts.pop(0)
+                for u in range(rows // half):
+                    base = jnp.where(who == 0, bases[at], bases[len(orders) + at])
+                    projt[rows_of(base, half), :] = piece[u * half : (u + 1) * half, :]
+                    at += 1
 
 
 def procrustes_body(block, plan, *refs):
-    n = 2 * len(plan) if plan else 1
-    parts, (weights_ref, core_ref, coret_ref, *rest) = refs[:n], refs[n:]
+    n = sum(len(cuts) + len(back) or 2 for _, cuts, back in plan) if plan else 1
+    parts, (weights_ref, core_ref, *rest) = refs[:n], refs[n:]
     if plan:
         masked_ref, wt_ref, rot_ref, proj_ref, *sends, projt = rest
     else:
@@ -155,11 +158,11 @@
         projt[...] = parts[0][...]
     proj = projt[...].T
     proj_ref[...] = proj
-    core, coret = core_ref[...], coret_ref[...]
+    core = core_ref[...]
     weights = weights_ref[...]
     wide = jnp.broadcast_to(weights[:, None, :], (npat, SLOT, rank)).reshape(npat * SLOT, rank)
     hi, lo = split2(proj * wide)
-    target = dot(hi, coret) + dot(lo, coret)
+    target = dot(hi, core, NT) + dot(lo, core, NT)
     pair = 2 * SLOT
     row = lax.broadcasted_iota(jnp.int32, (pair, pair), 0) // SLOT
     col = lax.broadcasted_iota(jnp.int32, (pair, pair), 1) // SLOT
@@ -207,7 +210,7 @@
         compiler_params=params(16),
         cost_estimate=cost(4.8),
         name="procrustes",
-    )(*parts, weights, core, core.T, *([] if masked is None else [masked]))
+    )(*parts, weights, core, *([] if masked is None else [masked]))
 
 
 def rows_body(rot_ref, proj_ref, out_ref):
@@ -272,6 +275,10 @@
     return lax.optimization_barrier((first, then))
 
 
+def cut(a, rows):
+    return jnp.split(a, a.shape[0] // rows, axis=0)
+
+
 def per_device(visits, tile_pattern, counts, codes_t, core, patient_weights):
     npat = visits.shape[0]
     block = codes_t.shape[0]
@@ -286,16 +293,23 @@
     masked, back = tie(masked, one[1])
     one = (one[0], back)
     two = step(*one)
-    proj0 = project([codes_t, *one, *two], masked, split=True)
-    core0 = proj0[0] + to_core(proj0[1])
-    tot0 = core0 + to_x(core0)
     three = step(*two)
-    four = step(three[0][:half], three[1][half:])
-    proj1 = project([*three, *four], masked, split=True)
-    core1 = proj1[0] + to_core(proj1[1])
-    tot1 = core1 + to_x(core1)
-    parts = [tot0, to_core(tot0), tot1, to_core(tot1)]
-    plan = (((0, -1, 1, -2, 2), True), ((-3, 3, 4), True),)
+    four = (lax.ppermute(three[1], "subj", BACK),)
+    cuts0 = (5 * half,)
+    sums0 = [m + to_core(t) for m, t in zip(*project([codes_t, *one, *two], masked, cuts0))]
+    from0 = [to_x(s) for s in sums0]
+    cuts1 = (2 * half,)
+    sums1 = [m + to_core(t) for m, t in zip(*project([*three], masked, cuts1))]
+    from1 = [to_x(s) for s in sums1]
+    sums2 = project([*four], masked)
+    sums2 = sums2 + to_core(sums2)
+    sums2, from1 = tie(sums2, from1)
+    sums0 = [s + f for s, f in zip(sums0, from0)]
+    sums1 = [s + f for s, f in zip(sums1, from1)]
+    back0 = [to_core(p) for s in sums0 for p in cut(s, half)]
+    back1 = [to_core(s) for s in sums1]
+    parts = [*sums0, *back0, *sums1, *back1, sums2, to_x(sums2)]
+    plan = (((0, -1, 1, -2, 2), cuts0, (half,) * 5), ((-3, 3), cuts1, cuts1), ((4,), (), ()))
     wt, rot, proj, there2, there3, near, own = procrustes(
         parts, plan, patient_weights, core, block, masked
     )

time: 61.2 us -> 60.9 us (level)
  waiting for transfers between devices: 23 us -> 20.3 us
  starting transfers between devices: 23.6 us -> 25.3 us
  Pallas kernels: 9.16 us -> 9.96 us
    ppermute x6 -> x13, starting transfers between devices: 3.5 us -> 7.83 us  [the longest x1 1.62 us: per_device(): four = (lax.ppermute(three[1], 'subj', BACK),)]
    ppermute x1, waiting for transfers between devices: 5.79 us -> 3.86 us  [per_device(): far2 = z2((here2 + got2.astype(F32)).astype(BF16)).astype(F32)]
    ppermute x1, waiting for transfers between devices: 0.01 us -> 1.84 us  [per_device(): far3 = z3((here3 + got3.astype(F32)).astype(BF16)).astype(F32)]
    ppermute x4 -> x3, starting transfers between devices: 8.22 us -> 6.6 us  [step(): lax.ppermute(back, 'subj', BACK)]
    ppermute x6 -> x13, waiting for transfers between devices: 5.71 us -> 4.71 us  [the longest x1 1.24 us: per_device(): sums1 = [m + to_core(t) for m, t in zip(*project([*three], masked, cuts1))]]
    ppermute x4 -> x3, waiting for transfers between devices: 1.7 us -> 0.82 us  [step(): lax.ppermute(ahead, 'subj', AHEAD)]
    pallas_call x2 -> x3, Pallas kernels: 1.96 us -> 2.8 us  [project(): pl.pallas_call(functools.partial(project_body, len(blocks), cuts), out_sh...]
    ppermute x4 -> x3, waiting for transfers between devices: 6.43 us -> 5.75 us  [step(): lax.ppermute(back, 'subj', BACK)]
  transfers between devices with their start and end apart: 22 -> 27, of which waited for: 10 -> 13; matrix products, arithmetic and copies ran while one was open for 2% -> 2% of each run, Pallas kernels for 7% -> 8%
where the time goes in v5:
time: 60.9 us; the launch traced here: 60.7 us
  starting transfers between devices  25.3 us (42%)
  waiting for transfers between devices  20.3 us (33%)
  Pallas kernels  9.96 us (16%)
  local copies, waits for them, and re-layouts  2.6 us (4%)
  other arithmetic  1.7 us (3%)
  between operations  0.84 us (1%)
    ppermute x3, starting transfers between devices, step(): lax.ppermute(back, 'subj', BACK)  6.6 us
    ppermute x3, waiting for transfers between devices, step(): lax.ppermute(back, 'subj', BACK)  5.75 us
    pallas_call x1, Pallas kernels, procrustes(): pl.pallas_call(functools.partial(procrustes_body, block, plan), out_shape...  4.84 us
    ppermute x1, waiting for transfers between devices, per_device(): far2 = z2((here2 + got2.astype(F32)).astype(BF16)).astype(F32)  3.86 us
    ppermute x1, waiting for transfers between devices, per_device(): got2, own = tie(y(there2), own)  3.3 us
    pallas_call x3, Pallas kernels, project(): pl.pallas_call(functools.partial(project_body, len(blocks), cuts), out_sh...  2.8 us
    unnamed x10, local copies, waits for them, and re-layouts  2.31 us
    ppermute x1, starting transfers between devices, per_device(): far2 = z2((here2 + got2.astype(F32)).astype(BF16)).astype(F32)  2.18 us
  transfers between devices with their start and end apart: 27, of which 13 were waited for; matrix products, arithmetic and copies ran while one was open for 2% of the time, Pallas kernels for 8%

profile of v5, /device:TPU:0, one launch (start us, length us, event | category | flops | bytes accessed | tf_op | source)
XLA Modules:
  0.0 60.7 jit_solution(7264452466429934160)
XLA Ops:
  0.6 3.0 %collective-permute-start.1 = (bf16[32,2560]{1,0:T(8,128)(2,1)}, bf16[32,2560]{1,0:T(8,128)(2,1)S(1)}, u32[]{:S(2)}, u32[]{:S(2)}) collective-permute-start(bf16[32,2560]{1,0:T(8,128)(2,1)} %refs_0_.1), channel_id=1, source_target_pairs={{8,0},{16,8},{24,16},{28,24},{20,28},{12,20},{4,12},{0,4},{9,1},{1... | collective-permute-start | bytes 491528 | tf_op jit(solution)/shard_map/ppermute | solution.py:289
  3.7 0.1 collective-permute-start
  3.8 0.7 %convert_element_type.27 = bf16[8,20]{1,0:T(8,128)(2,1)S(1)} convert(s32[8,20]{1,0:T(8,128)} %param.7) | non-fusion elementwise | flops 160 | bytes 960 | tf_op jit(solution)/shard_map/convert_element_type | solution.py:76
  4.5 0.1 copy.8
  4.6 0.1 broadcast_bitcast_fusion
  4.7 0.1 copy.9.gate_ref
  4.7 0.0 copy-start
  4.8 1.6 %copy-done = bf16[8,56,2560]{2,1,0:T(8,128)(2,1)S(1)} copy-done((bf16[8,56,2560]{2,1,0:T(8,128)(2,1)S(1)}, bf16[8,56,2560]{2,1,0:T(8,128)(2,1)}, u32[]{:S(2)}) %copy-start) | copy-done | bytes 2293784
  6.4 0.7 %copy-done.4 = s32[8]{0:T(128)S(1)} copy-done((s32[8]{0:T(128)S(1)}, s32[8]{0:T(128)}, u32[]{:S(2)}) %copy-start.4) | copy-done | bytes 56
  7.0 1.1 %mask_visits.1.refs_5_.refs_2_.refs_1_.refs_12_.masked_ref = bf16[512,2560]{1,0:T(8,128)(2,1)S(1)} custom-call(s32[8]{0:T(128)S(1)} %copy-done.4, bf16[8,1,2560]{2,1,0:T(2,128)(2,1)S(1)} %copy.9.gate_ref, bf16[8,56,2560]{2,1,0:T(8,128)(2,1)S(1)} %copy-done), custom_call_target="tpu_custom_call" | custom-call | tf_op jit(solution)/shard_map/mask_visits/pallas_call | solution.py:77
  8.2 0.0 collective-permute-done.1.refs_2_
  8.2 2.0 %collective-permute-start.3 = (bf16[32,2560]{1,0:T(8,128)(2,1)S(1)}, bf16[32,2560]{1,0:T(8,128)(2,1)S(1)}, u32[]{:S(2)}, u32[]{:S(2)}) collective-permute-start(bf16[32,2560]{1,0:T(8,128)(2,1)S(1)} %collective-permute-done.1.refs_2_), channel_id=1, source_target_pairs={{8,0},{16,8},{24,16},{28,24},{20,28},{12,20},{4,12},{0,4},{9,1},{1... | collective-permute-start | bytes 491528 | tf_op jit(solution)/shard_map/ppermute | solution.py:289
  10.2 0.0 collective-permute-done.refs_1_
  10.2 0.1 collective-permute-start.2
  10.3 3.6 %collective-permute-done.3.refs_4_ = bf16[32,2560]{1,0:T(8,128)(2,1)S(1)} collective-permute-done((bf16[32,2560]{1,0:T(8,128)(2,1)S(1)}, bf16[32,2560]{1,0:T(8,128)(2,1)S(1)}, u32[]{:S(2)}, u32[]{:S(2)}) %collective-permute-start.3) | collective-permute-done | bytes 163872 | tf_op jit(solution)/shard_map/ppermute | solution.py:289
  13.9 1.6 %collective-permute-start.12 = (bf16[32,2560]{1,0:T(8,128)(2,1)S(1)}, bf16[32,2560]{1,0:T(8,128)(2,1)S(1)}, u32[]{:S(2)}, u32[]{:S(2)}) collective-permute-start(bf16[32,2560]{1,0:T(8,128)(2,1)S(1)} %collective-permute-done.3.refs_4_), channel_id=1, source_target_pairs={{8,0},{16,8},{24,16},{28,24},{20,28},{12,20},{4,12},{0,4},{9,1},{1... | collective-permute-start | bytes 491528 | tf_op jit(solution)/shard_map/ppermute | solution.py:289
  15.5 0.0 collective-permute-done.2.refs_3_
  15.5 1.0 %project.3 = (f32[80,512]{1,0:T(8,128)S(1)}, f32[80,512]{1,0:T(8,128)S(1)}) custom-call(bf16[32,2560]{1,0:T(8,128)(2,1)S(1)} %copy-done.1, bf16[32,2560]{1,0:T(8,128)(2,1)S(1)} %collective-permute-done.refs_1_, bf16[32,2560]{1,0:T(8,128)(2,1)S(1)} %collective-permute-done.1.refs_2_, bf16[32,2560]{1,0:T(8,128)(2,1)S(1)} %collective-permute-done.2.refs_3_, ...), custom_call_target="tpu_custom_call" | custom-call | tf_op jit(solution)/shard_map/project/pallas_call | solution.py:114
  16.6 0.1 collective-permute-start.4
  16.7 0.5 collective-permute-start.11
  17.1 2.1 %collective-permute-done.12.refs_1_ = bf16[32,2560]{1,0:T(8,128)(2,1)S(1)} collective-permute-done((bf16[32,2560]{1,0:T(8,128)(2,1)S(1)}, bf16[32,2560]{1,0:T(8,128)(2,1)S(1)}, u32[]{:S(2)}, u32[]{:S(2)}) %collective-permute-start.12) | collective-permute-done | bytes 163872 | tf_op jit(solution)/shard_map/ppermute | solution.py:289
  19.2 1.6 %collective-permute-start.14 = (bf16[32,2560]{1,0:T(8,128)(2,1)S(1)}, bf16[32,2560]{1,0:T(8,128)(2,1)S(1)}, u32[]{:S(2)}, u32[]{:S(2)}) collective-permute-start(bf16[32,2560]{1,0:T(8,128)(2,1)S(1)} %collective-permute-done.12.refs_1_), channel_id=1, source_target_pairs={{8,0},{16,8},{24,16},{28,24},{20,28},{12,20},{4,12},{0,4},{9,1},{1... | collective-permute-start | bytes 491528 | tf_op jit(solution)/shard_map/ppermute | solution.py:297
  20.9 0.0 collective-permute-done.4
  20.9 1.6 %collective-permute-start.5 = (f32[80,512]{1,0:T(8,128)S(1)}, f32[80,512]{1,0:T(8,128)S(1)}, u32[]{:S(2)}, u32[]{:S(2)}) collective-permute-start(f32[80,512]{1,0:T(8,128)S(1)} %add.36), channel_id=1, source_target_pairs={{0,2},{1,3},{2,0},{3,1},{4,6},{5,7},{6,4},{7,5},{8,10},{9,11},{10,... | collective-permute-start | bytes 491528 | tf_op jit(solution)/shard_map/ppermute | solution.py:300
  22.4 0.8 %collective-permute-done.11.refs_0_ = bf16[32,2560]{1,0:T(8,128)(2,1)S(1)} collective-permute-done((bf16[32,2560]{1,0:T(8,128)(2,1)S(1)}, bf16[32,2560]{1,0:T(8,128)(2,1)S(1)}, u32[]{:S(2)}, u32[]{:S(2)}) %collective-permute-start.11) | collective-permute-done | bytes 163872 | tf_op jit(solution)/shard_map/ppermute | solution.py:289
  23.3 0.9 %project.4 = (f32[32,512]{1,0:T(8,128)S(1)}, f32[32,512]{1,0:T(8,128)S(1)}) custom-call(bf16[32,2560]{1,0:T(8,128)(2,1)S(1)} %collective-permute-done.11.refs_0_, bf16[32,2560]{1,0:T(8,128)(2,1)S(1)} %collective-permute-done.12.refs_1_, bf16[512,2560]{1,0:T(8,128)(2,1)S(1)} %mask_visits.1.refs_5_.refs_2_.refs_1_.refs_12_.masked_ref), custom_call_target="tpu_custom_call" | custom-call | tf_op jit(solution)/shard_map/project/pallas_call | solution.py:114
  24.2 0.0 copy-start.2
  24.2 0.0 copy-start.3
  24.2 0.1 collective-permute-start.13
  24.3 1.2 %collective-permute-done.13 = f32[32,512]{1,0:T(8,128)S(1)} collective-permute-done((f32[32,512]{1,0:T(8,128)S(1)}, f32[32,512]{1,0:T(8,128)S(1)}, u32[]{:S(2)}, u32[]{:S(2)}) %collective-permute-start.13) | collective-permute-done | bytes 65568 | tf_op jit(solution)/shard_map/ppermute | solution.py:302
  25.6 1.6 %collective-permute-start.16 = (f32[32,512]{1,0:T(8,128)S(1)}, f32[32,512]{1,0:T(8,128)S(1)}, u32[]{:S(2)}, u32[]{:S(2)}) collective-permute-start(f32[32,512]{1,0:T(8,128)S(1)} %add.38), channel_id=1, source_target_pairs={{0,2},{1,3},{2,0},{3,1},{4,6},{5,7},{6,4},{7,5},{8,10},{9,11},{10,... | collective-permute-start | bytes 196616 | tf_op jit(solution)/shard_map/ppermute | solution.py:303
  27.1 0.8 %project.5 = f32[32,512]{1,0:T(8,128)S(1)} custom-call(bf16[32,2560]{1,0:T(8,128)(2,1)S(1)} %collective-permute-done.14.refs_0_, bf16[512,2560]{1,0:T(8,128)(2,1)S(1)} %mask_visits.1.refs_5_.refs_2_.refs_1_.refs_12_.masked_ref), custom_call_target="tpu_custom_call" | custom-call | tf_op jit(solution)/shard_map/project/pallas_call | solution.py:114
  28.0 0.0 collective-permute-start.15
  28.0 0.0 collective-permute-done.5
  28.0 0.6 collective-permute-start.10
  28.6 0.1 collective-permute-start.6
  28.7 0.5 collective-permute-done.15
  29.2 0.6 %collective-permute-done.16 = f32[32,512]{1,0:T(8,128)S(1)} collective-permute-done((f32[32,512]{1,0:T(8,128)S(1)}, f32[32,512]{1,0:T(8,128)S(1)}, u32[]{:S(2)}, u32[]{:S(2)}) %collective-permute-start.16) | collective-permute-done | bytes 65568 | tf_op jit(solution)/shard_map/ppermute | solution.py:303
  29.9 0.1 collective-permute-start.17
  30.0 1.6 %collective-permute-start.18 = (f32[32,512]{1,0:T(8,128)S(1)}, f32[32,512]{1,0:T(8,128)S(1)}, u32[]{:S(2)}, u32[]{:S(2)}) collective-permute-start(f32[32,512]{1,0:T(8,128)S(1)} %add.39.refs_8_), channel_id=1, source_target_pairs={{0,2},{1,3},{2,0},{3,1},{4,6},{5,7},{6,4},{7,5},{8,10},{9,11},{10,... | collective-permute-start | bytes 196616 | tf_op jit(solution)/shard_map/ppermute | solution.py:311
  31.5 0.2 collective-permute-start.7
  31.7 0.3 collective-permute-start.8
  32.0 0.2 collective-permute-start.9
  32.2 0.5 collective-permute-done.7.refs_2_
  32.7 0.2 collective-permute-done.8.refs_3_
  32.9 0.3 collective-permute-done.9.refs_4_
  33.3 0.0 collective-permute-done.17.refs_7_
  33.3 1.2 %collective-permute-done.18.refs_9_ = f32[32,512]{1,0:T(8,128)S(1)} collective-permute-done((f32[32,512]{1,0:T(8,128)S(1)}, f32[32,512]{1,0:T(8,128)S(1)}, u32[]{:S(2)}, u32[]{:S(2)}) %collective-permute-start.18) | collective-permute-done | bytes 65568 | tf_op jit(solution)/shard_map/ppermute | solution.py:311
  34.5 4.8 %procrustes.1 = (bf16[256,512]{1,0:T(8,128)(2,1)S(1)}, f32[512,256]{1,0:T(8,128)S(1)}, f32[512,256]{1,0:T(8,128)S(1)}, bf16[32,2560]{1,0:T(8,128)(2,1)S(1)}, bf1...) custom-call(f32[80,512]{1,0:T(8,128)S(1)} %add.37.refs_0_, ...), custom_call_target="tpu_custom_call" | custom-call | bytes 17280000 | tf_op jit(solution)/shard_map/procrustes/pallas_call | solution.py:201
  39.3 1.6 %collective-permute-start.19 = (bf16[32,2560]{1,0:T(8,128)(2,1)S(1)}, bf16[32,2560]{1,0:T(8,128)(2,1)S(1)}, u32[]{:S(2)}, u32[]{:S(2)}) collective-permute-start(bf16[32,2560]{1,0:T(8,128)(2,1)S(1)} %get-tuple-element.33), channel_id=1, source_target_pairs={{0,4},{4,0},{8,12},{12,8},{16,20},{20,16},{24,28},{28,24},{1,5},{5... | collective-permute-start | bytes 491528 | tf_op jit(solution)/shard_map/ppermute | solution.py:321
  41.0 0.5 term.1
  41.5 0.5 collective-permute-start.22
  42.0 1.2 %collective-permute-start.24 = (bf16[32,2560]{1,0:T(8,128)(2,1)S(1)}, bf16[32,2560]{1,0:T(8,128)(2,1)S(1)}, u32[]{:S(2)}, u32[]{:S(2)}) collective-permute-start(bf16[32,2560]{1,0:T(8,128)(2,1)S(1)} %get-tuple-element.41), channel_id=1, source_target_pairs={{0,8},{4,12},{8,0},{12,4},{16,24},{20,28},{24,16},{28,20},{1,9},{5... | collective-permute-start | bytes 491528 | tf_op jit(solution)/shard_map/ppermute | solution.py:325
  43.2 3.3 %collective-permute-done.19 = bf16[32,2560]{1,0:T(8,128)(2,1)S(1)} collective-permute-done((bf16[32,2560]{1,0:T(8,128)(2,1)S(1)}, bf16[32,2560]{1,0:T(8,128)(2,1)S(1)}, u32[]{:S(2)}, u32[]{:S(2)}) %collective-permute-start.19) | collective-permute-done | bytes 163872 | tf_op jit(solution)/shard_map/ppermute | solution.py:321
  46.6 2.2 %collective-permute-start.21 = (bf16[32,2560]{1,0:T(8,128)(2,1)S(1)}, bf16[32,2560]{1,0:T(8,128)(2,1)S(1)}, u32[]{:S(2)}, u32[]{:S(2)}) collective-permute-start(bf16[32,2560]{1,0:T(8,128)(2,1)S(1)} %add_convert_fusion.1), channel_id=1, source_target_pairs={{0,16},{4,20},{8,24},{12,28},{16,0},{20,4},{24,8},{28,12},{1,17},{... | collective-permute-start | bytes 491528 | tf_op jit(solution)/shard_map/ppermute | solution.py:322
  48.7 1.0 %collective-permute-start.20 = (bf16[32,2560]{1,0:T(8,128)(2,1)S(1)}, bf16[32,2560]{1,0:T(8,128)(2,1)S(1)}, u32[]{:S(2)}, u32[]{:S(2)}) collective-permute-start(bf16[32,2560]{1,0:T(8,128)(2,1)S(1)} %get-tuple-element.35), channel_id=1, source_target_pairs={{0,8},{4,12},{8,0},{12,4},{16,24},{20,28},{24,16},{28,20},{1,9},{5... | collective-permute-start | bytes 491528 | tf_op jit(solution)/shard_map/ppermute | solution.py:327
  49.7 0.0 collective-permute-done.22
  49.8 1.6 %collective-permute-start.23 = (bf16[32,2560]{1,0:T(8,128)(2,1)S(1)}, bf16[32,2560]{1,0:T(8,128)(2,1)S(1)}, u32[]{:S(2)}, u32[]{:S(2)}) collective-permute-start(bf16[32,2560]{1,0:T(8,128)(2,1)S(1)} %add_convert_fusion), channel_id=1, source_target_pairs={{0,24},{4,28},{8,16},{12,20},{16,8},{20,12},{24,0},{28,4},{1,25},{... | collective-permute-start | bytes 491528 | tf_op jit(solution)/shard_map/ppermute | solution.py:324
  51.4 1.6 %collective-permute-start.25 = (f32[16,2560]{1,0:T(8,128)S(1)}, f32[16,2560]{1,0:T(8,128)S(1)}, u32[]{:S(2)}, u32[]{:S(2)}) collective-permute-start(f32[16,2560]{1,0:T(8,128)S(1)} %get-tuple-element.44), channel_id=1, source_target_pairs={{0,4},{4,0},{8,12},{12,8},{16,20},{20,16},{24,28},{28,24},{1,5},{5... | collective-permute-start | bytes 491528 | tf_op jit(solution)/shard_map/ppermute | solution.py:326
  53.0 0.4 collective-permute-start.26
  53.5 0.7 %patient_rows.1 = f32[8,256]{1,0:T(8,128)} custom-call(f32[512,256]{1,0:T(8,128)S(1)} %get-tuple-element.42.rot_ref, f32[512,256]{1,0:T(8,128)S(1)} %get-tuple-element.43.proj_ref), custom_call_target="tpu_custom_call" | custom-call | tf_op jit(solution)/shard_map/patient_rows/pallas_call | solution.py:223
  54.2 3.9 %collective-permute-done.21 = bf16[32,2560]{1,0:T(8,128)(2,1)S(1)} collective-permute-done((bf16[32,2560]{1,0:T(8,128)(2,1)S(1)}, bf16[32,2560]{1,0:T(8,128)(2,1)S(1)}, u32[]{:S(2)}, u32[]{:S(2)}) %collective-permute-start.21) | collective-permute-done | bytes 163872 | tf_op jit(solution)/shard_map/ppermute | solution.py:322
  58.0 1.8 %collective-permute-done.23 = bf16[32,2560]{1,0:T(8,128)(2,1)S(1)} collective-permute-done((bf16[32,2560]{1,0:T(8,128)(2,1)S(1)}, bf16[32,2560]{1,0:T(8,128)(2,1)S(1)}, u32[]{:S(2)}, u32[]{:S(2)}) %collective-permute-start.23) | collective-permute-done | bytes 163872 | tf_op jit(solution)/shard_map/ppermute | solution.py:324
  59.9 0.8 %maximum_add_fusion = f32[32,2560]{1,0:T(8,128)} fusion(f32[16,2560]{1,0:T(8,128)S(1)} %collective-permute-done.26, f32[16,2560]{1,0:T(8,128)S(1)} %collective-permute-done.25, bf16[32,2560]{1,0:T(8,128)(2,1)S(1)} %collective-permute-done.23, bf16[32,2560]{1,0:T(8,128)(2,1)S(1)} %collective-permute-done.21, f32[32,2560]{1,0:T(8,128)S(1)} %get-tuple-element.32, ...), kind=kLoop, calls=%fused_computation | loop fusion | flops 655360 | bytes 1474560 | tf_op jit(solution)/shard_map/add | solution.py:328
  (22 shorter events, 0.3 us)
Async XLA Ops:
  0.6 14.9 %copy-start.1 = (bf16[32,2560]{1,0:T(8,128)(2,1)S(1)}, bf16[32,2560]{1,0:T(8,128)(2,1)}, u32[]{:S(2)}) copy-start(bf16[32,2560]{1,0:T(8,128)(2,1)} %refs_0_.1) | copy-start | bytes 491524
  0.6 7.6 %collective-permute-start.1 = (bf16[32,2560]{1,0:T(8,128)(2,1)}, bf16[32,2560]{1,0:T(8,128)(2,1)S(1)}, u32[]{:S(2)}, u32[]{:S(2)}) collective-permute-start(bf16[32,2560]{1,0:T(8,128)(2,1)} %refs_0_.1), channel_id=1, source_target_pairs={{8,0},{16,8},{24,16},{28,24},{20,28},{12,20},{4,12},{0,4},{9,1},{1... | collective-permute-start | bytes 491528 | tf_op jit(solution)/shard_map/ppermute | solution.py:289
  3.7 6.5 %collective-permute-start = (bf16[32,2560]{1,0:T(8,128)(2,1)}, bf16[32,2560]{1,0:T(8,128)(2,1)S(1)}, u32[]{:S(2)}, u32[]{:S(2)}) collective-permute-start(bf16[32,2560]{1,0:T(8,128)(2,1)} %refs_0_.1), channel_id=1, source_target_pairs={{0,8},{8,16},{16,24},{24,28},{28,20},{20,12},{12,4},{4,0},{1,9},{9... | collective-permute-start | bytes 491528 | tf_op jit(solution)/shard_map/ppermute | solution.py:289
  4.7 1.6 %copy-start = (bf16[8,56,2560]{2,1,0:T(8,128)(2,1)S(1)}, bf16[8,56,2560]{2,1,0:T(8,128)(2,1)}, u32[]{:S(2)}) copy-start(bf16[8,56,2560]{2,1,0:T(8,128)(2,1)} %visits_ref.1) | copy-start | bytes 6881284
  6.4 0.7 %copy-start.4 = (s32[8]{0:T(128)S(1)}, s32[8]{0:T(128)}, u32[]{:S(2)}) copy-start(s32[8]{0:T(128)} %counts_ref.1) | copy-start | bytes 100
  8.2 5.7 %collective-permute-start.3 = (bf16[32,2560]{1,0:T(8,128)(2,1)S(1)}, bf16[32,2560]{1,0:T(8,128)(2,1)S(1)}, u32[]{:S(2)}, u32[]{:S(2)}) collective-permute-start(bf16[32,2560]{1,0:T(8,128)(2,1)S(1)} %collective-permute-done.1.refs_2_), channel_id=1, source_target_pairs={{8,0},{16,8},{24,16},{28,24},{20,28},{12,20},{4,12},{0,4},{9,1},{1... | collective-permute-start | bytes 491528 | tf_op jit(solution)/shard_map/ppermute | solution.py:289
  10.2 5.4 %collective-permute-start.2 = (bf16[32,2560]{1,0:T(8,128)(2,1)S(1)}, bf16[32,2560]{1,0:T(8,128)(2,1)S(1)}, u32[]{:S(2)}, u32[]{:S(2)}) collective-permute-start(bf16[32,2560]{1,0:T(8,128)(2,1)S(1)} %collective-permute-done.refs_1_), channel_id=1, source_target_pairs={{0,8},{8,16},{16,24},{24,28},{28,20},{20,12},{12,4},{4,0},{1,9},{9... | collective-permute-start | bytes 491528 | tf_op jit(solution)/shard_map/ppermute | solution.py:289
  13.9 5.3 %collective-permute-start.12 = (bf16[32,2560]{1,0:T(8,128)(2,1)S(1)}, bf16[32,2560]{1,0:T(8,128)(2,1)S(1)}, u32[]{:S(2)}, u32[]{:S(2)}) collective-permute-start(bf16[32,2560]{1,0:T(8,128)(2,1)S(1)} %collective-permute-done.3.refs_4_), channel_id=1, source_target_pairs={{8,0},{16,8},{24,16},{28,24},{20,28},{12,20},{4,12},{0,4},{9,1},{1... | collective-permute-start | bytes 491528 | tf_op jit(solution)/shard_map/ppermute | solution.py:289
  16.6 4.3 %collective-permute-start.4 = (f32[80,512]{1,0:T(8,128)S(1)}, f32[80,512]{1,0:T(8,128)S(1)}, u32[]{:S(2)}, u32[]{:S(2)}) collective-permute-start(f32[80,512]{1,0:T(8,128)S(1)} %get-tuple-element.26), channel_id=1, source_target_pairs={{0,1},{1,0},{2,3},{3,2},{4,5},{5,4},{6,7},{7,6},{8,9},{9,8},{10,11... | collective-permute-start | bytes 491528 | tf_op jit(solution)/shard_map/ppermute | solution.py:299
  16.7 6.6 %collective-permute-start.11 = (bf16[32,2560]{1,0:T(8,128)(2,1)S(1)}, bf16[32,2560]{1,0:T(8,128)(2,1)S(1)}, u32[]{:S(2)}, u32[]{:S(2)}) collective-permute-start(bf16[32,2560]{1,0:T(8,128)(2,1)S(1)} %collective-permute-done.2.refs_3_), channel_id=1, source_target_pairs={{0,8},{8,16},{16,24},{24,28},{28,20},{20,12},{12,4},{4,0},{1,9},{9... | collective-permute-start | bytes 491528 | tf_op jit(solution)/shard_map/ppermute | solution.py:289
  19.2 7.9 %collective-permute-start.14 = (bf16[32,2560]{1,0:T(8,128)(2,1)S(1)}, bf16[32,2560]{1,0:T(8,128)(2,1)S(1)}, u32[]{:S(2)}, u32[]{:S(2)}) collective-permute-start(bf16[32,2560]{1,0:T(8,128)(2,1)S(1)} %collective-permute-done.12.refs_1_), channel_id=1, source_target_pairs={{8,0},{16,8},{24,16},{28,24},{20,28},{12,20},{4,12},{0,4},{9,1},{1... | collective-permute-start | bytes 491528 | tf_op jit(solution)/shard_map/ppermute | solution.py:297
  20.9 7.1 %collective-permute-start.5 = (f32[80,512]{1,0:T(8,128)S(1)}, f32[80,512]{1,0:T(8,128)S(1)}, u32[]{:S(2)}, u32[]{:S(2)}) collective-permute-start(f32[80,512]{1,0:T(8,128)S(1)} %add.36), channel_id=1, source_target_pairs={{0,2},{1,3},{2,0},{3,1},{4,6},{5,7},{6,4},{7,5},{8,10},{9,11},{10,... | collective-permute-start | bytes 491528 | tf_op jit(solution)/shard_map/ppermute | solution.py:300
  24.2 10.3 %copy-start.2 = (bf16[256,256]{1,0:T(8,128)(2,1)S(1)}, bf16[256,256]{1,0:T(8,128)(2,1)}, u32[]{:S(2)}) copy-start(bf16[256,256]{1,0:T(8,128)(2,1)} %refs_11_.1) | copy-start | bytes 393220
  24.2 10.3 %copy-start.3 = (f32[8,256]{1,0:T(8,128)S(1)}, f32[8,256]{1,0:T(8,128)}, u32[]{:S(2)}) copy-start(f32[8,256]{1,0:T(8,128)} %refs_10_.1) | copy-start | bytes 24580
  24.2 1.3 %collective-permute-start.13 = (f32[32,512]{1,0:T(8,128)S(1)}, f32[32,512]{1,0:T(8,128)S(1)}, u32[]{:S(2)}, u32[]{:S(2)}) collective-permute-start(f32[32,512]{1,0:T(8,128)S(1)} %get-tuple-element.28), channel_id=1, source_target_pairs={{0,1},{1,0},{2,3},{3,2},{4,5},{5,4},{6,7},{7,6},{8,9},{9,8},{10,11... | collective-permute-start | bytes 196616 | tf_op jit(solution)/shard_map/ppermute | solution.py:302
  25.6 4.3 %collective-permute-start.16 = (f32[32,512]{1,0:T(8,128)S(1)}, f32[32,512]{1,0:T(8,128)S(1)}, u32[]{:S(2)}, u32[]{:S(2)}) collective-permute-start(f32[32,512]{1,0:T(8,128)S(1)} %add.38), channel_id=1, source_target_pairs={{0,2},{1,3},{2,0},{3,1},{4,6},{5,7},{6,4},{7,5},{8,10},{9,11},{10,... | collective-permute-start | bytes 196616 | tf_op jit(solution)/shard_map/ppermute | solution.py:303
  28.0 1.3 %collective-permute-start.15 = (f32[32,512]{1,0:T(8,128)S(1)}, f32[32,512]{1,0:T(8,128)S(1)}, u32[]{:S(2)}, u32[]{:S(2)}) collective-permute-start(f32[32,512]{1,0:T(8,128)S(1)} %project.5), channel_id=1, source_target_pairs={{0,1},{1,0},{2,3},{3,2},{4,5},{5,4},{6,7},{7,6},{8,9},{9,8},{10,11... | collective-permute-start | bytes 196616 | tf_op jit(solution)/shard_map/ppermute | solution.py:305
  28.0 3.7 %collective-permute-start.10 = (f32[16,512]{1,0:T(8,128)S(1)}, f32[16,512]{1,0:T(8,128)S(1)}, u32[]{:S(2)}, u32[]{:S(2)}) collective-permute-start(f32[16,512]{1,0:T(8,128)S(1)} %get-tuple-element.46), channel_id=1, source_target_pairs={{0,1},{1,0},{2,3},{3,2},{4,5},{5,4},{6,7},{7,6},{8,9},{9,8},{10,11... | collective-permute-start | bytes 98312 | tf_op jit(solution)/shard_map/ppermute | solution.py:309
  28.6 3.4 %collective-permute-start.6 = (f32[16,512]{1,0:T(8,128)S(1)}, f32[16,512]{1,0:T(8,128)S(1)}, u32[]{:S(2)}, u32[]{:S(2)}) collective-permute-start(f32[16,512]{1,0:T(8,128)S(1)} %get-tuple-element.50), channel_id=1, source_target_pairs={{0,1},{1,0},{2,3},{3,2},{4,5},{5,4},{6,7},{7,6},{8,9},{9,8},{10,11... | collective-permute-start | bytes 98312 | tf_op jit(solution)/shard_map/ppermute | solution.py:309
  29.9 3.4 %collective-permute-start.17 = (f32[32,512]{1,0:T(8,128)S(1)}, f32[32,512]{1,0:T(8,128)S(1)}, u32[]{:S(2)}, u32[]{:S(2)}) collective-permute-start(f32[32,512]{1,0:T(8,128)S(1)} %add.40.refs_6_), channel_id=1, source_target_pairs={{0,1},{1,0},{2,3},{3,2},{4,5},{5,4},{6,7},{7,6},{8,9},{9,8},{10,11... | collective-permute-start | bytes 196616 | tf_op jit(solution)/shard_map/ppermute | solution.py:310
  30.0 4.5 %collective-permute-start.18 = (f32[32,512]{1,0:T(8,128)S(1)}, f32[32,512]{1,0:T(8,128)S(1)}, u32[]{:S(2)}, u32[]{:S(2)}) collective-permute-start(f32[32,512]{1,0:T(8,128)S(1)} %add.39.refs_8_), channel_id=1, source_target_pairs={{0,2},{1,3},{2,0},{3,1},{4,6},{5,7},{6,4},{7,5},{8,10},{9,11},{10,... | collective-permute-start | bytes 196616 | tf_op jit(solution)/shard_map/ppermute | solution.py:311
  31.5 1.2 %collective-permute-start.7 = (f32[16,512]{1,0:T(8,128)S(1)}, f32[16,512]{1,0:T(8,128)S(1)}, u32[]{:S(2)}, u32[]{:S(2)}) collective-permute-start(f32[16,512]{1,0:T(8,128)S(1)} %get-tuple-element.49), channel_id=1, source_target_pairs={{0,1},{1,0},{2,3},{3,2},{4,5},{5,4},{6,7},{7,6},{8,9},{9,8},{10,11... | collective-permute-start | bytes 98312 | tf_op jit(solution)/shard_map/ppermute | solution.py:309
  31.7 1.2 %collective-permute-start.8 = (f32[16,512]{1,0:T(8,128)S(1)}, f32[16,512]{1,0:T(8,128)S(1)}, u32[]{:S(2)}, u32[]{:S(2)}) collective-permute-start(f32[16,512]{1,0:T(8,128)S(1)} %get-tuple-element.48), channel_id=1, source_target_pairs={{0,1},{1,0},{2,3},{3,2},{4,5},{5,4},{6,7},{7,6},{8,9},{9,8},{10,11... | collective-permute-start | bytes 98312 | tf_op jit(solution)/shard_map/ppermute | solution.py:309
  32.0 1.2 %collective-permute-start.9 = (f32[16,512]{1,0:T(8,128)S(1)}, f32[16,512]{1,0:T(8,128)S(1)}, u32[]{:S(2)}, u32[]{:S(2)}) collective-permute-start(f32[16,512]{1,0:T(8,128)S(1)} %get-tuple-element.47), channel_id=1, source_target_pairs={{0,1},{1,0},{2,3},{3,2},{4,5},{5,4},{6,7},{7,6},{8,9},{9,8},{10,11... | collective-permute-start | bytes 98312 | tf_op jit(solution)/shard_map/ppermute | solution.py:309
  39.3 7.2 %collective-permute-start.19 = (bf16[32,2560]{1,0:T(8,128)(2,1)S(1)}, bf16[32,2560]{1,0:T(8,128)(2,1)S(1)}, u32[]{:S(2)}, u32[]{:S(2)}) collective-permute-start(bf16[32,2560]{1,0:T(8,128)(2,1)S(1)} %get-tuple-element.33), channel_id=1, source_target_pairs={{0,4},{4,0},{8,12},{12,8},{16,20},{20,16},{24,28},{28,24},{1,5},{5... | collective-permute-start | bytes 491528 | tf_op jit(solution)/shard_map/ppermute | solution.py:321
  41.5 8.2 %collective-permute-start.22 = (bf16[32,2560]{1,0:T(8,128)(2,1)S(1)}, bf16[32,2560]{1,0:T(8,128)(2,1)S(1)}, u32[]{:S(2)}, u32[]{:S(2)}) collective-permute-start(bf16[32,2560]{1,0:T(8,128)(2,1)S(1)} %get-tuple-element.39), channel_id=1, source_target_pairs={{0,4},{4,0},{8,12},{12,8},{16,20},{20,16},{24,28},{28,24},{1,5},{5... | collective-permute-start | bytes 491528 | tf_op jit(solution)/shard_map/ppermute | solution.py:323
  42.0 9.3 %collective-permute-start.24 = (bf16[32,2560]{1,0:T(8,128)(2,1)S(1)}, bf16[32,2560]{1,0:T(8,128)(2,1)S(1)}, u32[]{:S(2)}, u32[]{:S(2)}) collective-permute-start(bf16[32,2560]{1,0:T(8,128)(2,1)S(1)} %get-tuple-element.41), channel_id=1, source_target_pairs={{0,8},{4,12},{8,0},{12,4},{16,24},{20,28},{24,16},{28,20},{1,9},{5... | collective-permute-start | bytes 491528 | tf_op jit(solution)/shard_map/ppermute | solution.py:325
  46.6 11.5 %collective-permute-start.21 = (bf16[32,2560]{1,0:T(8,128)(2,1)S(1)}, bf16[32,2560]{1,0:T(8,128)(2,1)S(1)}, u32[]{:S(2)}, u32[]{:S(2)}) collective-permute-start(bf16[32,2560]{1,0:T(8,128)(2,1)S(1)} %add_convert_fusion.1), channel_id=1, source_target_pairs={{0,16},{4,20},{8,24},{12,28},{16,0},{20,4},{24,8},{28,12},{1,17},{... | collective-permute-start | bytes 491528 | tf_op jit(solution)/shard_map/ppermute | solution.py:322
  48.7 9.3 %collective-permute-start.20 = (bf16[32,2560]{1,0:T(8,128)(2,1)S(1)}, bf16[32,2560]{1,0:T(8,128)(2,1)S(1)}, u32[]{:S(2)}, u32[]{:S(2)}) collective-permute-start(bf16[32,2560]{1,0:T(8,128)(2,1)S(1)} %get-tuple-element.35), channel_id=1, source_target_pairs={{0,8},{4,12},{8,0},{12,4},{16,24},{20,28},{24,16},{28,20},{1,9},{5... | collective-permute-start | bytes 491528 | tf_op jit(solution)/shard_map/ppermute | solution.py:327
  49.8 10.1 %collective-permute-start.23 = (bf16[32,2560]{1,0:T(8,128)(2,1)S(1)}, bf16[32,2560]{1,0:T(8,128)(2,1)S(1)}, u32[]{:S(2)}, u32[]{:S(2)}) collective-permute-start(bf16[32,2560]{1,0:T(8,128)(2,1)S(1)} %add_convert_fusion), channel_id=1, source_target_pairs={{0,24},{4,28},{8,16},{12,20},{16,8},{20,12},{24,0},{28,4},{1,25},{... | collective-permute-start | bytes 491528 | tf_op jit(solution)/shard_map/ppermute | solution.py:324
  51.4 8.5 %collective-permute-start.25 = (f32[16,2560]{1,0:T(8,128)S(1)}, f32[16,2560]{1,0:T(8,128)S(1)}, u32[]{:S(2)}, u32[]{:S(2)}) collective-permute-start(f32[16,2560]{1,0:T(8,128)S(1)} %get-tuple-element.44), channel_id=1, source_target_pairs={{0,4},{4,0},{8,12},{12,8},{16,20},{20,16},{24,28},{28,24},{1,5},{5... | collective-permute-start | bytes 491528 | tf_op jit(solution)/shard_map/ppermute | solution.py:326
  53.0 6.8 %collective-permute-start.26 = (f32[16,2560]{1,0:T(8,128)S(1)}, f32[16,2560]{1,0:T(8,128)S(1)}, u32[]{:S(2)}, u32[]{:S(2)}) collective-permute-start(f32[16,2560]{1,0:T(8,128)S(1)} %get-tuple-element.45), channel_id=1, source_target_pairs={{0,4},{4,0},{8,12},{12,8},{16,20},{20,16},{24,28},{28,24},{1,5},{5... | collective-permute-start | bytes 491528 | tf_op jit(solution)/shard_map/ppermute | solution.py:326

commit v6 on v5

--- a/solution.py
+++ b/solution.py
@@ -8,6 +8,7 @@
 from jax.sharding import PartitionSpec as P
 
 NS_STEPS = 8
+HALF_ROOT = 0.5**0.5
 SLOT = 64
 BF16, F32 = jnp.bfloat16, jnp.float32
 FIRST = ((5,), (7,), (3,), (2,))
@@ -171,7 +172,7 @@
     for p in range(npat // 2):
         two = target[p * pair : (p + 1) * pair].reshape(2, SLOT, rank)
         total = jnp.sum(jnp.sum(two * two, axis=1, keepdims=True), axis=2, keepdims=True)
-        qs.append((two * lax.rsqrt(total + 1e-06)).reshape(pair, rank))
+        qs.append((two * (lax.rsqrt(total + 1e-06) * HALF_ROOT)).reshape(pair, rank))
     for step in range(NS_STEPS):
         halves = [split2(q) for q in qs]
         stacks = [jnp.concatenate(h, 0) for h in halves]
@@ -182,10 +183,10 @@
             dot(jnp.concatenate([g[0], g[0]], 1), k) + dot(g[1], h[0])
             for g, h, k in zip(grams, halves, stacks)
         ]
-        qs = [1.5 * q - 0.5 * x for q, x in zip(qs, prods)]
+        qs = [1.5 * q - x for q, x in zip(qs, prods)]
     q = jnp.concatenate(qs, 0)
     hi, lo = split2(q)
-    rotated = dot(hi, core) + dot(lo, core)
+    rotated = (dot(hi, core) + dot(lo, core)) * (2.0 * HALF_ROOT)
     rot_ref[...] = rotated
     wt_ref[...] = (rotated * wide).T.astype(jnp.bfloat16)
     if plan:
@@ -290,9 +291,9 @@
 
     masked = mask_visits(visits, tile_pattern, counts)
     one = step(codes_t, codes_t)
-    masked, back = tie(masked, one[1])
-    one = (one[0], back)
     two = step(*one)
+    masked, back = tie(masked, two[1])
+    two = (two[0], back)
     three = step(*two)
     four = (lax.ppermute(three[1], "subj", BACK),)
     cuts0 = (5 * half,)
@@ -323,7 +324,7 @@
     got3 = y(there3)
     far3 = z3((here3 + got3.astype(F32)).astype(BF16)).astype(F32)
     other = there0 + z1(near).astype(F32)
-    other = jnp.concatenate([y(p) for p in jnp.split(other, 2, axis=0)], 0)
+    other = y(other)
     own = z1(own).astype(F32)
     out = (((here0 + own) + far2) + far3) + other
     rows = patient_rows(rot, proj, npat)

time: 60.9 us -> 60.9 us (level)
    ppermute x2 -> x1, starting transfers between devices: 2.09 us -> 1.64 us  [per_device(): other = y(other)]
  transfers between devices with their start and end apart: 27 -> 26, of which waited for: 13 -> 13; matrix products, arithmetic and copies ran while one was open for 2% -> 2% of each run, Pallas kernels for 8% -> 8%
where the time goes in v6:
time: 60.9 us; the launch traced here: 60.7 us
  starting transfers between devices  24.7 us (41%)
  waiting for transfers between devices  20.9 us (34%)
  Pallas kernels  9.94 us (16%)
  local copies, waits for them, and re-layouts  2.57 us (4%)
  other arithmetic  1.7 us (3%)
  between operations  0.84 us (1%)
    ppermute x3, starting transfers between devices, step(): lax.ppermute(back, 'subj', BACK)  6.42 us
    ppermute x3, waiting for transfers between devices, step(): lax.ppermute(back, 'subj', BACK)  5.69 us
    pallas_call x1, Pallas kernels, procrustes(): pl.pallas_call(functools.partial(procrustes_body, block, plan), out_shape...  4.82 us
    ppermute x1, waiting for transfers between devices, per_device(): far2 = z2((here2 + got2.astype(F32)).astype(BF16)).astype(F32)  4.28 us
    ppermute x1, waiting for transfers between devices, per_device(): got2, own = tie(y(there2), own)  3.31 us
    pallas_call x3, Pallas kernels, project(): pl.pallas_call(functools.partial(project_body, len(blocks), cuts), out_sh...  2.8 us
    unnamed x10, local copies, waits for them, and re-layouts  2.31 us
    ppermute x1, starting transfers between devices, per_device(): far2 = z2((here2 + got2.astype(F32)).astype(BF16)).astype(F32)  2.17 us
  transfers between devices with their start and end apart: 26, of which 13 were waited for; matrix products, arithmetic and copies ran while one was open for 2% of the time, Pallas kernels for 8%

profile of v6, /device:TPU:0, one launch (start us, length us, event | category | flops | bytes accessed | tf_op | source)
XLA Modules:
  0.0 60.7 jit_solution(4772777517309181977)
XLA Ops:
  0.6 3.0 %collective-permute-start.1 = (bf16[32,2560]{1,0:T(8,128)(2,1)}, bf16[32,2560]{1,0:T(8,128)(2,1)S(1)}, u32[]{:S(2)}, u32[]{:S(2)}) collective-permute-start(bf16[32,2560]{1,0:T(8,128)(2,1)} %refs_0_.1), channel_id=1, source_target_pairs={{8,0},{16,8},{24,16},{28,24},{20,28},{12,20},{4,12},{0,4},{9,1},{1... | collective-permute-start | bytes 491528 | tf_op jit(solution)/shard_map/ppermute | solution.py:290
  3.7 0.1 collective-permute-start
  3.8 0.7 %convert_element_type.27 = bf16[8,20]{1,0:T(8,128)(2,1)S(1)} convert(s32[8,20]{1,0:T(8,128)} %param.7) | non-fusion elementwise | flops 160 | bytes 960 | tf_op jit(solution)/shard_map/convert_element_type | solution.py:77
  4.5 0.1 copy.8
  4.6 3.6 %collective-permute-done.1.refs_2_ = bf16[32,2560]{1,0:T(8,128)(2,1)S(1)} collective-permute-done((bf16[32,2560]{1,0:T(8,128)(2,1)}, bf16[32,2560]{1,0:T(8,128)(2,1)S(1)}, u32[]{:S(2)}, u32[]{:S(2)}) %collective-permute-start.1) | collective-permute-done | bytes 163872 | tf_op jit(solution)/shard_map/ppermute | solution.py:290
  8.1 1.7 %collective-permute-start.3 = (bf16[32,2560]{1,0:T(8,128)(2,1)S(1)}, bf16[32,2560]{1,0:T(8,128)(2,1)S(1)}, u32[]{:S(2)}, u32[]{:S(2)}) collective-permute-start(bf16[32,2560]{1,0:T(8,128)(2,1)S(1)} %collective-permute-done.1.refs_2_), channel_id=1, source_target_pairs={{8,0},{16,8},{24,16},{28,24},{20,28},{12,20},{4,12},{0,4},{9,1},{1... | collective-permute-start | bytes 491528 | tf_op jit(solution)/shard_map/ppermute | solution.py:290
  9.8 0.4 collective-permute-start.2
  10.2 0.1 broadcast_bitcast_fusion
  10.3 0.1 copy.9.gate_ref
  10.3 0.0 copy-start
  10.3 1.6 %copy-done = bf16[8,56,2560]{2,1,0:T(8,128)(2,1)S(1)} copy-done((bf16[8,56,2560]{2,1,0:T(8,128)(2,1)S(1)}, bf16[8,56,2560]{2,1,0:T(8,128)(2,1)}, u32[]{:S(2)}) %copy-start) | copy-done | bytes 2293784
  12.0 0.7 %copy-done.4 = s32[8]{0:T(128)S(1)} copy-done((s32[8]{0:T(128)S(1)}, s32[8]{0:T(128)}, u32[]{:S(2)}) %copy-start.4) | copy-done | bytes 56
  12.6 1.1 %mask_visits.1.refs_5_.refs_2_.refs_1_.refs_12_.masked_ref = bf16[512,2560]{1,0:T(8,128)(2,1)S(1)} custom-call(s32[8]{0:T(128)S(1)} %copy-done.4, bf16[8,1,2560]{2,1,0:T(2,128)(2,1)S(1)} %copy.9.gate_ref, bf16[8,56,2560]{2,1,0:T(8,128)(2,1)S(1)} %copy-done), custom_call_target="tpu_custom_call" | custom-call | tf_op jit(solution)/shard_map/mask_visits/pallas_call | solution.py:78
  13.8 1.7 %collective-permute-start.12 = (bf16[32,2560]{1,0:T(8,128)(2,1)S(1)}, bf16[32,2560]{1,0:T(8,128)(2,1)S(1)}, u32[]{:S(2)}, u32[]{:S(2)}) collective-permute-start(bf16[32,2560]{1,0:T(8,128)(2,1)S(1)} %collective-permute-done.3.refs_4_), channel_id=1, source_target_pairs={{8,0},{16,8},{24,16},{28,24},{20,28},{12,20},{4,12},{0,4},{9,1},{1... | collective-permute-start | bytes 491528 | tf_op jit(solution)/shard_map/ppermute | solution.py:290
  15.5 0.0 collective-permute-done.2.refs_3_
  15.5 1.0 %project.3 = (f32[80,512]{1,0:T(8,128)S(1)}, f32[80,512]{1,0:T(8,128)S(1)}) custom-call(bf16[32,2560]{1,0:T(8,128)(2,1)S(1)} %copy-done.1, bf16[32,2560]{1,0:T(8,128)(2,1)S(1)} %collective-permute-done.refs_1_, bf16[32,2560]{1,0:T(8,128)(2,1)S(1)} %collective-permute-done.1.refs_2_, bf16[32,2560]{1,0:T(8,128)(2,1)S(1)} %collective-permute-done.2.refs_3_, ...), custom_call_target="tpu_custom_call" | custom-call | tf_op jit(solution)/shard_map/project/pallas_call | solution.py:115
  16.6 0.1 collective-permute-start.4
  16.6 0.4 collective-permute-start.11
  17.0 2.1 %collective-permute-done.12.refs_1_ = bf16[32,2560]{1,0:T(8,128)(2,1)S(1)} collective-permute-done((bf16[32,2560]{1,0:T(8,128)(2,1)S(1)}, bf16[32,2560]{1,0:T(8,128)(2,1)S(1)}, u32[]{:S(2)}, u32[]{:S(2)}) %collective-permute-start.12) | collective-permute-done | bytes 163872 | tf_op jit(solution)/shard_map/ppermute | solution.py:290
  19.2 1.7 %collective-permute-start.14 = (bf16[32,2560]{1,0:T(8,128)(2,1)S(1)}, bf16[32,2560]{1,0:T(8,128)(2,1)S(1)}, u32[]{:S(2)}, u32[]{:S(2)}) collective-permute-start(bf16[32,2560]{1,0:T(8,128)(2,1)S(1)} %collective-permute-done.12.refs_1_), channel_id=1, source_target_pairs={{8,0},{16,8},{24,16},{28,24},{20,28},{12,20},{4,12},{0,4},{9,1},{1... | collective-permute-start | bytes 491528 | tf_op jit(solution)/shard_map/ppermute | solution.py:298
  20.8 0.0 collective-permute-done.4
  20.9 1.6 %collective-permute-start.5 = (f32[80,512]{1,0:T(8,128)S(1)}, f32[80,512]{1,0:T(8,128)S(1)}, u32[]{:S(2)}, u32[]{:S(2)}) collective-permute-start(f32[80,512]{1,0:T(8,128)S(1)} %add.36), channel_id=1, source_target_pairs={{0,2},{1,3},{2,0},{3,1},{4,6},{5,7},{6,4},{7,5},{8,10},{9,11},{10,... | collective-permute-start | bytes 491528 | tf_op jit(solution)/shard_map/ppermute | solution.py:301
  22.4 0.8 %collective-permute-done.11.refs_0_ = bf16[32,2560]{1,0:T(8,128)(2,1)S(1)} collective-permute-done((bf16[32,2560]{1,0:T(8,128)(2,1)S(1)}, bf16[32,2560]{1,0:T(8,128)(2,1)S(1)}, u32[]{:S(2)}, u32[]{:S(2)}) %collective-permute-start.11) | collective-permute-done | bytes 163872 | tf_op jit(solution)/shard_map/ppermute | solution.py:290
  23.2 0.9 %project.4 = (f32[32,512]{1,0:T(8,128)S(1)}, f32[32,512]{1,0:T(8,128)S(1)}) custom-call(bf16[32,2560]{1,0:T(8,128)(2,1)S(1)} %collective-permute-done.11.refs_0_, bf16[32,2560]{1,0:T(8,128)(2,1)S(1)} %collective-permute-done.12.refs_1_, bf16[512,2560]{1,0:T(8,128)(2,1)S(1)} %mask_visits.1.refs_5_.refs_2_.refs_1_.refs_12_.masked_ref), custom_call_target="tpu_custom_call" | custom-call | tf_op jit(solution)/shard_map/project/pallas_call | solution.py:115
  24.2 0.0 copy-start.2
  24.2 0.0 copy-start.3
  24.2 0.1 collective-permute-start.13
  24.3 1.2 %collective-permute-done.13 = f32[32,512]{1,0:T(8,128)S(1)} collective-permute-done((f32[32,512]{1,0:T(8,128)S(1)}, f32[32,512]{1,0:T(8,128)S(1)}, u32[]{:S(2)}, u32[]{:S(2)}) %collective-permute-start.13) | collective-permute-done | bytes 65568 | tf_op jit(solution)/shard_map/ppermute | solution.py:303
  25.5 1.6 %collective-permute-start.16 = (f32[32,512]{1,0:T(8,128)S(1)}, f32[32,512]{1,0:T(8,128)S(1)}, u32[]{:S(2)}, u32[]{:S(2)}) collective-permute-start(f32[32,512]{1,0:T(8,128)S(1)} %add.38), channel_id=1, source_target_pairs={{0,2},{1,3},{2,0},{3,1},{4,6},{5,7},{6,4},{7,5},{8,10},{9,11},{10,... | collective-permute-start | bytes 196616 | tf_op jit(solution)/shard_map/ppermute | solution.py:304
  27.1 0.8 %project.5 = f32[32,512]{1,0:T(8,128)S(1)} custom-call(bf16[32,2560]{1,0:T(8,128)(2,1)S(1)} %collective-permute-done.14.refs_0_, bf16[512,2560]{1,0:T(8,128)(2,1)S(1)} %mask_visits.1.refs_5_.refs_2_.refs_1_.refs_12_.masked_ref), custom_call_target="tpu_custom_call" | custom-call | tf_op jit(solution)/shard_map/project/pallas_call | solution.py:115
  27.9 0.0 collective-permute-start.15
  28.0 0.0 collective-permute-done.5
  28.0 0.6 collective-permute-start.10
  28.6 0.1 collective-permute-start.6
  28.7 0.5 collective-permute-done.15
  29.2 0.6 %collective-permute-done.16 = f32[32,512]{1,0:T(8,128)S(1)} collective-permute-done((f32[32,512]{1,0:T(8,128)S(1)}, f32[32,512]{1,0:T(8,128)S(1)}, u32[]{:S(2)}, u32[]{:S(2)}) %collective-permute-start.16) | collective-permute-done | bytes 65568 | tf_op jit(solution)/shard_map/ppermute | solution.py:304
  29.9 0.1 collective-permute-start.17
  30.0 1.6 %collective-permute-start.18 = (f32[32,512]{1,0:T(8,128)S(1)}, f32[32,512]{1,0:T(8,128)S(1)}, u32[]{:S(2)}, u32[]{:S(2)}) collective-permute-start(f32[32,512]{1,0:T(8,128)S(1)} %add.39.refs_8_), channel_id=1, source_target_pairs={{0,2},{1,3},{2,0},{3,1},{4,6},{5,7},{6,4},{7,5},{8,10},{9,11},{10,... | collective-permute-start | bytes 196616 | tf_op jit(solution)/shard_map/ppermute | solution.py:312
  31.5 0.2 collective-permute-start.7
  31.7 0.3 collective-permute-start.8
  32.0 0.0 collective-permute-done.6.refs_1_
  32.0 0.2 collective-permute-start.9
  32.2 0.5 collective-permute-done.7.refs_2_
  32.7 0.2 collective-permute-done.8.refs_3_
  32.9 0.3 collective-permute-done.9.refs_4_
  33.2 0.0 collective-permute-done.17.refs_7_
  33.2 1.2 %collective-permute-done.18.refs_9_ = f32[32,512]{1,0:T(8,128)S(1)} collective-permute-done((f32[32,512]{1,0:T(8,128)S(1)}, f32[32,512]{1,0:T(8,128)S(1)}, u32[]{:S(2)}, u32[]{:S(2)}) %collective-permute-start.18) | collective-permute-done | bytes 65568 | tf_op jit(solution)/shard_map/ppermute | solution.py:312
  34.5 4.8 %procrustes.1 = (bf16[256,512]{1,0:T(8,128)(2,1)S(1)}, f32[512,256]{1,0:T(8,128)S(1)}, f32[512,256]{1,0:T(8,128)S(1)}, bf16[32,2560]{1,0:T(8,128)(2,1)S(1)}, bf1...) custom-call(f32[80,512]{1,0:T(8,128)S(1)} %add.37.refs_0_, ...), custom_call_target="tpu_custom_call" | custom-call | bytes 17280000 | tf_op jit(solution)/shard_map/procrustes/pallas_call | solution.py:202
  39.3 1.6 %collective-permute-start.19 = (bf16[32,2560]{1,0:T(8,128)(2,1)S(1)}, bf16[32,2560]{1,0:T(8,128)(2,1)S(1)}, u32[]{:S(2)}, u32[]{:S(2)}) collective-permute-start(bf16[32,2560]{1,0:T(8,128)(2,1)S(1)} %get-tuple-element.33), channel_id=1, source_target_pairs={{0,4},{4,0},{8,12},{12,8},{16,20},{20,16},{24,28},{28,24},{1,5},{5... | collective-permute-start | bytes 491528 | tf_op jit(solution)/shard_map/ppermute | solution.py:322
  40.9 0.5 term.1
  41.4 0.5 collective-permute-start.22
  42.0 1.2 %collective-permute-start.24 = (bf16[32,2560]{1,0:T(8,128)(2,1)S(1)}, bf16[32,2560]{1,0:T(8,128)(2,1)S(1)}, u32[]{:S(2)}, u32[]{:S(2)}) collective-permute-start(bf16[32,2560]{1,0:T(8,128)(2,1)S(1)} %get-tuple-element.41), channel_id=1, source_target_pairs={{0,8},{4,12},{8,0},{12,4},{16,24},{20,28},{24,16},{28,20},{1,9},{5... | collective-permute-start | bytes 491528 | tf_op jit(solution)/shard_map/ppermute | solution.py:326
  43.2 3.3 %collective-permute-done.19 = bf16[32,2560]{1,0:T(8,128)(2,1)S(1)} collective-permute-done((bf16[32,2560]{1,0:T(8,128)(2,1)S(1)}, bf16[32,2560]{1,0:T(8,128)(2,1)S(1)}, u32[]{:S(2)}, u32[]{:S(2)}) %collective-permute-start.19) | collective-permute-done | bytes 163872 | tf_op jit(solution)/shard_map/ppermute | solution.py:322
  46.5 2.2 %collective-permute-start.21 = (bf16[32,2560]{1,0:T(8,128)(2,1)S(1)}, bf16[32,2560]{1,0:T(8,128)(2,1)S(1)}, u32[]{:S(2)}, u32[]{:S(2)}) collective-permute-start(bf16[32,2560]{1,0:T(8,128)(2,1)S(1)} %add_convert_fusion.1), channel_id=1, source_target_pairs={{0,16},{4,20},{8,24},{12,28},{16,0},{20,4},{24,8},{28,12},{1,17},{... | collective-permute-start | bytes 491528 | tf_op jit(solution)/shard_map/ppermute | solution.py:323
  48.7 1.0 %collective-permute-start.20 = (bf16[32,2560]{1,0:T(8,128)(2,1)S(1)}, bf16[32,2560]{1,0:T(8,128)(2,1)S(1)}, u32[]{:S(2)}, u32[]{:S(2)}) collective-permute-start(bf16[32,2560]{1,0:T(8,128)(2,1)S(1)} %get-tuple-element.35), channel_id=1, source_target_pairs={{0,8},{4,12},{8,0},{12,4},{16,24},{20,28},{24,16},{28,20},{1,9},{5... | collective-permute-start | bytes 491528 | tf_op jit(solution)/shard_map/ppermute | solution.py:328
  49.7 0.0 collective-permute-done.24
  49.7 1.6 %collective-permute-start.25 = (f32[32,2560]{1,0:T(8,128)S(1)}, f32[32,2560]{1,0:T(8,128)S(1)}, u32[]{:S(2)}, u32[]{:S(2)}) collective-permute-start(f32[32,2560]{1,0:T(8,128)S(1)} %convert_add_fusion), channel_id=1, source_target_pairs={{0,4},{4,0},{8,12},{12,8},{16,20},{20,16},{24,28},{28,24},{1,5},{5... | collective-permute-start | bytes 983048 | tf_op jit(solution)/shard_map/ppermute | solution.py:327
  51.4 1.4 %collective-permute-start.23 = (bf16[32,2560]{1,0:T(8,128)(2,1)S(1)}, bf16[32,2560]{1,0:T(8,128)(2,1)S(1)}, u32[]{:S(2)}, u32[]{:S(2)}) collective-permute-start(bf16[32,2560]{1,0:T(8,128)(2,1)S(1)} %add_convert_fusion), channel_id=1, source_target_pairs={{0,24},{4,28},{8,16},{12,20},{16,8},{20,12},{24,0},{28,4},{1,25},{... | collective-permute-start | bytes 491528 | tf_op jit(solution)/shard_map/ppermute | solution.py:325
  52.7 0.7 %patient_rows.1 = f32[8,256]{1,0:T(8,128)} custom-call(f32[512,256]{1,0:T(8,128)S(1)} %get-tuple-element.42.rot_ref, f32[512,256]{1,0:T(8,128)S(1)} %get-tuple-element.43.proj_ref), custom_call_target="tpu_custom_call" | custom-call | tf_op jit(solution)/shard_map/patient_rows/pallas_call | solution.py:224
  53.4 4.3 %collective-permute-done.21 = bf16[32,2560]{1,0:T(8,128)(2,1)S(1)} collective-permute-done((bf16[32,2560]{1,0:T(8,128)(2,1)S(1)}, bf16[32,2560]{1,0:T(8,128)(2,1)S(1)}, u32[]{:S(2)}, u32[]{:S(2)}) %collective-permute-start.21) | collective-permute-done | bytes 163872 | tf_op jit(solution)/shard_map/ppermute | solution.py:323
  57.7 0.0 collective-permute-done.20
  57.7 2.1 %collective-permute-done.23 = bf16[32,2560]{1,0:T(8,128)(2,1)S(1)} collective-permute-done((bf16[32,2560]{1,0:T(8,128)(2,1)S(1)}, bf16[32,2560]{1,0:T(8,128)(2,1)S(1)}, u32[]{:S(2)}, u32[]{:S(2)}) %collective-permute-start.23) | collective-permute-done | bytes 163872 | tf_op jit(solution)/shard_map/ppermute | solution.py:325
  59.8 0.0 collective-permute-done.25
  59.8 0.8 %add_add_fusion = f32[32,2560]{1,0:T(8,128)} fusion(f32[32,2560]{1,0:T(8,128)S(1)} %collective-permute-done.25, bf16[32,2560]{1,0:T(8,128)(2,1)S(1)} %collective-permute-done.23, bf16[32,2560]{1,0:T(8,128)(2,1)S(1)} %collective-permute-done.21, f32[32,2560]{1,0:T(8,128)S(1)} %get-tuple-element.32, bf16[32,2560]{1,0:T(8,128)(2,1)S(1)} %collective-permute-done.20), kind=kLoop, calls=%fused_computation.1 | loop fusion | flops 573440 | bytes 1474560 | tf_op jit(solution)/shard_map/add | solution.py:329
  (19 shorter events, 0.2 us)
Async XLA Ops:
  0.6 14.9 %copy-start.1 = (bf16[32,2560]{1,0:T(8,128)(2,1)S(1)}, bf16[32,2560]{1,0:T(8,128)(2,1)}, u32[]{:S(2)}) copy-start(bf16[32,2560]{1,0:T(8,128)(2,1)} %refs_0_.1) | copy-start | bytes 491524
  0.6 7.5 %collective-permute-start.1 = (bf16[32,2560]{1,0:T(8,128)(2,1)}, bf16[32,2560]{1,0:T(8,128)(2,1)S(1)}, u32[]{:S(2)}, u32[]{:S(2)}) collective-permute-start(bf16[32,2560]{1,0:T(8,128)(2,1)} %refs_0_.1), channel_id=1, source_target_pairs={{8,0},{16,8},{24,16},{28,24},{20,28},{12,20},{4,12},{0,4},{9,1},{1... | collective-permute-start | bytes 491528 | tf_op jit(solution)/shard_map/ppermute | solution.py:290
  3.7 6.2 %collective-permute-start = (bf16[32,2560]{1,0:T(8,128)(2,1)}, bf16[32,2560]{1,0:T(8,128)(2,1)S(1)}, u32[]{:S(2)}, u32[]{:S(2)}) collective-permute-start(bf16[32,2560]{1,0:T(8,128)(2,1)} %refs_0_.1), channel_id=1, source_target_pairs={{0,8},{8,16},{16,24},{24,28},{28,20},{20,12},{12,4},{4,0},{1,9},{9... | collective-permute-start | bytes 491528 | tf_op jit(solution)/shard_map/ppermute | solution.py:290
  8.1 5.6 %collective-permute-start.3 = (bf16[32,2560]{1,0:T(8,128)(2,1)S(1)}, bf16[32,2560]{1,0:T(8,128)(2,1)S(1)}, u32[]{:S(2)}, u32[]{:S(2)}) collective-permute-start(bf16[32,2560]{1,0:T(8,128)(2,1)S(1)} %collective-permute-done.1.refs_2_), channel_id=1, source_target_pairs={{8,0},{16,8},{24,16},{28,24},{20,28},{12,20},{4,12},{0,4},{9,1},{1... | collective-permute-start | bytes 491528 | tf_op jit(solution)/shard_map/ppermute | solution.py:290
  9.8 5.7 %collective-permute-start.2 = (bf16[32,2560]{1,0:T(8,128)(2,1)S(1)}, bf16[32,2560]{1,0:T(8,128)(2,1)S(1)}, u32[]{:S(2)}, u32[]{:S(2)}) collective-permute-start(bf16[32,2560]{1,0:T(8,128)(2,1)S(1)} %collective-permute-done.refs_1_), channel_id=1, source_target_pairs={{0,8},{8,16},{16,24},{24,28},{28,20},{20,12},{12,4},{4,0},{1,9},{9... | collective-permute-start | bytes 491528 | tf_op jit(solution)/shard_map/ppermute | solution.py:290
  10.3 1.6 %copy-start = (bf16[8,56,2560]{2,1,0:T(8,128)(2,1)S(1)}, bf16[8,56,2560]{2,1,0:T(8,128)(2,1)}, u32[]{:S(2)}) copy-start(bf16[8,56,2560]{2,1,0:T(8,128)(2,1)} %visits_ref.1) | copy-start | bytes 6881284
  12.0 0.7 %copy-start.4 = (s32[8]{0:T(128)S(1)}, s32[8]{0:T(128)}, u32[]{:S(2)}) copy-start(s32[8]{0:T(128)} %counts_ref.1) | copy-start | bytes 100
  13.8 5.4 %collective-permute-start.12 = (bf16[32,2560]{1,0:T(8,128)(2,1)S(1)}, bf16[32,2560]{1,0:T(8,128)(2,1)S(1)}, u32[]{:S(2)}, u32[]{:S(2)}) collective-permute-start(bf16[32,2560]{1,0:T(8,128)(2,1)S(1)} %collective-permute-done.3.refs_4_), channel_id=1, source_target_pairs={{8,0},{16,8},{24,16},{28,24},{20,28},{12,20},{4,12},{0,4},{9,1},{1... | collective-permute-start | bytes 491528 | tf_op jit(solution)/shard_map/ppermute | solution.py:290
  16.6 4.3 %collective-permute-start.4 = (f32[80,512]{1,0:T(8,128)S(1)}, f32[80,512]{1,0:T(8,128)S(1)}, u32[]{:S(2)}, u32[]{:S(2)}) collective-permute-start(f32[80,512]{1,0:T(8,128)S(1)} %get-tuple-element.26), channel_id=1, source_target_pairs={{0,1},{1,0},{2,3},{3,2},{4,5},{5,4},{6,7},{7,6},{8,9},{9,8},{10,11... | collective-permute-start | bytes 491528 | tf_op jit(solution)/shard_map/ppermute | solution.py:300
  16.6 6.6 %collective-permute-start.11 = (bf16[32,2560]{1,0:T(8,128)(2,1)S(1)}, bf16[32,2560]{1,0:T(8,128)(2,1)S(1)}, u32[]{:S(2)}, u32[]{:S(2)}) collective-permute-start(bf16[32,2560]{1,0:T(8,128)(2,1)S(1)} %collective-permute-done.2.refs_3_), channel_id=1, source_target_pairs={{0,8},{8,16},{16,24},{24,28},{28,20},{20,12},{12,4},{4,0},{1,9},{9... | collective-permute-start | bytes 491528 | tf_op jit(solution)/shard_map/ppermute | solution.py:290
  19.2 7.9 %collective-permute-start.14 = (bf16[32,2560]{1,0:T(8,128)(2,1)S(1)}, bf16[32,2560]{1,0:T(8,128)(2,1)S(1)}, u32[]{:S(2)}, u32[]{:S(2)}) collective-permute-start(bf16[32,2560]{1,0:T(8,128)(2,1)S(1)} %collective-permute-done.12.refs_1_), channel_id=1, source_target_pairs={{8,0},{16,8},{24,16},{28,24},{20,28},{12,20},{4,12},{0,4},{9,1},{1... | collective-permute-start | bytes 491528 | tf_op jit(solution)/shard_map/ppermute | solution.py:298
  20.9 7.1 %collective-permute-start.5 = (f32[80,512]{1,0:T(8,128)S(1)}, f32[80,512]{1,0:T(8,128)S(1)}, u32[]{:S(2)}, u32[]{:S(2)}) collective-permute-start(f32[80,512]{1,0:T(8,128)S(1)} %add.36), channel_id=1, source_target_pairs={{0,2},{1,3},{2,0},{3,1},{4,6},{5,7},{6,4},{7,5},{8,10},{9,11},{10,... | collective-permute-start | bytes 491528 | tf_op jit(solution)/shard_map/ppermute | solution.py:301
  24.2 10.3 %copy-start.2 = (bf16[256,256]{1,0:T(8,128)(2,1)S(1)}, bf16[256,256]{1,0:T(8,128)(2,1)}, u32[]{:S(2)}) copy-start(bf16[256,256]{1,0:T(8,128)(2,1)} %refs_11_.1) | copy-start | bytes 393220
  24.2 10.3 %copy-start.3 = (f32[8,256]{1,0:T(8,128)S(1)}, f32[8,256]{1,0:T(8,128)}, u32[]{:S(2)}) copy-start(f32[8,256]{1,0:T(8,128)} %refs_10_.1) | copy-start | bytes 24580
  24.2 1.3 %collective-permute-start.13 = (f32[32,512]{1,0:T(8,128)S(1)}, f32[32,512]{1,0:T(8,128)S(1)}, u32[]{:S(2)}, u32[]{:S(2)}) collective-permute-start(f32[32,512]{1,0:T(8,128)S(1)} %get-tuple-element.28), channel_id=1, source_target_pairs={{0,1},{1,0},{2,3},{3,2},{4,5},{5,4},{6,7},{7,6},{8,9},{9,8},{10,11... | collective-permute-start | bytes 196616 | tf_op jit(solution)/shard_map/ppermute | solution.py:303
  25.5 4.3 %collective-permute-start.16 = (f32[32,512]{1,0:T(8,128)S(1)}, f32[32,512]{1,0:T(8,128)S(1)}, u32[]{:S(2)}, u32[]{:S(2)}) collective-permute-start(f32[32,512]{1,0:T(8,128)S(1)} %add.38), channel_id=1, source_target_pairs={{0,2},{1,3},{2,0},{3,1},{4,6},{5,7},{6,4},{7,5},{8,10},{9,11},{10,... | collective-permute-start | bytes 196616 | tf_op jit(solution)/shard_map/ppermute | solution.py:304
  27.9 1.3 %collective-permute-start.15 = (f32[32,512]{1,0:T(8,128)S(1)}, f32[32,512]{1,0:T(8,128)S(1)}, u32[]{:S(2)}, u32[]{:S(2)}) collective-permute-start(f32[32,512]{1,0:T(8,128)S(1)} %project.5), channel_id=1, source_target_pairs={{0,1},{1,0},{2,3},{3,2},{4,5},{5,4},{6,7},{7,6},{8,9},{9,8},{10,11... | collective-permute-start | bytes 196616 | tf_op jit(solution)/shard_map/ppermute | solution.py:306
  28.0 3.7 %collective-permute-start.10 = (f32[16,512]{1,0:T(8,128)S(1)}, f32[16,512]{1,0:T(8,128)S(1)}, u32[]{:S(2)}, u32[]{:S(2)}) collective-permute-start(f32[16,512]{1,0:T(8,128)S(1)} %get-tuple-element.44), channel_id=1, source_target_pairs={{0,1},{1,0},{2,3},{3,2},{4,5},{5,4},{6,7},{7,6},{8,9},{9,8},{10,11... | collective-permute-start | bytes 98312 | tf_op jit(solution)/shard_map/ppermute | solution.py:310
  28.6 3.4 %collective-permute-start.6 = (f32[16,512]{1,0:T(8,128)S(1)}, f32[16,512]{1,0:T(8,128)S(1)}, u32[]{:S(2)}, u32[]{:S(2)}) collective-permute-start(f32[16,512]{1,0:T(8,128)S(1)} %get-tuple-element.48), channel_id=1, source_target_pairs={{0,1},{1,0},{2,3},{3,2},{4,5},{5,4},{6,7},{7,6},{8,9},{9,8},{10,11... | collective-permute-start | bytes 98312 | tf_op jit(solution)/shard_map/ppermute | solution.py:310
  29.9 3.4 %collective-permute-start.17 = (f32[32,512]{1,0:T(8,128)S(1)}, f32[32,512]{1,0:T(8,128)S(1)}, u32[]{:S(2)}, u32[]{:S(2)}) collective-permute-start(f32[32,512]{1,0:T(8,128)S(1)} %add.40.refs_6_), channel_id=1, source_target_pairs={{0,1},{1,0},{2,3},{3,2},{4,5},{5,4},{6,7},{7,6},{8,9},{9,8},{10,11... | collective-permute-start | bytes 196616 | tf_op jit(solution)/shard_map/ppermute | solution.py:311
  30.0 4.5 %collective-permute-start.18 = (f32[32,512]{1,0:T(8,128)S(1)}, f32[32,512]{1,0:T(8,128)S(1)}, u32[]{:S(2)}, u32[]{:S(2)}) collective-permute-start(f32[32,512]{1,0:T(8,128)S(1)} %add.39.refs_8_), channel_id=1, source_target_pairs={{0,2},{1,3},{2,0},{3,1},{4,6},{5,7},{6,4},{7,5},{8,10},{9,11},{10,... | collective-permute-start | bytes 196616 | tf_op jit(solution)/shard_map/ppermute | solution.py:312
  31.5 1.2 %collective-permute-start.7 = (f32[16,512]{1,0:T(8,128)S(1)}, f32[16,512]{1,0:T(8,128)S(1)}, u32[]{:S(2)}, u32[]{:S(2)}) collective-permute-start(f32[16,512]{1,0:T(8,128)S(1)} %get-tuple-element.47), channel_id=1, source_target_pairs={{0,1},{1,0},{2,3},{3,2},{4,5},{5,4},{6,7},{7,6},{8,9},{9,8},{10,11... | collective-permute-start | bytes 98312 | tf_op jit(solution)/shard_map/ppermute | solution.py:310
  31.7 1.2 %collective-permute-start.8 = (f32[16,512]{1,0:T(8,128)S(1)}, f32[16,512]{1,0:T(8,128)S(1)}, u32[]{:S(2)}, u32[]{:S(2)}) collective-permute-start(f32[16,512]{1,0:T(8,128)S(1)} %get-tuple-element.46), channel_id=1, source_target_pairs={{0,1},{1,0},{2,3},{3,2},{4,5},{5,4},{6,7},{7,6},{8,9},{9,8},{10,11... | collective-permute-start | bytes 98312 | tf_op jit(solution)/shard_map/ppermute | solution.py:310
  32.0 1.2 %collective-permute-start.9 = (f32[16,512]{1,0:T(8,128)S(1)}, f32[16,512]{1,0:T(8,128)S(1)}, u32[]{:S(2)}, u32[]{:S(2)}) collective-permute-start(f32[16,512]{1,0:T(8,128)S(1)} %get-tuple-element.45), channel_id=1, source_target_pairs={{0,1},{1,0},{2,3},{3,2},{4,5},{5,4},{6,7},{7,6},{8,9},{9,8},{10,11... | collective-permute-start | bytes 98312 | tf_op jit(solution)/shard_map/ppermute | solution.py:310
  39.3 7.2 %collective-permute-start.19 = (bf16[32,2560]{1,0:T(8,128)(2,1)S(1)}, bf16[32,2560]{1,0:T(8,128)(2,1)S(1)}, u32[]{:S(2)}, u32[]{:S(2)}) collective-permute-start(bf16[32,2560]{1,0:T(8,128)(2,1)S(1)} %get-tuple-element.33), channel_id=1, source_target_pairs={{0,4},{4,0},{8,12},{12,8},{16,20},{20,16},{24,28},{28,24},{1,5},{5... | collective-permute-start | bytes 491528 | tf_op jit(solution)/shard_map/ppermute | solution.py:322
  41.4 9.9 %collective-permute-start.22 = (bf16[32,2560]{1,0:T(8,128)(2,1)S(1)}, bf16[32,2560]{1,0:T(8,128)(2,1)S(1)}, u32[]{:S(2)}, u32[]{:S(2)}) collective-permute-start(bf16[32,2560]{1,0:T(8,128)(2,1)S(1)} %get-tuple-element.39), channel_id=1, source_target_pairs={{0,4},{4,0},{8,12},{12,8},{16,20},{20,16},{24,28},{28,24},{1,5},{5... | collective-permute-start | bytes 491528 | tf_op jit(solution)/shard_map/ppermute | solution.py:324
  42.0 7.7 %collective-permute-start.24 = (bf16[32,2560]{1,0:T(8,128)(2,1)S(1)}, bf16[32,2560]{1,0:T(8,128)(2,1)S(1)}, u32[]{:S(2)}, u32[]{:S(2)}) collective-permute-start(bf16[32,2560]{1,0:T(8,128)(2,1)S(1)} %get-tuple-element.41), channel_id=1, source_target_pairs={{0,8},{4,12},{8,0},{12,4},{16,24},{20,28},{24,16},{28,20},{1,9},{5... | collective-permute-start | bytes 491528 | tf_op jit(solution)/shard_map/ppermute | solution.py:326
  46.5 11.2 %collective-permute-start.21 = (bf16[32,2560]{1,0:T(8,128)(2,1)S(1)}, bf16[32,2560]{1,0:T(8,128)(2,1)S(1)}, u32[]{:S(2)}, u32[]{:S(2)}) collective-permute-start(bf16[32,2560]{1,0:T(8,128)(2,1)S(1)} %add_convert_fusion.1), channel_id=1, source_target_pairs={{0,16},{4,20},{8,24},{12,28},{16,0},{20,4},{24,8},{28,12},{1,17},{... | collective-permute-start | bytes 491528 | tf_op jit(solution)/shard_map/ppermute | solution.py:323
  48.7 9.0 %collective-permute-start.20 = (bf16[32,2560]{1,0:T(8,128)(2,1)S(1)}, bf16[32,2560]{1,0:T(8,128)(2,1)S(1)}, u32[]{:S(2)}, u32[]{:S(2)}) collective-permute-start(bf16[32,2560]{1,0:T(8,128)(2,1)S(1)} %get-tuple-element.35), channel_id=1, source_target_pairs={{0,8},{4,12},{8,0},{12,4},{16,24},{20,28},{24,16},{28,20},{1,9},{5... | collective-permute-start | bytes 491528 | tf_op jit(solution)/shard_map/ppermute | solution.py:328
  49.7 10.1 %collective-permute-start.25 = (f32[32,2560]{1,0:T(8,128)S(1)}, f32[32,2560]{1,0:T(8,128)S(1)}, u32[]{:S(2)}, u32[]{:S(2)}) collective-permute-start(f32[32,2560]{1,0:T(8,128)S(1)} %convert_add_fusion), channel_id=1, source_target_pairs={{0,4},{4,0},{8,12},{12,8},{16,20},{20,16},{24,28},{28,24},{1,5},{5... | collective-permute-start | bytes 983048 | tf_op jit(solution)/shard_map/ppermute | solution.py:327
  51.4 8.4 %collective-permute-start.23 = (bf16[32,2560]{1,0:T(8,128)(2,1)S(1)}, bf16[32,2560]{1,0:T(8,128)(2,1)S(1)}, u32[]{:S(2)}, u32[]{:S(2)}) collective-permute-start(bf16[32,2560]{1,0:T(8,128)(2,1)S(1)} %add_convert_fusion), channel_id=1, source_target_pairs={{0,24},{4,28},{8,16},{12,20},{16,8},{20,12},{24,0},{28,4},{1,25},{... | collective-permute-start | bytes 491528 | tf_op jit(solution)/shard_map/ppermute | solution.py:325

commit v7 on v5

--- a/solution.py
+++ b/solution.py
@@ -307,9 +307,9 @@
     sums0 = [s + f for s, f in zip(sums0, from0)]
     sums1 = [s + f for s, f in zip(sums1, from1)]
     back0 = [to_core(p) for s in sums0 for p in cut(s, half)]
-    back1 = [to_core(s) for s in sums1]
+    back1 = [to_core(p) for s in sums1 for p in cut(s, half)]
     parts = [*sums0, *back0, *sums1, *back1, sums2, to_x(sums2)]
-    plan = (((0, -1, 1, -2, 2), cuts0, (half,) * 5), ((-3, 3), cuts1, cuts1), ((4,), (), ()))
+    plan = (((0, -1, 1, -2, 2), cuts0, (half,) * 5), ((-3, 3), cuts1, (half,) * 2), ((4,), (), ()))
     wt, rot, proj, there2, there3, near, own = procrustes(
         parts, plan, patient_weights, core, block, masked
     )

time: 60.9 us -> 60.4 us (level)
  waiting for transfers between devices: 20.3 us -> 19.5 us
  transfers between devices with their start and end apart: 27 -> 28, of which waited for: 13 -> 13; matrix products, arithmetic and copies ran while one was open for 2% -> 2% of each run, Pallas kernels for 8% -> 9%
where the time goes in v7:
time: 60.4 us; the launch traced here: 60.2 us
  starting transfers between devices  25.6 us (42%)
  waiting for transfers between devices  19.5 us (32%)
  Pallas kernels  9.96 us (16%)
  local copies, waits for them, and re-layouts  2.61 us (4%)
  other arithmetic  1.7 us (3%)
  between operations  0.85 us (1%)
    ppermute x3, starting transfers between devices, step(): lax.ppermute(back, 'subj', BACK)  6.6 us
    ppermute x3, waiting for transfers between devices, step(): lax.ppermute(back, 'subj', BACK)  5.75 us
    pallas_call x1, Pallas kernels, procrustes(): pl.pallas_call(functools.partial(procrustes_body, block, plan), out_shape...  4.84 us
    ppermute x1, waiting for transfers between devices, per_device(): far2 = z2((here2 + got2.astype(F32)).astype(BF16)).astype(F32)  3.93 us
    ppermute x1, waiting for transfers between devices, per_device(): got2, own = tie(y(there2), own)  3.16 us
    pallas_call x3, Pallas kernels, project(): pl.pallas_call(functools.partial(project_body, len(blocks), cuts), out_sh...  2.8 us
    ppermute x1, starting transfers between devices, per_device(): far2 = z2((here2 + got2.astype(F32)).astype(BF16)).astype(F32)  2.33 us
    unnamed x10, local copies, waits for them, and re-layouts  2.31 us
  transfers between devices with their start and end apart: 28, of which 13 were waited for; matrix products, arithmetic and copies ran while one was open for 2% of the time, Pallas kernels for 9%

profile of v7, /device:TPU:0, one launch (start us, length us, event | category | flops | bytes accessed | tf_op | source)
XLA Modules:
  0.0 60.2 jit_solution(17862887086717936792)
XLA Ops:
  0.6 3.0 %collective-permute-start.1 = (bf16[32,2560]{1,0:T(8,128)(2,1)}, bf16[32,2560]{1,0:T(8,128)(2,1)S(1)}, u32[]{:S(2)}, u32[]{:S(2)}) collective-permute-start(bf16[32,2560]{1,0:T(8,128)(2,1)} %refs_0_.1), channel_id=1, source_target_pairs={{8,0},{16,8},{24,16},{28,24},{20,28},{12,20},{4,12},{0,4},{9,1},{1... | collective-permute-start | bytes 491528 | tf_op jit(solution)/shard_map/ppermute | solution.py:289
  3.7 0.1 collective-permute-start
  3.8 0.7 %convert_element_type.27 = bf16[8,20]{1,0:T(8,128)(2,1)S(1)} convert(s32[8,20]{1,0:T(8,128)} %param.7) | non-fusion elementwise | flops 160 | bytes 960 | tf_op jit(solution)/shard_map/convert_element_type | solution.py:76
  4.5 0.1 copy.8
  4.6 0.1 broadcast_bitcast_fusion
  4.7 0.1 copy.9.gate_ref
  4.7 0.0 copy-start
  4.8 1.6 %copy-done = bf16[8,56,2560]{2,1,0:T(8,128)(2,1)S(1)} copy-done((bf16[8,56,2560]{2,1,0:T(8,128)(2,1)S(1)}, bf16[8,56,2560]{2,1,0:T(8,128)(2,1)}, u32[]{:S(2)}) %copy-start) | copy-done | bytes 2293784
  6.4 0.7 %copy-done.4 = s32[8]{0:T(128)S(1)} copy-done((s32[8]{0:T(128)S(1)}, s32[8]{0:T(128)}, u32[]{:S(2)}) %copy-start.4) | copy-done | bytes 56
  7.0 1.1 %mask_visits.1.refs_5_.refs_2_.refs_1_.refs_13_.masked_ref = bf16[512,2560]{1,0:T(8,128)(2,1)S(1)} custom-call(s32[8]{0:T(128)S(1)} %copy-done.4, bf16[8,1,2560]{2,1,0:T(2,128)(2,1)S(1)} %copy.9.gate_ref, bf16[8,56,2560]{2,1,0:T(8,128)(2,1)S(1)} %copy-done), custom_call_target="tpu_custom_call" | custom-call | tf_op jit(solution)/shard_map/mask_visits/pallas_call | solution.py:77
  8.2 0.0 collective-permute-done.1.refs_2_
  8.2 2.0 %collective-permute-start.3 = (bf16[32,2560]{1,0:T(8,128)(2,1)S(1)}, bf16[32,2560]{1,0:T(8,128)(2,1)S(1)}, u32[]{:S(2)}, u32[]{:S(2)}) collective-permute-start(bf16[32,2560]{1,0:T(8,128)(2,1)S(1)} %collective-permute-done.1.refs_2_), channel_id=1, source_target_pairs={{8,0},{16,8},{24,16},{28,24},{20,28},{12,20},{4,12},{0,4},{9,1},{1... | collective-permute-start | bytes 491528 | tf_op jit(solution)/shard_map/ppermute | solution.py:289
  10.2 0.0 collective-permute-done.refs_1_
  10.2 0.1 collective-permute-start.2
  10.3 3.6 %collective-permute-done.3.refs_4_ = bf16[32,2560]{1,0:T(8,128)(2,1)S(1)} collective-permute-done((bf16[32,2560]{1,0:T(8,128)(2,1)S(1)}, bf16[32,2560]{1,0:T(8,128)(2,1)S(1)}, u32[]{:S(2)}, u32[]{:S(2)}) %collective-permute-start.3) | collective-permute-done | bytes 163872 | tf_op jit(solution)/shard_map/ppermute | solution.py:289
  13.9 1.6 %collective-permute-start.12 = (bf16[32,2560]{1,0:T(8,128)(2,1)S(1)}, bf16[32,2560]{1,0:T(8,128)(2,1)S(1)}, u32[]{:S(2)}, u32[]{:S(2)}) collective-permute-start(bf16[32,2560]{1,0:T(8,128)(2,1)S(1)} %collective-permute-done.3.refs_4_), channel_id=1, source_target_pairs={{8,0},{16,8},{24,16},{28,24},{20,28},{12,20},{4,12},{0,4},{9,1},{1... | collective-permute-start | bytes 491528 | tf_op jit(solution)/shard_map/ppermute | solution.py:289
  15.5 1.0 %project.3 = (f32[80,512]{1,0:T(8,128)S(1)}, f32[80,512]{1,0:T(8,128)S(1)}) custom-call(bf16[32,2560]{1,0:T(8,128)(2,1)S(1)} %copy-done.1, bf16[32,2560]{1,0:T(8,128)(2,1)S(1)} %collective-permute-done.refs_1_, bf16[32,2560]{1,0:T(8,128)(2,1)S(1)} %collective-permute-done.1.refs_2_, bf16[32,2560]{1,0:T(8,128)(2,1)S(1)} %collective-permute-done.2.refs_3_, ...), custom_call_target="tpu_custom_call" | custom-call | tf_op jit(solution)/shard_map/project/pallas_call | solution.py:114
  16.6 0.1 collective-permute-start.4
  16.7 0.5 collective-permute-start.11
  17.1 2.1 %collective-permute-done.12.refs_1_ = bf16[32,2560]{1,0:T(8,128)(2,1)S(1)} collective-permute-done((bf16[32,2560]{1,0:T(8,128)(2,1)S(1)}, bf16[32,2560]{1,0:T(8,128)(2,1)S(1)}, u32[]{:S(2)}, u32[]{:S(2)}) %collective-permute-start.12) | collective-permute-done | bytes 163872 | tf_op jit(solution)/shard_map/ppermute | solution.py:289
  19.2 1.6 %collective-permute-start.14 = (bf16[32,2560]{1,0:T(8,128)(2,1)S(1)}, bf16[32,2560]{1,0:T(8,128)(2,1)S(1)}, u32[]{:S(2)}, u32[]{:S(2)}) collective-permute-start(bf16[32,2560]{1,0:T(8,128)(2,1)S(1)} %collective-permute-done.12.refs_1_), channel_id=1, source_target_pairs={{8,0},{16,8},{24,16},{28,24},{20,28},{12,20},{4,12},{0,4},{9,1},{1... | collective-permute-start | bytes 491528 | tf_op jit(solution)/shard_map/ppermute | solution.py:297
  20.9 1.6 %collective-permute-start.5 = (f32[80,512]{1,0:T(8,128)S(1)}, f32[80,512]{1,0:T(8,128)S(1)}, u32[]{:S(2)}, u32[]{:S(2)}) collective-permute-start(f32[80,512]{1,0:T(8,128)S(1)} %add.36), channel_id=1, source_target_pairs={{0,2},{1,3},{2,0},{3,1},{4,6},{5,7},{6,4},{7,5},{8,10},{9,11},{10,... | collective-permute-start | bytes 491528 | tf_op jit(solution)/shard_map/ppermute | solution.py:300
  22.4 0.8 %collective-permute-done.11.refs_0_ = bf16[32,2560]{1,0:T(8,128)(2,1)S(1)} collective-permute-done((bf16[32,2560]{1,0:T(8,128)(2,1)S(1)}, bf16[32,2560]{1,0:T(8,128)(2,1)S(1)}, u32[]{:S(2)}, u32[]{:S(2)}) %collective-permute-start.11) | collective-permute-done | bytes 163872 | tf_op jit(solution)/shard_map/ppermute | solution.py:289
  23.3 0.9 %project.4 = (f32[32,512]{1,0:T(8,128)S(1)}, f32[32,512]{1,0:T(8,128)S(1)}) custom-call(bf16[32,2560]{1,0:T(8,128)(2,1)S(1)} %collective-permute-done.11.refs_0_, bf16[32,2560]{1,0:T(8,128)(2,1)S(1)} %collective-permute-done.12.refs_1_, bf16[512,2560]{1,0:T(8,128)(2,1)S(1)} %mask_visits.1.refs_5_.refs_2_.refs_1_.refs_13_.masked_ref), custom_call_target="tpu_custom_call" | custom-call | tf_op jit(solution)/shard_map/project/pallas_call | solution.py:114
  24.2 0.0 copy-start.2
  24.2 0.0 copy-start.3
  24.2 0.1 collective-permute-start.13
  24.3 1.2 %collective-permute-done.13 = f32[32,512]{1,0:T(8,128)S(1)} collective-permute-done((f32[32,512]{1,0:T(8,128)S(1)}, f32[32,512]{1,0:T(8,128)S(1)}, u32[]{:S(2)}, u32[]{:S(2)}) %collective-permute-start.13) | collective-permute-done | bytes 65568 | tf_op jit(solution)/shard_map/ppermute | solution.py:302
  25.6 1.6 %collective-permute-start.16 = (f32[32,512]{1,0:T(8,128)S(1)}, f32[32,512]{1,0:T(8,128)S(1)}, u32[]{:S(2)}, u32[]{:S(2)}) collective-permute-start(f32[32,512]{1,0:T(8,128)S(1)} %add.38), channel_id=1, source_target_pairs={{0,2},{1,3},{2,0},{3,1},{4,6},{5,7},{6,4},{7,5},{8,10},{9,11},{10,... | collective-permute-start | bytes 196616 | tf_op jit(solution)/shard_map/ppermute | solution.py:303
  27.1 0.0 collective-permute-done.14.refs_0_
  27.1 0.8 %project.5 = f32[32,512]{1,0:T(8,128)S(1)} custom-call(bf16[32,2560]{1,0:T(8,128)(2,1)S(1)} %collective-permute-done.14.refs_0_, bf16[512,2560]{1,0:T(8,128)(2,1)S(1)} %mask_visits.1.refs_5_.refs_2_.refs_1_.refs_13_.masked_ref), custom_call_target="tpu_custom_call" | custom-call | tf_op jit(solution)/shard_map/project/pallas_call | solution.py:114
  28.0 0.0 collective-permute-done.5
  28.0 0.6 collective-permute-start.10
  28.6 0.1 collective-permute-start.6
  28.7 0.4 collective-permute-start.7
  29.1 0.1 collective-permute-done.15
  29.2 0.2 collective-permute-start.8
  29.4 0.5 collective-permute-done.16
  29.9 1.6 %collective-permute-start.19 = (f32[32,512]{1,0:T(8,128)S(1)}, f32[32,512]{1,0:T(8,128)S(1)}, u32[]{:S(2)}, u32[]{:S(2)}) collective-permute-start(f32[32,512]{1,0:T(8,128)S(1)} %add.39.refs_9_), channel_id=1, source_target_pairs={{0,2},{1,3},{2,0},{3,1},{4,6},{5,7},{6,4},{7,5},{8,10},{9,11},{10,... | collective-permute-start | bytes 196616 | tf_op jit(solution)/shard_map/ppermute | solution.py:311
  31.5 0.1 collective-permute-start.9
  31.5 0.0 collective-permute-done.6.refs_1_
  31.6 0.5 collective-permute-start.17
  32.0 0.0 collective-permute-done.7.refs_2_
  32.0 0.1 collective-permute-start.18
  32.1 0.6 collective-permute-done.9.refs_4_
  32.7 0.2 collective-permute-done.17.refs_7_
  32.9 0.4 collective-permute-done.18.refs_8_
  33.3 1.0 %collective-permute-done.19.refs_10_ = f32[32,512]{1,0:T(8,128)S(1)} collective-permute-done((f32[32,512]{1,0:T(8,128)S(1)}, f32[32,512]{1,0:T(8,128)S(1)}, u32[]{:S(2)}, u32[]{:S(2)}) %collective-permute-start.19) | collective-permute-done | bytes 65568 | tf_op jit(solution)/shard_map/ppermute | solution.py:311
  34.2 4.8 %procrustes.1 = (bf16[256,512]{1,0:T(8,128)(2,1)S(1)}, f32[512,256]{1,0:T(8,128)S(1)}, f32[512,256]{1,0:T(8,128)S(1)}, bf16[32,2560]{1,0:T(8,128)(2,1)S(1)}, bf1...) custom-call(f32[80,512]{1,0:T(8,128)S(1)} %add.37.refs_0_, ...), custom_call_target="tpu_custom_call" | custom-call | bytes 17280000 | tf_op jit(solution)/shard_map/procrustes/pallas_call | solution.py:201
  39.1 1.6 %collective-permute-start.20 = (bf16[32,2560]{1,0:T(8,128)(2,1)S(1)}, bf16[32,2560]{1,0:T(8,128)(2,1)S(1)}, u32[]{:S(2)}, u32[]{:S(2)}) collective-permute-start(bf16[32,2560]{1,0:T(8,128)(2,1)S(1)} %get-tuple-element.33), channel_id=1, source_target_pairs={{0,4},{4,0},{8,12},{12,8},{16,20},{20,16},{24,28},{28,24},{1,5},{5... | collective-permute-start | bytes 491528 | tf_op jit(solution)/shard_map/ppermute | solution.py:321
  40.7 0.5 term.1
  41.2 0.5 collective-permute-start.23
  41.8 1.2 %collective-permute-start.25 = (bf16[32,2560]{1,0:T(8,128)(2,1)S(1)}, bf16[32,2560]{1,0:T(8,128)(2,1)S(1)}, u32[]{:S(2)}, u32[]{:S(2)}) collective-permute-start(bf16[32,2560]{1,0:T(8,128)(2,1)S(1)} %get-tuple-element.41), channel_id=1, source_target_pairs={{0,8},{4,12},{8,0},{12,4},{16,24},{20,28},{24,16},{28,20},{1,9},{5... | collective-permute-start | bytes 491528 | tf_op jit(solution)/shard_map/ppermute | solution.py:325
  43.0 3.2 %collective-permute-done.20 = bf16[32,2560]{1,0:T(8,128)(2,1)S(1)} collective-permute-done((bf16[32,2560]{1,0:T(8,128)(2,1)S(1)}, bf16[32,2560]{1,0:T(8,128)(2,1)S(1)}, u32[]{:S(2)}, u32[]{:S(2)}) %collective-permute-start.20) | collective-permute-done | bytes 163872 | tf_op jit(solution)/shard_map/ppermute | solution.py:321
  46.2 2.3 %collective-permute-start.22 = (bf16[32,2560]{1,0:T(8,128)(2,1)S(1)}, bf16[32,2560]{1,0:T(8,128)(2,1)S(1)}, u32[]{:S(2)}, u32[]{:S(2)}) collective-permute-start(bf16[32,2560]{1,0:T(8,128)(2,1)S(1)} %add_convert_fusion.1), channel_id=1, source_target_pairs={{0,16},{4,20},{8,24},{12,28},{16,0},{20,4},{24,8},{28,12},{1,17},{... | collective-permute-start | bytes 491528 | tf_op jit(solution)/shard_map/ppermute | solution.py:322
  48.5 0.8 %collective-permute-start.21 = (bf16[32,2560]{1,0:T(8,128)(2,1)S(1)}, bf16[32,2560]{1,0:T(8,128)(2,1)S(1)}, u32[]{:S(2)}, u32[]{:S(2)}) collective-permute-start(bf16[32,2560]{1,0:T(8,128)(2,1)S(1)} %get-tuple-element.35), channel_id=1, source_target_pairs={{0,8},{4,12},{8,0},{12,4},{16,24},{20,28},{24,16},{28,20},{1,9},{5... | collective-permute-start | bytes 491528 | tf_op jit(solution)/shard_map/ppermute | solution.py:327
  49.3 0.0 collective-permute-done.23
  49.4 1.4 %collective-permute-start.24 = (bf16[32,2560]{1,0:T(8,128)(2,1)S(1)}, bf16[32,2560]{1,0:T(8,128)(2,1)S(1)}, u32[]{:S(2)}, u32[]{:S(2)}) collective-permute-start(bf16[32,2560]{1,0:T(8,128)(2,1)S(1)} %add_convert_fusion), channel_id=1, source_target_pairs={{0,24},{4,28},{8,16},{12,20},{16,8},{20,12},{24,0},{28,4},{1,25},{... | collective-permute-start | bytes 491528 | tf_op jit(solution)/shard_map/ppermute | solution.py:324
  50.8 1.8 %collective-permute-start.26 = (f32[16,2560]{1,0:T(8,128)S(1)}, f32[16,2560]{1,0:T(8,128)S(1)}, u32[]{:S(2)}, u32[]{:S(2)}) collective-permute-start(f32[16,2560]{1,0:T(8,128)S(1)} %get-tuple-element.44), channel_id=1, source_target_pairs={{0,4},{4,0},{8,12},{12,8},{16,20},{20,16},{24,28},{28,24},{1,5},{5... | collective-permute-start | bytes 491528 | tf_op jit(solution)/shard_map/ppermute | solution.py:326
  52.6 0.3 collective-permute-start.27
  52.9 0.7 %patient_rows.1 = f32[8,256]{1,0:T(8,128)} custom-call(f32[512,256]{1,0:T(8,128)S(1)} %get-tuple-element.42.rot_ref, f32[512,256]{1,0:T(8,128)S(1)} %get-tuple-element.43.proj_ref), custom_call_target="tpu_custom_call" | custom-call | tf_op jit(solution)/shard_map/patient_rows/pallas_call | solution.py:223
  53.6 3.9 %collective-permute-done.22 = bf16[32,2560]{1,0:T(8,128)(2,1)S(1)} collective-permute-done((bf16[32,2560]{1,0:T(8,128)(2,1)S(1)}, bf16[32,2560]{1,0:T(8,128)(2,1)S(1)}, u32[]{:S(2)}, u32[]{:S(2)}) %collective-permute-start.22) | collective-permute-done | bytes 163872 | tf_op jit(solution)/shard_map/ppermute | solution.py:322
  57.5 1.9 %collective-permute-done.24 = bf16[32,2560]{1,0:T(8,128)(2,1)S(1)} collective-permute-done((bf16[32,2560]{1,0:T(8,128)(2,1)S(1)}, bf16[32,2560]{1,0:T(8,128)(2,1)S(1)}, u32[]{:S(2)}, u32[]{:S(2)}) %collective-permute-start.24) | collective-permute-done | bytes 163872 | tf_op jit(solution)/shard_map/ppermute | solution.py:324
  59.4 0.8 %maximum_add_fusion = f32[32,2560]{1,0:T(8,128)} fusion(f32[16,2560]{1,0:T(8,128)S(1)} %collective-permute-done.27, f32[16,2560]{1,0:T(8,128)S(1)} %collective-permute-done.26, bf16[32,2560]{1,0:T(8,128)(2,1)S(1)} %collective-permute-done.24, bf16[32,2560]{1,0:T(8,128)(2,1)S(1)} %collective-permute-done.22, f32[32,2560]{1,0:T(8,128)S(1)} %get-tuple-element.32, ...), kind=kLoop, calls=%fused_computation | loop fusion | flops 655360 | bytes 1474560 | tf_op jit(solution)/shard_map/add | solution.py:328
  (25 shorter events, 0.3 us)
Async XLA Ops:
  0.6 14.9 %copy-start.1 = (bf16[32,2560]{1,0:T(8,128)(2,1)S(1)}, bf16[32,2560]{1,0:T(8,128)(2,1)}, u32[]{:S(2)}) copy-start(bf16[32,2560]{1,0:T(8,128)(2,1)} %refs_0_.1) | copy-start | bytes 491524
  0.6 7.6 %collective-permute-start.1 = (bf16[32,2560]{1,0:T(8,128)(2,1)}, bf16[32,2560]{1,0:T(8,128)(2,1)S(1)}, u32[]{:S(2)}, u32[]{:S(2)}) collective-permute-start(bf16[32,2560]{1,0:T(8,128)(2,1)} %refs_0_.1), channel_id=1, source_target_pairs={{8,0},{16,8},{24,16},{28,24},{20,28},{12,20},{4,12},{0,4},{9,1},{1... | collective-permute-start | bytes 491528 | tf_op jit(solution)/shard_map/ppermute | solution.py:289
  3.7 6.5 %collective-permute-start = (bf16[32,2560]{1,0:T(8,128)(2,1)}, bf16[32,2560]{1,0:T(8,128)(2,1)S(1)}, u32[]{:S(2)}, u32[]{:S(2)}) collective-permute-start(bf16[32,2560]{1,0:T(8,128)(2,1)} %refs_0_.1), channel_id=1, source_target_pairs={{0,8},{8,16},{16,24},{24,28},{28,20},{20,12},{12,4},{4,0},{1,9},{9... | collective-permute-start | bytes 491528 | tf_op jit(solution)/shard_map/ppermute | solution.py:289
  4.7 1.6 %copy-start = (bf16[8,56,2560]{2,1,0:T(8,128)(2,1)S(1)}, bf16[8,56,2560]{2,1,0:T(8,128)(2,1)}, u32[]{:S(2)}) copy-start(bf16[8,56,2560]{2,1,0:T(8,128)(2,1)} %visits_ref.1) | copy-start | bytes 6881284
  6.4 0.7 %copy-start.4 = (s32[8]{0:T(128)S(1)}, s32[8]{0:T(128)}, u32[]{:S(2)}) copy-start(s32[8]{0:T(128)} %counts_ref.1) | copy-start | bytes 100
  8.2 5.7 %collective-permute-start.3 = (bf16[32,2560]{1,0:T(8,128)(2,1)S(1)}, bf16[32,2560]{1,0:T(8,128)(2,1)S(1)}, u32[]{:S(2)}, u32[]{:S(2)}) collective-permute-start(bf16[32,2560]{1,0:T(8,128)(2,1)S(1)} %collective-permute-done.1.refs_2_), channel_id=1, source_target_pairs={{8,0},{16,8},{24,16},{28,24},{20,28},{12,20},{4,12},{0,4},{9,1},{1... | collective-permute-start | bytes 491528 | tf_op jit(solution)/shard_map/ppermute | solution.py:289
  10.2 5.4 %collective-permute-start.2 = (bf16[32,2560]{1,0:T(8,128)(2,1)S(1)}, bf16[32,2560]{1,0:T(8,128)(2,1)S(1)}, u32[]{:S(2)}, u32[]{:S(2)}) collective-permute-start(bf16[32,2560]{1,0:T(8,128)(2,1)S(1)} %collective-permute-done.refs_1_), channel_id=1, source_target_pairs={{0,8},{8,16},{16,24},{24,28},{28,20},{20,12},{12,4},{4,0},{1,9},{9... | collective-permute-start | bytes 491528 | tf_op jit(solution)/shard_map/ppermute | solution.py:289
  13.9 5.3 %collective-permute-start.12 = (bf16[32,2560]{1,0:T(8,128)(2,1)S(1)}, bf16[32,2560]{1,0:T(8,128)(2,1)S(1)}, u32[]{:S(2)}, u32[]{:S(2)}) collective-permute-start(bf16[32,2560]{1,0:T(8,128)(2,1)S(1)} %collective-permute-done.3.refs_4_), channel_id=1, source_target_pairs={{8,0},{16,8},{24,16},{28,24},{20,28},{12,20},{4,12},{0,4},{9,1},{1... | collective-permute-start | bytes 491528 | tf_op jit(solution)/shard_map/ppermute | solution.py:289
  16.6 4.3 %collective-permute-start.4 = (f32[80,512]{1,0:T(8,128)S(1)}, f32[80,512]{1,0:T(8,128)S(1)}, u32[]{:S(2)}, u32[]{:S(2)}) collective-permute-start(f32[80,512]{1,0:T(8,128)S(1)} %get-tuple-element.26), channel_id=1, source_target_pairs={{0,1},{1,0},{2,3},{3,2},{4,5},{5,4},{6,7},{7,6},{8,9},{9,8},{10,11... | collective-permute-start | bytes 491528 | tf_op jit(solution)/shard_map/ppermute | solution.py:299
  16.7 6.6 %collective-permute-start.11 = (bf16[32,2560]{1,0:T(8,128)(2,1)S(1)}, bf16[32,2560]{1,0:T(8,128)(2,1)S(1)}, u32[]{:S(2)}, u32[]{:S(2)}) collective-permute-start(bf16[32,2560]{1,0:T(8,128)(2,1)S(1)} %collective-permute-done.2.refs_3_), channel_id=1, source_target_pairs={{0,8},{8,16},{16,24},{24,28},{28,20},{20,12},{12,4},{4,0},{1,9},{9... | collective-permute-start | bytes 491528 | tf_op jit(solution)/shard_map/ppermute | solution.py:289
  19.2 7.9 %collective-permute-start.14 = (bf16[32,2560]{1,0:T(8,128)(2,1)S(1)}, bf16[32,2560]{1,0:T(8,128)(2,1)S(1)}, u32[]{:S(2)}, u32[]{:S(2)}) collective-permute-start(bf16[32,2560]{1,0:T(8,128)(2,1)S(1)} %collective-permute-done.12.refs_1_), channel_id=1, source_target_pairs={{8,0},{16,8},{24,16},{28,24},{20,28},{12,20},{4,12},{0,4},{9,1},{1... | collective-permute-start | bytes 491528 | tf_op jit(solution)/shard_map/ppermute | solution.py:297
  20.9 7.1 %collective-permute-start.5 = (f32[80,512]{1,0:T(8,128)S(1)}, f32[80,512]{1,0:T(8,128)S(1)}, u32[]{:S(2)}, u32[]{:S(2)}) collective-permute-start(f32[80,512]{1,0:T(8,128)S(1)} %add.36), channel_id=1, source_target_pairs={{0,2},{1,3},{2,0},{3,1},{4,6},{5,7},{6,4},{7,5},{8,10},{9,11},{10,... | collective-permute-start | bytes 491528 | tf_op jit(solution)/shard_map/ppermute | solution.py:300
  24.2 10.0 %copy-start.2 = (bf16[256,256]{1,0:T(8,128)(2,1)S(1)}, bf16[256,256]{1,0:T(8,128)(2,1)}, u32[]{:S(2)}) copy-start(bf16[256,256]{1,0:T(8,128)(2,1)} %refs_12_.1) | copy-start | bytes 393220
  24.2 10.0 %copy-start.3 = (f32[8,256]{1,0:T(8,128)S(1)}, f32[8,256]{1,0:T(8,128)}, u32[]{:S(2)}) copy-start(f32[8,256]{1,0:T(8,128)} %refs_11_.1) | copy-start | bytes 24580
  24.2 1.3 %collective-permute-start.13 = (f32[32,512]{1,0:T(8,128)S(1)}, f32[32,512]{1,0:T(8,128)S(1)}, u32[]{:S(2)}, u32[]{:S(2)}) collective-permute-start(f32[32,512]{1,0:T(8,128)S(1)} %get-tuple-element.28), channel_id=1, source_target_pairs={{0,1},{1,0},{2,3},{3,2},{4,5},{5,4},{6,7},{7,6},{8,9},{9,8},{10,11... | collective-permute-start | bytes 196616 | tf_op jit(solution)/shard_map/ppermute | solution.py:302
  25.6 4.3 %collective-permute-start.16 = (f32[32,512]{1,0:T(8,128)S(1)}, f32[32,512]{1,0:T(8,128)S(1)}, u32[]{:S(2)}, u32[]{:S(2)}) collective-permute-start(f32[32,512]{1,0:T(8,128)S(1)} %add.38), channel_id=1, source_target_pairs={{0,2},{1,3},{2,0},{3,1},{4,6},{5,7},{6,4},{7,5},{8,10},{9,11},{10,... | collective-permute-start | bytes 196616 | tf_op jit(solution)/shard_map/ppermute | solution.py:303
  28.0 1.3 %collective-permute-start.15 = (f32[32,512]{1,0:T(8,128)S(1)}, f32[32,512]{1,0:T(8,128)S(1)}, u32[]{:S(2)}, u32[]{:S(2)}) collective-permute-start(f32[32,512]{1,0:T(8,128)S(1)} %project.5), channel_id=1, source_target_pairs={{0,1},{1,0},{2,3},{3,2},{4,5},{5,4},{6,7},{7,6},{8,9},{9,8},{10,11... | collective-permute-start | bytes 196616 | tf_op jit(solution)/shard_map/ppermute | solution.py:305
  28.0 3.4 %collective-permute-start.10 = (f32[16,512]{1,0:T(8,128)S(1)}, f32[16,512]{1,0:T(8,128)S(1)}, u32[]{:S(2)}, u32[]{:S(2)}) collective-permute-start(f32[16,512]{1,0:T(8,128)S(1)} %get-tuple-element.46), channel_id=1, source_target_pairs={{0,1},{1,0},{2,3},{3,2},{4,5},{5,4},{6,7},{7,6},{8,9},{9,8},{10,11... | collective-permute-start | bytes 98312 | tf_op jit(solution)/shard_map/ppermute | solution.py:309
  28.6 2.9 %collective-permute-start.6 = (f32[16,512]{1,0:T(8,128)S(1)}, f32[16,512]{1,0:T(8,128)S(1)}, u32[]{:S(2)}, u32[]{:S(2)}) collective-permute-start(f32[16,512]{1,0:T(8,128)S(1)} %get-tuple-element.50), channel_id=1, source_target_pairs={{0,1},{1,0},{2,3},{3,2},{4,5},{5,4},{6,7},{7,6},{8,9},{9,8},{10,11... | collective-permute-start | bytes 98312 | tf_op jit(solution)/shard_map/ppermute | solution.py:309
  28.7 3.4 %collective-permute-start.7 = (f32[16,512]{1,0:T(8,128)S(1)}, f32[16,512]{1,0:T(8,128)S(1)}, u32[]{:S(2)}, u32[]{:S(2)}) collective-permute-start(f32[16,512]{1,0:T(8,128)S(1)} %get-tuple-element.49), channel_id=1, source_target_pairs={{0,1},{1,0},{2,3},{3,2},{4,5},{5,4},{6,7},{7,6},{8,9},{9,8},{10,11... | collective-permute-start | bytes 98312 | tf_op jit(solution)/shard_map/ppermute | solution.py:309
  29.2 2.9 %collective-permute-start.8 = (f32[16,512]{1,0:T(8,128)S(1)}, f32[16,512]{1,0:T(8,128)S(1)}, u32[]{:S(2)}, u32[]{:S(2)}) collective-permute-start(f32[16,512]{1,0:T(8,128)S(1)} %get-tuple-element.48), channel_id=1, source_target_pairs={{0,1},{1,0},{2,3},{3,2},{4,5},{5,4},{6,7},{7,6},{8,9},{9,8},{10,11... | collective-permute-start | bytes 98312 | tf_op jit(solution)/shard_map/ppermute | solution.py:309
  29.9 4.3 %collective-permute-start.19 = (f32[32,512]{1,0:T(8,128)S(1)}, f32[32,512]{1,0:T(8,128)S(1)}, u32[]{:S(2)}, u32[]{:S(2)}) collective-permute-start(f32[32,512]{1,0:T(8,128)S(1)} %add.39.refs_9_), channel_id=1, source_target_pairs={{0,2},{1,3},{2,0},{3,1},{4,6},{5,7},{6,4},{7,5},{8,10},{9,11},{10,... | collective-permute-start | bytes 196616 | tf_op jit(solution)/shard_map/ppermute | solution.py:311
  31.5 1.3 %collective-permute-start.9 = (f32[16,512]{1,0:T(8,128)S(1)}, f32[16,512]{1,0:T(8,128)S(1)}, u32[]{:S(2)}, u32[]{:S(2)}) collective-permute-start(f32[16,512]{1,0:T(8,128)S(1)} %get-tuple-element.47), channel_id=1, source_target_pairs={{0,1},{1,0},{2,3},{3,2},{4,5},{5,4},{6,7},{7,6},{8,9},{9,8},{10,11... | collective-permute-start | bytes 98312 | tf_op jit(solution)/shard_map/ppermute | solution.py:309
  31.6 1.4 %collective-permute-start.17 = (f32[16,512]{1,0:T(8,128)S(1)}, f32[16,512]{1,0:T(8,128)S(1)}, u32[]{:S(2)}, u32[]{:S(2)}) collective-permute-start(f32[16,512]{1,0:T(8,128)S(1)} %get-tuple-element.52), channel_id=1, source_target_pairs={{0,1},{1,0},{2,3},{3,2},{4,5},{5,4},{6,7},{7,6},{8,9},{9,8},{10,11... | collective-permute-start | bytes 98312 | tf_op jit(solution)/shard_map/ppermute | solution.py:310
  32.0 1.2 %collective-permute-start.18 = (f32[16,512]{1,0:T(8,128)S(1)}, f32[16,512]{1,0:T(8,128)S(1)}, u32[]{:S(2)}, u32[]{:S(2)}) collective-permute-start(f32[16,512]{1,0:T(8,128)S(1)} %get-tuple-element.51), channel_id=1, source_target_pairs={{0,1},{1,0},{2,3},{3,2},{4,5},{5,4},{6,7},{7,6},{8,9},{9,8},{10,11... | collective-permute-start | bytes 98312 | tf_op jit(solution)/shard_map/ppermute | solution.py:310
  39.1 7.0 %collective-permute-start.20 = (bf16[32,2560]{1,0:T(8,128)(2,1)S(1)}, bf16[32,2560]{1,0:T(8,128)(2,1)S(1)}, u32[]{:S(2)}, u32[]{:S(2)}) collective-permute-start(bf16[32,2560]{1,0:T(8,128)(2,1)S(1)} %get-tuple-element.33), channel_id=1, source_target_pairs={{0,4},{4,0},{8,12},{12,8},{16,20},{20,16},{24,28},{28,24},{1,5},{5... | collective-permute-start | bytes 491528 | tf_op jit(solution)/shard_map/ppermute | solution.py:321
  41.2 8.1 %collective-permute-start.23 = (bf16[32,2560]{1,0:T(8,128)(2,1)S(1)}, bf16[32,2560]{1,0:T(8,128)(2,1)S(1)}, u32[]{:S(2)}, u32[]{:S(2)}) collective-permute-start(bf16[32,2560]{1,0:T(8,128)(2,1)S(1)} %get-tuple-element.39), channel_id=1, source_target_pairs={{0,4},{4,0},{8,12},{12,8},{16,20},{20,16},{24,28},{28,24},{1,5},{5... | collective-permute-start | bytes 491528 | tf_op jit(solution)/shard_map/ppermute | solution.py:323
  41.8 9.0 %collective-permute-start.25 = (bf16[32,2560]{1,0:T(8,128)(2,1)S(1)}, bf16[32,2560]{1,0:T(8,128)(2,1)S(1)}, u32[]{:S(2)}, u32[]{:S(2)}) collective-permute-start(bf16[32,2560]{1,0:T(8,128)(2,1)S(1)} %get-tuple-element.41), channel_id=1, source_target_pairs={{0,8},{4,12},{8,0},{12,4},{16,24},{20,28},{24,16},{28,20},{1,9},{5... | collective-permute-start | bytes 491528 | tf_op jit(solution)/shard_map/ppermute | solution.py:325
  46.2 11.3 %collective-permute-start.22 = (bf16[32,2560]{1,0:T(8,128)(2,1)S(1)}, bf16[32,2560]{1,0:T(8,128)(2,1)S(1)}, u32[]{:S(2)}, u32[]{:S(2)}) collective-permute-start(bf16[32,2560]{1,0:T(8,128)(2,1)S(1)} %add_convert_fusion.1), channel_id=1, source_target_pairs={{0,16},{4,20},{8,24},{12,28},{16,0},{20,4},{24,8},{28,12},{1,17},{... | collective-permute-start | bytes 491528 | tf_op jit(solution)/shard_map/ppermute | solution.py:322
  48.5 9.0 %collective-permute-start.21 = (bf16[32,2560]{1,0:T(8,128)(2,1)S(1)}, bf16[32,2560]{1,0:T(8,128)(2,1)S(1)}, u32[]{:S(2)}, u32[]{:S(2)}) collective-permute-start(bf16[32,2560]{1,0:T(8,128)(2,1)S(1)} %get-tuple-element.35), channel_id=1, source_target_pairs={{0,8},{4,12},{8,0},{12,4},{16,24},{20,28},{24,16},{28,20},{1,9},{5... | collective-permute-start | bytes 491528 | tf_op jit(solution)/shard_map/ppermute | solution.py:327
  49.4 10.0 %collective-permute-start.24 = (bf16[32,2560]{1,0:T(8,128)(2,1)S(1)}, bf16[32,2560]{1,0:T(8,128)(2,1)S(1)}, u32[]{:S(2)}, u32[]{:S(2)}) collective-permute-start(bf16[32,2560]{1,0:T(8,128)(2,1)S(1)} %add_convert_fusion), channel_id=1, source_target_pairs={{0,24},{4,28},{8,16},{12,20},{16,8},{20,12},{24,0},{28,4},{1,25},{... | collective-permute-start | bytes 491528 | tf_op jit(solution)/shard_map/ppermute | solution.py:324
  50.8 8.6 %collective-permute-start.26 = (f32[16,2560]{1,0:T(8,128)S(1)}, f32[16,2560]{1,0:T(8,128)S(1)}, u32[]{:S(2)}, u32[]{:S(2)}) collective-permute-start(f32[16,2560]{1,0:T(8,128)S(1)} %get-tuple-element.44), channel_id=1, source_target_pairs={{0,4},{4,0},{8,12},{12,8},{16,20},{20,16},{24,28},{28,24},{1,5},{5... | collective-permute-start | bytes 491528 | tf_op jit(solution)/shard_map/ppermute | solution.py:326
  52.6 6.9 %collective-permute-start.27 = (f32[16,2560]{1,0:T(8,128)S(1)}, f32[16,2560]{1,0:T(8,128)S(1)}, u32[]{:S(2)}, u32[]{:S(2)}) collective-permute-start(f32[16,2560]{1,0:T(8,128)S(1)} %get-tuple-element.45), channel_id=1, source_target_pairs={{0,4},{4,0},{8,12},{12,8},{16,20},{20,16},{24,28},{28,24},{1,5},{5... | collective-permute-start | bytes 491528 | tf_op jit(solution)/shard_map/ppermute | solution.py:326
